TPU v7x, 32 devices: a whole 2x2x4 slice. The times are simulated.
32 devices in a mesh: member: 2 (over y), lon: 4 (over z), lat: 2 (over x), lev: 2 (over core).
Axes of the slice: x: 2, y: 2, z: 4, core: 2. Of those that a mesh axis runs over, the one named last changes fastest.
Arguments:
- trajectory: bfloat16 [4, 3, 2, 512, 512], P('member', None, 'lev', 'lat', 'lon'), parts along dimension 0, may hold values from -6 to 6
- block_weights: float32 [8, 8], replicated, may hold values from 0.005 to 0.03
- wind_speed: float32 [2, 64, 64], P('lev', 'lat', 'lon'), may hold values from 0.05 to 0.45
- settling: float32 [3, 2], replicated, may hold values from 0.02 to 0.25
- source_mask: int32 [64, 64], P('lat', 'lon'), may hold values 0 or 1
- obs_columns: int32 [128, 32], P('member'), parts along dimension 0, may hold values from 0 to 63
- obs_values: float32 [4, 64, 32], P('member'), parts along dimension 0, may hold values from -6 to 6
- obs_weights: float32 [4, 64, 32], P('member'), parts along dimension 0, may hold values from 0.3 to 3
Outputs:
- analysis: bfloat16 [4, 3, 2, 512, 512], P('member', None, 'lev', 'lat', 'lon'), parts along dimension 0
- correction: float32 [4, 3, 2, 64, 64], P('member', None, 'lev', 'lat', 'lon'), parts along dimension 0
There are 2 independent parts, one for each index of `member`. A program takes and returns all parts, laid end to end along the dimension named above; an argument that names none is the same for every part. Nothing has to cross between parts.
All inputs are finite; a program needn't handle non-finite values. No bound on the sum of `source_mask` on one device may be relied on, other than what follows from the above.
Results may differ from a plain program's by a relative error of at most 0.001.
Values sent between devices are 32-bit elements; how exact they have to be, the bound alone decides.
No kernel may reach another device: no remote copies, remote signals or barrier semaphores. Data moves between devices by JAX's collectives and lax.ppermute only.
A program may use at most 64 MiB of HBM per device.

v0:
```python
import jax
import jax.numpy as jnp
from jax import lax
from jax.sharding import PartitionSpec as P

BLOCK = 8
STEPS = 4
SWEEPS = 2


diffusion = 0.05
background = 0.1
step_length = 4.0


def extended_2(block, sides, width):
    for axis, dim in sides:
        count = lax.axis_size(axis)
        forward = [(i, i + 1) for i in range(count - 1)]
        forward.append((count - 1, 0))
        backward = [(target, source) for source, target in forward]
        low = lax.ppermute(
            lax.slice_in_dim(block, block.shape[dim] - width, None, axis=dim), axis, forward
        )
        high = lax.ppermute(lax.slice_in_dim(block, 0, width, axis=dim), axis, backward)
        block = jnp.concatenate([low, block, high], axis=dim)
    return block


def row_rims(extended, row_index, row_count):
    lower_keep = (row_index > 0).astype(jnp.float32)
    upper_keep = (row_index < row_count - 1).astype(jnp.float32)
    extended = extended.at[..., 0, :].multiply(lower_keep)
    return extended.at[..., -1, :].multiply(upper_keep)


def halo_relaid(stacked):
    extended = extended_2(stacked, (("lon", 5), (("lat", "lev"), 4)), 1)
    return row_rims(extended, lax.axis_index(("lat", "lev")), lax.axis_size(("lat", "lev")))


def forward_update(values, mass_flux, sinking, extended, above_rim):
    cells = extended[0]
    west_cells = cells[..., 1:-1, :-2]
    east_cells = cells[..., 1:-1, 2:]
    south_cells = cells[..., :-2, 1:-1]
    north_cells = cells[..., 2:, 1:-1]
    flux_west = extended[1][..., 1:-1, :-2]
    from_above = jnp.concatenate([above_rim, sinking[:, :, :-1]], axis=2)
    return (
        values
        + (flux_west - mass_flux)
        + diffusion * (east_cells + west_cells - 2.0 * values)
        + diffusion * (north_cells + south_cells - 2.0 * values)
        + (from_above - sinking)
    )


def adjoint_update(values, wind, rates, extended, below_rim):
    cells = extended[0]
    west_cells = cells[..., 1:-1, :-2]
    east_cells = cells[..., 1:-1, 2:]
    south_cells = cells[..., :-2, 1:-1]
    north_cells = cells[..., 2:, 1:-1]
    from_below = jnp.concatenate([values[:, :, 1:], below_rim], axis=2)
    return (
        values
        + wind * (east_cells - values)
        + diffusion * (east_cells + west_cells - 2.0 * values)
        + diffusion * (north_cells + south_cells - 2.0 * values)
        + rates * (from_below - values)
    )


def per_device(
    trajectory,
    block_weights,
    wind_speed,
    settling,
    source_mask,
    obs_columns,
    obs_values,
    obs_weights,
):
    highest = lax.Precision.HIGHEST
    slot_count, bin_count, level_block, fine_rows, fine_cols = trajectory.shape
    level_total = settling.shape[1]
    lat_total = obs_columns.shape[0]
    obs_count = obs_columns.shape[1]
    row_block = fine_rows // BLOCK
    col_block = fine_cols // BLOCK
    blocks = trajectory.astype(jnp.float32).reshape(
        slot_count, bin_count, level_block, row_block, BLOCK, col_block, BLOCK
    )
    restricted = jnp.einsum("sbkiajc,ac->sbkij", blocks, block_weights, precision=highest)
    mask_block = source_mask.astype(jnp.float32)
    moved = (
        lax.all_to_all(restricted, "lev", split_axis=3, concat_axis=2, tiled=True),
        lax.all_to_all(wind_speed[None, None], "lev", split_axis=3, concat_axis=2, tiled=True),
    )
    coarse = moved[0]
    wind = moved[1][0, 0]
    rates = settling[None, :, :, None, None]
    rows_here = row_block // lax.axis_size("lev")
    first_row = lax.axis_index(("lat", "lev")) * rows_here
    control_mask = lax.dynamic_slice_in_dim(
        mask_block, lax.axis_index("lev") * rows_here, rows_here, 0
    )
    first_col = lax.axis_index("lon") * col_block
    own_cols = first_col + jnp.arange(col_block, dtype=jnp.int32)
    my_obs = lax.dynamic_slice_in_dim(obs_columns, first_row, rows_here, 0)
    picker = (my_obs[:, :, None] == own_cols[None, None, :]).astype(jnp.float32)
    column_scale = 1.0 / (bin_count * level_total)
    correction = jnp.zeros_like(coarse)
    for sweep_index in range(SWEEPS):
        tracer = coarse + correction
        for step_index in range(STEPS):
            mass_flux = wind * tracer
            sinking = rates * tracer
            stacked = jnp.stack([tracer, mass_flux])
            extended = halo_relaid(stacked)
            above_rim = jnp.zeros_like(sinking[:, :, :1])
            tracer = forward_update(tracer, mass_flux, sinking, extended, above_rim)
        columns = jnp.sum(tracer, axis=(1, 2)) * column_scale
        partial_obs = jnp.einsum("sic,ioc->sio", columns, picker, precision=highest)
        placed = lax.dynamic_update_slice_in_dim(
            jnp.zeros((slot_count, lat_total, obs_count), jnp.float32), partial_obs, first_row, 1
        )
        observed = lax.psum(placed, ("lon", "lat", "lev"))
        misfit = obs_weights * (observed - obs_values)
        my_misfit = lax.dynamic_slice_in_dim(misfit, first_row, rows_here, 1)
        spread = jnp.einsum("sio,ioc->sic", my_misfit, picker, precision=highest) * column_scale
        adjoint = jnp.broadcast_to(spread[:, None, None], coarse.shape)
        for step_index in range(STEPS):
            extended = halo_relaid(adjoint[None])
            below_rim = jnp.zeros_like(adjoint[:, :, :1])
            adjoint = adjoint_update(adjoint, wind, rates, extended, below_rim)
        gradient = background * correction + adjoint
        correction = control_mask * (correction - step_length * gradient)
    own_correction = lax.all_to_all(correction, "lev", split_axis=2, concat_axis=3, tiled=True)
    growth = BLOCK * BLOCK * block_weights
    increment = jnp.einsum("sbkij,ac->sbkiajc", own_correction, growth, precision=highest)
    increment = increment.reshape(slot_count, bin_count, level_block, fine_rows, fine_cols)
    analysis = (trajectory.astype(jnp.float32) + increment).astype(jnp.bfloat16)
    return (analysis, own_correction)


def solution(mesh):
    placed = (
        P("member", None, "lev", "lat", "lon"),
        P(),
        P("lev", "lat", "lon"),
        P(),
        P("lat", "lon"),
        P("member", None),
        P("member", None, None),
        P("member", None, None),
    )
    return jax.shard_map(
        per_device,
        mesh=mesh,
        in_specs=placed,
        out_specs=(P("member", None, "lev", "lat", "lon"), P("member", None, "lev", "lat", "lon")),
        check_vma=False,
    )
```

profile of v0, /device:TPU:0, one launch (start us, length us, event | category | flops | bytes accessed | tf_op | source)
XLA Modules:
  0.0 420.4 jit_solution(14785640180381588731)
XLA Ops:
  6.7 9.3 %reshape.1330 = bf16[2,3,32,8,16,8]{5,4,3,2,1,0:T(8,128)(2,1)} reshape(bf16[2,3,1,256,128]{4,3,2,1,0:T(8,128)(2,1)} %param.72) | data formatting | bytes 786432 | tf_op jit(solution)/shard_map/reshape.1252
  16.0 24.0 %fusion.177 = f32[1,2,3,32,16,1]{4,0,5,3,2,1:T(1,128)S(1)} fusion(bf16[2,3,32,8,16,8]{5,4,3,2,1,0:T(8,128)(2,1)} %reshape.1330, f32[8,8,1,1,1,1]{1,2,0,5,4,3:T(1,128)} %bitcast.257), kind=kOutput, calls=%fused_computation.374 | convolution fusion | flops 2359296 | bytes 405760 | tf_op jit(solution)/shard_map/sbkiajc,ac->sbkij/dot_general | solution.py:95
  51.7 5.6 %collective-permute-done = f32[2,2,3,2,16,1]{5,4,3,2,1,0:T(8,128)S(1)} collective-permute-done((f32[2,2,3,2,16,1]{5,4,3,2,1,0:T(8,128)S(1)}, f32[2,2,3,2,16,1]{5,4,3,2,1,0:T(8,128)S(1)}, u32[]{:S(2)}, u32[]{:S(2)}) %collective-permute-start) | collective-permute-done | bytes 1568 | tf_op jit(solution)/shard_map/ppermute | solution.py:22
  68.6 5.3 %collective-permute-done.4 = f32[2,2,3,2,16,1]{5,4,3,2,1,0:T(8,128)S(1)} collective-permute-done((f32[2,2,3,2,16,1]{5,4,3,2,1,0:T(8,128)S(1)}, f32[2,2,3,2,16,1]{5,4,3,2,1,0:T(8,128)S(1)}, u32[]{:S(2)}, u32[]{:S(2)}) %collective-permute-start.4) | collective-permute-done | bytes 1568 | tf_op jit(solution)/shard_map/ppermute | solution.py:22
  74.0 3.6 collective-permute-done.5
  85.6 5.6 %collective-permute-done.8 = f32[2,2,3,2,16,1]{5,4,3,2,1,0:T(8,128)S(1)} collective-permute-done((f32[2,2,3,2,16,1]{5,4,3,2,1,0:T(8,128)S(1)}, f32[2,2,3,2,16,1]{5,4,3,2,1,0:T(8,128)S(1)}, u32[]{:S(2)}, u32[]{:S(2)}) %collective-permute-start.8) | collective-permute-done | bytes 1568 | tf_op jit(solution)/shard_map/ppermute | solution.py:22
  102.6 5.8 %collective-permute-done.12 = f32[2,2,3,2,16,1]{5,4,3,2,1,0:T(8,128)S(1)} collective-permute-done((f32[2,2,3,2,16,1]{5,4,3,2,1,0:T(8,128)S(1)}, f32[2,2,3,2,16,1]{5,4,3,2,1,0:T(8,128)S(1)}, u32[]{:S(2)}, u32[]{:S(2)}) %collective-permute-start.12) | collective-permute-done | bytes 1568 | tf_op jit(solution)/shard_map/ppermute | solution.py:22
  115.8 60.7 %psum.14 = f32[2,64,32]{1,2,0:T(8,128)S(1)} all-reduce(f32[2,64,32]{1,2,0:T(8,128)S(1)} %dynamic_update_slice.6), channel_id=1, replica_groups=mesh['member'=2,'lon'=4,'lat'=2,'lev'=2] {'lon','lat','lev'}, use_global_device_ids=true, to_apply=%region_1.0 | all-reduce | flops 4096 | bytes 32768 | tf_op jit(solution)/shard_map/psum | solution.py:129
  177.4 3.8 collective-permute-start.17
  187.8 3.9 collective-permute-start.21
  202.5 3.5 collective-permute-done.24
  215.0 3.8 collective-permute-done.28
  227.3 5.8 %collective-permute-done.32 = f32[2,2,3,2,16,1]{5,4,3,2,1,0:T(8,128)S(1)} collective-permute-done((f32[2,2,3,2,16,1]{5,4,3,2,1,0:T(8,128)S(1)}, f32[2,2,3,2,16,1]{5,4,3,2,1,0:T(8,128)S(1)}, u32[]{:S(2)}, u32[]{:S(2)}) %collective-permute-start.32) | collective-permute-done | bytes 1568 | tf_op jit(solution)/shard_map/ppermute | solution.py:22
  243.8 5.7 %collective-permute-done.36 = f32[2,2,3,2,16,1]{5,4,3,2,1,0:T(8,128)S(1)} collective-permute-done((f32[2,2,3,2,16,1]{5,4,3,2,1,0:T(8,128)S(1)}, f32[2,2,3,2,16,1]{5,4,3,2,1,0:T(8,128)S(1)}, u32[]{:S(2)}, u32[]{:S(2)}) %collective-permute-start.36) | collective-permute-done | bytes 1568 | tf_op jit(solution)/shard_map/ppermute | solution.py:22
  249.5 3.9 collective-permute-done.37
  261.4 5.9 %collective-permute-done.40 = f32[2,2,3,2,16,1]{5,4,3,2,1,0:T(8,128)S(1)} collective-permute-done((f32[2,2,3,2,16,1]{5,4,3,2,1,0:T(8,128)S(1)}, f32[2,2,3,2,16,1]{5,4,3,2,1,0:T(8,128)S(1)}, u32[]{:S(2)}, u32[]{:S(2)}) %collective-permute-start.40) | collective-permute-done | bytes 1568 | tf_op jit(solution)/shard_map/ppermute | solution.py:22
  277.8 5.6 %collective-permute-done.44 = f32[2,2,3,2,16,1]{5,4,3,2,1,0:T(8,128)S(1)} collective-permute-done((f32[2,2,3,2,16,1]{5,4,3,2,1,0:T(8,128)S(1)}, f32[2,2,3,2,16,1]{5,4,3,2,1,0:T(8,128)S(1)}, u32[]{:S(2)}, u32[]{:S(2)}) %collective-permute-start.44) | collective-permute-done | bytes 1568 | tf_op jit(solution)/shard_map/ppermute | solution.py:22
  291.2 61.1 %psum.15 = f32[2,64,32]{1,2,0:T(8,128)S(1)} all-reduce(f32[2,64,32]{1,2,0:T(8,128)S(1)} %dynamic_update_slice.7), channel_id=1, replica_groups=mesh['member'=2,'lon'=4,'lat'=2,'lev'=2] {'lon','lat','lev'}, use_global_device_ids=true, to_apply=%region_3.0 | all-reduce | flops 4096 | bytes 32768 | tf_op jit(solution)/shard_map/psum | solution.py:129
  353.2 3.8 collective-permute-start.49
  363.4 3.9 collective-permute-start.53
  390.7 3.8 collective-permute-done.60
  399.0 4.2 %all_to_all.33 = f32[2,1,1536]{2,1,0:T(1,128)S(1)} all-to-all(f32[2,1,1536]{2,1,0:T(1,128)S(1)} %reshape.1339), channel_id=1, replica_groups=mesh['member'=2,'lon'=4,'lat'=2,'lev'=2] {'lev'}, dimensions={0} | all-to-all | bytes 24576 | tf_op jit(solution)/shard_map/all_to_all | solution.py:140
  405.0 5.5 %multiply_bitcast_fusion = f32[2,3,1,32,8,16,8]{6,5,4,3,1,0,2:T(8,128)} fusion(f32[2,3,32,16]{3,2,1,0:T(8,128)S(1)} %bitcast.250, f32[8,8]{1,0:T(8,128)S(1)} %broadcast_multiply_fusion.26), kind=kLoop, calls=%fused_computation | loop fusion | flops 196608 | bytes 798976 | tf_op jit(solution)/shard_map/sbkij,ac->sbkiajc/transpose | solution.py:142
  410.5 9.1 %reshape.1332 = f32[2,3,1,256,128]{4,3,1,0,2:T(8,128)S(1)} reshape(f32[2,3,1,32,8,16,8]{6,5,4,3,1,0,2:T(8,128)} %multiply_bitcast_fusion) | data formatting | bytes 1572864 | tf_op jit(solution)/shard_map/reshape | solution.py:143
  (352 shorter events, 165.0 us)
Async XLA Ops:
  3.4 37.4 %all-to-all-start.1 = ((f32[2,1,256]{2,1,0:T(1,128)}), f32[2,1,256]{2,1,0:T(1,128)S(1)}, u32[]{:S(2)}, u32[]{:S(2)}) async-start(f32[2,1,256]{2,1,0:T(1,128)} %reshape.1335), calls=%async_computation.1 | async-start | bytes 4096 | tf_op jit(solution)/shard_map/all_to_all | solution.py:99
  46.5 10.8 %collective-permute-start = (f32[2,2,3,2,16,1]{5,4,3,2,1,0:T(8,128)S(1)}, f32[2,2,3,2,16,1]{5,4,3,2,1,0:T(8,128)S(1)}, u32[]{:S(2)}, u32[]{:S(2)}) collective-permute-start(f32[2,2,3,2,16,1]{5,4,3,2,1,0:T(8,128)S(1)} %get-tuple-element.477), channel_id=1, source_target_pairs={{0,4},{4,8},{8,12},{12,0},{1,5},{5,9},{9,13},{13,1},{2,6},{6,10},{... | collective-permute-start | bytes 4616 | tf_op jit(solution)/shard_map/ppermute | solution.py:22
  49.5 10.9 %collective-permute-start.1 = (f32[2,2,3,2,16,1]{5,4,3,2,1,0:T(8,128)S(1)}, f32[2,2,3,2,16,1]{5,4,3,2,1,0:T(8,128)S(1)}, u32[]{:S(2)}, u32[]{:S(2)}) collective-permute-start(f32[2,2,3,2,16,1]{5,4,3,2,1,0:T(8,128)S(1)} %get-tuple-element.478), channel_id=1, source_target_pairs={{4,0},{8,4},{12,8},{0,12},{5,1},{9,5},{13,9},{1,13},{6,2},{10,6},{... | collective-permute-start | bytes 4616 | tf_op jit(solution)/shard_map/ppermute | solution.py:25
  64.7 9.2 %collective-permute-start.4 = (f32[2,2,3,2,16,1]{5,4,3,2,1,0:T(8,128)S(1)}, f32[2,2,3,2,16,1]{5,4,3,2,1,0:T(8,128)S(1)}, u32[]{:S(2)}, u32[]{:S(2)}) collective-permute-start(f32[2,2,3,2,16,1]{5,4,3,2,1,0:T(8,128)S(1)} %get-tuple-element.475), channel_id=1, source_target_pairs={{0,4},{4,8},{8,12},{12,0},{1,5},{5,9},{9,13},{13,1},{2,6},{6,10},{... | collective-permute-start | bytes 4616 | tf_op jit(solution)/shard_map/ppermute | solution.py:22
  65.9 11.7 %collective-permute-start.5 = (f32[2,2,3,2,16,1]{5,4,3,2,1,0:T(8,128)S(1)}, f32[2,2,3,2,16,1]{5,4,3,2,1,0:T(8,128)S(1)}, u32[]{:S(2)}, u32[]{:S(2)}) collective-permute-start(f32[2,2,3,2,16,1]{5,4,3,2,1,0:T(8,128)S(1)} %get-tuple-element.476), channel_id=1, source_target_pairs={{4,0},{8,4},{12,8},{0,12},{5,1},{9,5},{13,9},{1,13},{6,2},{10,6},{... | collective-permute-start | bytes 4616 | tf_op jit(solution)/shard_map/ppermute | solution.py:25
  81.7 9.5 %collective-permute-start.8 = (f32[2,2,3,2,16,1]{5,4,3,2,1,0:T(8,128)S(1)}, f32[2,2,3,2,16,1]{5,4,3,2,1,0:T(8,128)S(1)}, u32[]{:S(2)}, u32[]{:S(2)}) collective-permute-start(f32[2,2,3,2,16,1]{5,4,3,2,1,0:T(8,128)S(1)} %get-tuple-element.473), channel_id=1, source_target_pairs={{0,4},{4,8},{8,12},{12,0},{1,5},{5,9},{9,13},{13,1},{2,6},{6,10},{... | collective-permute-start | bytes 4616 | tf_op jit(solution)/shard_map/ppermute | solution.py:22
  82.5 12.0 %collective-permute-start.9 = (f32[2,2,3,2,16,1]{5,4,3,2,1,0:T(8,128)S(1)}, f32[2,2,3,2,16,1]{5,4,3,2,1,0:T(8,128)S(1)}, u32[]{:S(2)}, u32[]{:S(2)}) collective-permute-start(f32[2,2,3,2,16,1]{5,4,3,2,1,0:T(8,128)S(1)} %get-tuple-element.474), channel_id=1, source_target_pairs={{4,0},{8,4},{12,8},{0,12},{5,1},{9,5},{13,9},{1,13},{6,2},{10,6},{... | collective-permute-start | bytes 4616 | tf_op jit(solution)/shard_map/ppermute | solution.py:25
  98.6 9.8 %collective-permute-start.12 = (f32[2,2,3,2,16,1]{5,4,3,2,1,0:T(8,128)S(1)}, f32[2,2,3,2,16,1]{5,4,3,2,1,0:T(8,128)S(1)}, u32[]{:S(2)}, u32[]{:S(2)}) collective-permute-start(f32[2,2,3,2,16,1]{5,4,3,2,1,0:T(8,128)S(1)} %get-tuple-element.471), channel_id=1, source_target_pairs={{0,4},{4,8},{8,12},{12,0},{1,5},{5,9},{9,13},{13,1},{2,6},{6,10},{... | collective-permute-start | bytes 4616 | tf_op jit(solution)/shard_map/ppermute | solution.py:22
  99.1 11.8 %collective-permute-start.13 = (f32[2,2,3,2,16,1]{5,4,3,2,1,0:T(8,128)S(1)}, f32[2,2,3,2,16,1]{5,4,3,2,1,0:T(8,128)S(1)}, u32[]{:S(2)}, u32[]{:S(2)}) collective-permute-start(f32[2,2,3,2,16,1]{5,4,3,2,1,0:T(8,128)S(1)} %get-tuple-element.472), channel_id=1, source_target_pairs={{4,0},{8,4},{12,8},{0,12},{5,1},{9,5},{13,9},{1,13},{6,2},{10,6},{... | collective-permute-start | bytes 4616 | tf_op jit(solution)/shard_map/ppermute | solution.py:25
  198.6 7.4 %collective-permute-start.24 = (f32[1,2,3,2,16,1]{5,4,3,2,1,0:T(8,128)S(1)}, f32[1,2,3,2,16,1]{5,4,3,2,1,0:T(8,128)S(1)}, u32[]{:S(2)}, u32[]{:S(2)}) collective-permute-start(f32[1,2,3,2,16,1]{5,4,3,2,1,0:T(8,128)S(1)} %get-tuple-element.487), channel_id=1, source_target_pairs={{0,4},{4,8},{8,12},{12,0},{1,5},{5,9},{9,13},{13,1},{2,6},{6,10},{... | collective-permute-start | bytes 2312 | tf_op jit(solution)/shard_map/ppermute | solution.py:22
  200.2 7.2 %collective-permute-start.25 = (f32[1,2,3,2,16,1]{5,4,3,2,1,0:T(8,128)S(1)}, f32[1,2,3,2,16,1]{5,4,3,2,1,0:T(8,128)S(1)}, u32[]{:S(2)}, u32[]{:S(2)}) collective-permute-start(f32[1,2,3,2,16,1]{5,4,3,2,1,0:T(8,128)S(1)} %get-tuple-element.488), channel_id=1, source_target_pairs={{4,0},{8,4},{12,8},{0,12},{5,1},{9,5},{13,9},{1,13},{6,2},{10,6},{... | collective-permute-start | bytes 2312 | tf_op jit(solution)/shard_map/ppermute | solution.py:25
  211.1 7.7 %collective-permute-start.28 = (f32[1,2,3,2,16,1]{5,4,3,2,1,0:T(8,128)S(1)}, f32[1,2,3,2,16,1]{5,4,3,2,1,0:T(8,128)S(1)}, u32[]{:S(2)}, u32[]{:S(2)}) collective-permute-start(f32[1,2,3,2,16,1]{5,4,3,2,1,0:T(8,128)S(1)} %get-tuple-element.485), channel_id=1, source_target_pairs={{0,4},{4,8},{8,12},{12,0},{1,5},{5,9},{9,13},{13,1},{2,6},{6,10},{... | collective-permute-start | bytes 2312 | tf_op jit(solution)/shard_map/ppermute | solution.py:22
  211.8 7.7 %collective-permute-start.29 = (f32[1,2,3,2,16,1]{5,4,3,2,1,0:T(8,128)S(1)}, f32[1,2,3,2,16,1]{5,4,3,2,1,0:T(8,128)S(1)}, u32[]{:S(2)}, u32[]{:S(2)}) collective-permute-start(f32[1,2,3,2,16,1]{5,4,3,2,1,0:T(8,128)S(1)} %get-tuple-element.486), channel_id=1, source_target_pairs={{4,0},{8,4},{12,8},{0,12},{5,1},{9,5},{13,9},{1,13},{6,2},{10,6},{... | collective-permute-start | bytes 2312 | tf_op jit(solution)/shard_map/ppermute | solution.py:25
  223.5 9.7 %collective-permute-start.32 = (f32[2,2,3,2,16,1]{5,4,3,2,1,0:T(8,128)S(1)}, f32[2,2,3,2,16,1]{5,4,3,2,1,0:T(8,128)S(1)}, u32[]{:S(2)}, u32[]{:S(2)}) collective-permute-start(f32[2,2,3,2,16,1]{5,4,3,2,1,0:T(8,128)S(1)} %get-tuple-element.469), channel_id=1, source_target_pairs={{0,4},{4,8},{8,12},{12,0},{1,5},{5,9},{9,13},{13,1},{2,6},{6,10},{... | collective-permute-start | bytes 4616 | tf_op jit(solution)/shard_map/ppermute | solution.py:22
  224.0 11.8 %collective-permute-start.33 = (f32[2,2,3,2,16,1]{5,4,3,2,1,0:T(8,128)S(1)}, f32[2,2,3,2,16,1]{5,4,3,2,1,0:T(8,128)S(1)}, u32[]{:S(2)}, u32[]{:S(2)}) collective-permute-start(f32[2,2,3,2,16,1]{5,4,3,2,1,0:T(8,128)S(1)} %get-tuple-element.470), channel_id=1, source_target_pairs={{4,0},{8,4},{12,8},{0,12},{5,1},{9,5},{13,9},{1,13},{6,2},{10,6},{... | collective-permute-start | bytes 4616 | tf_op jit(solution)/shard_map/ppermute | solution.py:25
  239.9 9.6 %collective-permute-start.36 = (f32[2,2,3,2,16,1]{5,4,3,2,1,0:T(8,128)S(1)}, f32[2,2,3,2,16,1]{5,4,3,2,1,0:T(8,128)S(1)}, u32[]{:S(2)}, u32[]{:S(2)}) collective-permute-start(f32[2,2,3,2,16,1]{5,4,3,2,1,0:T(8,128)S(1)} %get-tuple-element.467), channel_id=1, source_target_pairs={{0,4},{4,8},{8,12},{12,0},{1,5},{5,9},{9,13},{13,1},{2,6},{6,10},{... | collective-permute-start | bytes 4616 | tf_op jit(solution)/shard_map/ppermute | solution.py:22
  241.8 11.5 %collective-permute-start.37 = (f32[2,2,3,2,16,1]{5,4,3,2,1,0:T(8,128)S(1)}, f32[2,2,3,2,16,1]{5,4,3,2,1,0:T(8,128)S(1)}, u32[]{:S(2)}, u32[]{:S(2)}) collective-permute-start(f32[2,2,3,2,16,1]{5,4,3,2,1,0:T(8,128)S(1)} %get-tuple-element.468), channel_id=1, source_target_pairs={{4,0},{8,4},{12,8},{0,12},{5,1},{9,5},{13,9},{1,13},{6,2},{10,6},{... | collective-permute-start | bytes 4616 | tf_op jit(solution)/shard_map/ppermute | solution.py:25
  257.5 9.8 %collective-permute-start.40 = (f32[2,2,3,2,16,1]{5,4,3,2,1,0:T(8,128)S(1)}, f32[2,2,3,2,16,1]{5,4,3,2,1,0:T(8,128)S(1)}, u32[]{:S(2)}, u32[]{:S(2)}) collective-permute-start(f32[2,2,3,2,16,1]{5,4,3,2,1,0:T(8,128)S(1)} %get-tuple-element.465), channel_id=1, source_target_pairs={{0,4},{4,8},{8,12},{12,0},{1,5},{5,9},{9,13},{13,1},{2,6},{6,10},{... | collective-permute-start | bytes 4616 | tf_op jit(solution)/shard_map/ppermute | solution.py:22
  258.1 11.7 %collective-permute-start.41 = (f32[2,2,3,2,16,1]{5,4,3,2,1,0:T(8,128)S(1)}, f32[2,2,3,2,16,1]{5,4,3,2,1,0:T(8,128)S(1)}, u32[]{:S(2)}, u32[]{:S(2)}) collective-permute-start(f32[2,2,3,2,16,1]{5,4,3,2,1,0:T(8,128)S(1)} %get-tuple-element.466), channel_id=1, source_target_pairs={{4,0},{8,4},{12,8},{0,12},{5,1},{9,5},{13,9},{1,13},{6,2},{10,6},{... | collective-permute-start | bytes 4616 | tf_op jit(solution)/shard_map/ppermute | solution.py:25
  274.0 9.5 %collective-permute-start.44 = (f32[2,2,3,2,16,1]{5,4,3,2,1,0:T(8,128)S(1)}, f32[2,2,3,2,16,1]{5,4,3,2,1,0:T(8,128)S(1)}, u32[]{:S(2)}, u32[]{:S(2)}) collective-permute-start(f32[2,2,3,2,16,1]{5,4,3,2,1,0:T(8,128)S(1)} %get-tuple-element.463), channel_id=1, source_target_pairs={{0,4},{4,8},{8,12},{12,0},{1,5},{5,9},{9,13},{13,1},{2,6},{6,10},{... | collective-permute-start | bytes 4616 | tf_op jit(solution)/shard_map/ppermute | solution.py:22
  274.8 11.6 %collective-permute-start.45 = (f32[2,2,3,2,16,1]{5,4,3,2,1,0:T(8,128)S(1)}, f32[2,2,3,2,16,1]{5,4,3,2,1,0:T(8,128)S(1)}, u32[]{:S(2)}, u32[]{:S(2)}) collective-permute-start(f32[2,2,3,2,16,1]{5,4,3,2,1,0:T(8,128)S(1)} %get-tuple-element.464), channel_id=1, source_target_pairs={{4,0},{8,4},{12,8},{0,12},{5,1},{9,5},{13,9},{1,13},{6,2},{10,6},{... | collective-permute-start | bytes 4616 | tf_op jit(solution)/shard_map/ppermute | solution.py:25
  374.2 7.4 %collective-permute-start.56 = (f32[1,2,3,2,16,1]{5,4,3,2,1,0:T(8,128)S(1)}, f32[1,2,3,2,16,1]{5,4,3,2,1,0:T(8,128)S(1)}, u32[]{:S(2)}, u32[]{:S(2)}) collective-permute-start(f32[1,2,3,2,16,1]{5,4,3,2,1,0:T(8,128)S(1)} %get-tuple-element.481), channel_id=1, source_target_pairs={{0,4},{4,8},{8,12},{12,0},{1,5},{5,9},{9,13},{13,1},{2,6},{6,10},{... | collective-permute-start | bytes 2312 | tf_op jit(solution)/shard_map/ppermute | solution.py:22
  386.8 7.7 %collective-permute-start.60 = (f32[1,2,3,2,16,1]{5,4,3,2,1,0:T(8,128)S(1)}, f32[1,2,3,2,16,1]{5,4,3,2,1,0:T(8,128)S(1)}, u32[]{:S(2)}, u32[]{:S(2)}) collective-permute-start(f32[1,2,3,2,16,1]{5,4,3,2,1,0:T(8,128)S(1)} %get-tuple-element.479), channel_id=1, source_target_pairs={{0,4},{4,8},{8,12},{12,0},{1,5},{5,9},{9,13},{13,1},{2,6},{6,10},{... | collective-permute-start | bytes 2312 | tf_op jit(solution)/shard_map/ppermute | solution.py:22
  387.4 7.7 %collective-permute-start.61 = (f32[1,2,3,2,16,1]{5,4,3,2,1,0:T(8,128)S(1)}, f32[1,2,3,2,16,1]{5,4,3,2,1,0:T(8,128)S(1)}, u32[]{:S(2)}, u32[]{:S(2)}) collective-permute-start(f32[1,2,3,2,16,1]{5,4,3,2,1,0:T(8,128)S(1)} %get-tuple-element.480), channel_id=1, source_target_pairs={{4,0},{8,4},{12,8},{0,12},{5,1},{9,5},{13,9},{1,13},{6,2},{10,6},{... | collective-permute-start | bytes 2312 | tf_op jit(solution)/shard_map/ppermute | solution.py:25
  (49 other events, 1004.3 us)
where the time goes:
time: 421 us; the launch traced here: 420 us
  blocking collectives  126 us (30%)
  waiting for transfers between devices  121 us (29%)
  starting transfers between devices  99.1 us (24%)
  local copies, waits for them, and re-layouts  27.8 us (7%)
  matrix products  25.1 us (6%)
  other arithmetic  19.1 us (5%)
    psum x2, blocking collectives, per_device(): observed = lax.psum(placed, ('lon', 'lat', 'lev'))  122 us
    ppermute x32, waiting for transfers between devices, extended_2(): lax.ppermute(lax.slice_in_dim(block, block.shape[dim] - width, None, axis...  90.9 us
    ppermute x32, starting transfers between devices, extended_2(): lax.ppermute(lax.slice_in_dim(block, 0, width, axis=dim), axis, backward)  77 us
    ppermute x32, waiting for transfers between devices, extended_2(): lax.ppermute(lax.slice_in_dim(block, 0, width, axis=dim), axis, backward)  29.8 us
    dot_general x1, matrix products, per_device(): jnp.einsum('sbkiajc,ac->sbkij', blocks, block_weights, precision=highest)  24 us
    ppermute x32, starting transfers between devices, extended_2(): lax.ppermute(lax.slice_in_dim(block, block.shape[dim] - width, None, axis...  15.7 us
    another operation x5, local copies, waits for them, and re-layouts  9.4 us
    reshape x1, local copies, waits for them, and re-layouts, per_device(): increment.reshape(slot_count, bin_count, level_block, fine_rows, fine_cols)  9.07 us
  transfers between devices with their start and end apart: 66, of which 51 were waited for; matrix products, arithmetic and copies ran while one was open for 9% of the time, Pallas kernels for 0%

commit v1 on v0

v1 whole, which is shorter than its diff:
```python
import jax
import jax.numpy as jnp
from jax import lax
from jax.experimental import pallas as pl
from jax.experimental.pallas import tpu as pltpu
from jax.sharding import PartitionSpec as P

BLOCK = 8
STEPS = 4
SWEEPS = 2
REACH = STEPS * 2 * SWEEPS
LANES = 128
HALF = LANES // 2
EDGE = 8

diffusion = 0.05
background = 0.1
step_length = 4.0
AXES = ("lon", "lat", "lev")


def lane_iota(rows):
    return lax.broadcasted_iota(jnp.int32, (rows, LANES), 1)


def three_parts(values):
    high = values.astype(jnp.bfloat16)
    rest = values - high.astype(jnp.float32)
    middle = rest.astype(jnp.bfloat16)
    low = (rest - middle.astype(jnp.float32)).astype(jnp.bfloat16)
    return jnp.concatenate([high, middle, low], axis=0)


def weight_rows(weights):
    picks = lax.broadcasted_iota(jnp.int32, (BLOCK, LANES), 0) == lane_iota(BLOCK) % BLOCK
    return jnp.dot(
        weights,
        picks.astype(jnp.float32),
        precision=lax.Precision.HIGHEST,
        preferred_element_type=jnp.float32,
    )


def restrict_kernel(slots, bins, rows, cols, trajectory, weights, wind, mask, packed):
    rows_of_weights = weight_rows(weights[...])
    groups = slots * bins
    fine = trajectory[...].astype(jnp.float32).reshape(groups * rows, BLOCK, LANES)
    row_sums = jnp.sum(fine * rows_of_weights[None], axis=1)
    cell = lax.broadcasted_iota(jnp.int32, (LANES, LANES), 0) // BLOCK
    pool = (cell == lane_iota(LANES) % cols).astype(jnp.float32).astype(jnp.bfloat16)
    pooled = jnp.dot(three_parts(row_sums), pool, preferred_element_type=jnp.float32)
    count = groups * rows
    pooled = pooled[:count] + pooled[count : 2 * count] + pooled[2 * count :]
    group = lane_iota(rows) // cols
    filler = jnp.zeros((rows, bins * cols), jnp.float32)
    out = jnp.concatenate(
        [filler, wind[0], filler, mask[...].astype(jnp.float32)], axis=1
    )
    for slot in range(slots):
        for size in range(bins):
            start = (slot * bins + size) * rows
            out = jnp.where(
                group == slot * (bins + 1) + size, pooled[start : start + rows], out
            )
    packed[...] = out


def window_start(lat_count, rows, window):
    lat = lax.axis_index("lat")
    own = jnp.where(lat == 0, 0, jnp.where(lat == lat_count - 1, window - rows, REACH))
    return lat, own


def obs_kernel(lat_count, lon_total, rows, cols, window, columns, values, obs_weights, table):
    lat, own = window_start(lat_count, rows, window)
    first = pl.multiple_of(lat * rows - own, 8)
    span = pl.ds(first, window)
    slots = values.shape[0]
    obs = columns.shape[1]

    def turned(pieces):
        pad = jnp.zeros((HALF - window, obs), pieces[0].dtype)
        laid = []
        for piece in pieces:
            laid += [piece, pad] if window < HALF else [piece]
        return jnp.concatenate(laid, axis=0).T

    place = turned([columns[span, :].astype(jnp.float32)] * slots)
    weight = turned([obs_weights[slot, span, :] for slot in range(slots)])
    product = turned([obs_weights[slot, span, :] * values[slot, span, :] for slot in range(slots)])
    sub = lax.broadcasted_iota(jnp.int32, (HALF, LANES), 0)
    start = lax.axis_index("lon") * cols - cols + lon_total
    here = lax.rem(sub + start, lon_total).astype(jnp.float32)
    sum_weight = jnp.zeros((HALF, LANES), jnp.float32)
    sum_product = jnp.zeros((HALF, LANES), jnp.float32)
    for index in range(obs):
        hit = here == place[index : index + 1]
        sum_weight += jnp.where(hit, weight[index : index + 1], 0.0)
        sum_product += jnp.where(hit, product[index : index + 1], 0.0)
    both = jnp.concatenate([sum_weight, sum_product], axis=0).T
    left, right = both[:window], both[HALF : HALF + window]
    low = lane_iota(window) < HALF
    table[0] = jnp.where(low, left, pltpu.roll(right, HALF, 1))
    table[1] = jnp.where(low, pltpu.roll(left, HALF, 1), right)


def cycle_kernel(
    lat_count,
    slots,
    bins,
    rows,
    cols,
    window,
    own_cells,
    near_cells,
    far_cells,
    table,
    settling,
    weights,
    trajectory,
    analysis,
    correction,
    fine,
    here,
    there,
    coarse,
    change,
    winds,
    laid,
    copied,
):
    fetch = pltpu.make_async_copy(trajectory, fine, copied)
    fetch.start()
    levels = 2
    fields = levels * bins
    lat, own = window_start(lat_count, rows, window)
    level = lax.axis_index("lev")
    lon = lax.axis_index("lon")
    near_is_west = lax.rem(lon + level, 2)
    inner = slice(EDGE, EDGE + window)
    north = slice(EDGE + 1, EDGE + 1 + window)
    south = slice(EDGE - 1, EDGE - 1 + window)
    edge = jnp.zeros((EDGE, LANES), jnp.float32)
    for held in (here, there):
        for field in range(fields):
            held[field, :EDGE] = edge
            held[field, EDGE + window :] = edge

    def lay(place, block, rank):
        laid[place, pl.ds(pl.multiple_of(own, 8), rows)] = block[rank, :rows]
        if lat_count == 2:
            rim = pl.multiple_of(jnp.where(lat == 0, rows, 0), 8)
            laid[place, pl.ds(rim, REACH)] = block[rank, rows:]
        else:
            @pl.when(lat == 0)
            def _():
                laid[place, window - REACH :] = jnp.zeros((REACH, LANES), jnp.float32)

            @pl.when(lat == lat_count - 1)
            def _():
                laid[place, :REACH] = jnp.zeros((REACH, LANES), jnp.float32)

            @pl.when(lat > 0)
            def _():
                laid[place, pl.ds(pl.multiple_of(own - REACH, 8), REACH)] = block[rank, rows : rows + REACH]

            @pl.when(lat < lat_count - 1)
            def _():
                laid[place, pl.ds(pl.multiple_of(own + rows, 8), REACH)] = block[rank, rows + REACH :]

    for rank in range(levels):
        at = (rank + level) % levels
        lay(at * 3 + 2 * (1 - near_is_west), near_cells, rank)
        lay(at * 3 + 1, own_cells, rank)
        lay(at * 3 + 2 * near_is_west, far_cells, levels - 1 - rank)

    lane = lane_iota(window)
    spot = lane % HALF // cols
    low = lane < HALF
    mask = None
    for k in range(levels):
        blocks = [laid[3 * k + place] for place in range(3)]

        def gathered(group):
            out = jnp.zeros((window, LANES), jnp.float32)
            for place in range(3):
                turn = (place - group) * cols % LANES
                moved = pltpu.roll(blocks[place], turn, 1) if turn else blocks[place]
                out = jnp.where(spot == place, moved, out)
            return out

        for size in range(bins):
            cells = gathered(size)
            coarse[k * bins + size] = cells
            change[k * bins + size] = jnp.zeros((window, LANES), jnp.float32)
        sides = jnp.zeros((window, LANES), jnp.float32)
        for place in range(3):
            sides = jnp.where(spot == place, pltpu.roll(blocks[place], (place - 3) * cols % LANES, 1), sides)
        turned = pltpu.roll(sides, HALF, 1)
        wind = jnp.where(low, sides, turned)
        winds[3 * k] = 1.0 - 4.0 * diffusion - wind
        winds[3 * k + 1] = pltpu.roll(wind, 1, 1) + diffusion
        winds[3 * k + 2] = wind + diffusion
        if k == 0:
            mask = jnp.where(low, turned, sides)

    rates = [[settling[size, k] for k in range(levels)] for size in range(bins)]

    def spread_of(held, field, k, backward):
        cells = held[field, inner]
        west, east = pltpu.roll(cells, 1, 1), pltpu.roll(cells, LANES - 1, 1)
        swept, other = (east, west) if backward else (west, east)
        near = diffusion * (held[field, north] + held[field, south] + other)
        return cells, near + winds[3 * k + 1 + backward] * swept + winds[3 * k] * cells

    def step(source, target, backward):
        for k in range(levels):
            for size in range(bins):
                field = k * bins + size
                cells, moved = spread_of(source, field, k, backward)
                moved -= rates[size][k] * cells
                if backward and k + 1 < levels:
                    moved += rates[size][k] * source[field + bins, inner]
                if not backward and k > 0:
                    moved += rates[size][k - 1] * source[field - bins, inner]
                target[field, inner] = moved

    def sweep(index, carry):
        for field in range(fields):
            here[field, inner] = coarse[field] + change[field]
        pair = (here, there)
        for count in range(STEPS - 1):
            step(pair[count % 2], pair[(count + 1) % 2], False)
        held, free = pair[(STEPS - 1) % 2], pair[STEPS % 2]
        total = jnp.zeros((window, LANES), jnp.float32)
        for k in range(levels):
            summed = held[k * bins, inner]
            for size in range(1, bins):
                summed += held[k * bins + size, inner]
            free[k, inner] = summed
            total += spread_of(free, k, k, False)[1]
        for size in range(bins):
            total -= rates[size][levels - 1] * held[(levels - 1) * bins + size, inner]
        scale = 1.0 / fields
        held[0, inner] = table[0] * (total * (scale * scale)) - table[1] * scale
        source, target = held, free
        for k in range(levels):
            cells, moved = spread_of(source, 0, k, True)
            for size in range(bins):
                last = k == levels - 1
                target[k * bins + size, inner] = moved - rates[size][k] * cells if last else moved
        for count in range(STEPS - 1):
            source, target = target, source
            step(source, target, True)
        for field in range(fields):
            old = change[field]
            gradient = background * old + target[field, inner]
            change[field] = mask * (old - step_length * gradient)
        return carry

    lax.fori_loop(0, SWEEPS, sweep, 0)

    at = pl.ds(pl.multiple_of(own, 8), rows)
    final = [change[level * bins + size, at] for size in range(bins)]
    for size in range(bins):
        for slot in range(slots):
            moved = pltpu.roll(final[size], (LANES - slot * HALF - cols) % LANES, 1)
            correction[slot, size, 0] = moved[:, :cols]
    source_lane = lax.broadcasted_iota(jnp.int32, (LANES, slots * LANES), 0)
    target_lane = lax.broadcasted_iota(jnp.int32, (LANES, slots * LANES), 1)
    picks = source_lane == target_lane // LANES * HALF + cols + target_lane % LANES // BLOCK
    picks = picks.astype(jnp.float32).astype(jnp.bfloat16)
    wide = jnp.dot(three_parts(jnp.concatenate(final, axis=0)), picks, preferred_element_type=jnp.float32)
    count = bins * rows
    wide = wide[:count] + wide[count : 2 * count] + wide[2 * count :]
    growth = (BLOCK * BLOCK) * weight_rows(weights[...])
    fetch.wait()
    for slot in range(slots):
        for size in range(bins):
            cells = wide[size * rows : (size + 1) * rows, slot * LANES : (slot + 1) * LANES]
            raised = (cells[:, None, :] * growth[None]).reshape(rows * BLOCK, LANES)
            analysis[slot, size, 0] = (fine[slot, size, 0].astype(jnp.float32) + raised).astype(jnp.bfloat16)


def solution(mesh):
    lon_count, lat_count, lev_count = (mesh.shape[axis] for axis in AXES)

    def place_of(lon, lat, lev):
        return (lon % lon_count * lat_count + lat) * lev_count + lev

    def moved(values, source_of):
        pairs = []
        for lon in range(lon_count):
            for lat in range(lat_count):
                for lev in range(lev_count):
                    source = source_of(lon, lat, lev)
                    if source is not None:
                        pairs.append((place_of(*source), place_of(lon, lat, lev)))
        return lax.ppermute(values, AXES, pairs)

    def per_device(
        trajectory,
        block_weights,
        wind_speed,
        settling,
        source_mask,
        obs_columns,
        obs_values,
        obs_weights,
    ):
        slots, bins, _, fine_rows, fine_cols = trajectory.shape
        rows, cols = fine_rows // BLOCK, fine_cols // BLOCK
        rims = min(lat_count - 1, 2)
        window = rows + rims * REACH
        in_vmem = pl.BlockSpec(memory_space=pltpu.VMEM)
        anywhere = pl.BlockSpec(memory_space=pl.ANY)

        def restrict(*refs):
            restrict_kernel(slots, bins, rows, cols, *refs)

        packed = pl.pallas_call(
            restrict,
            out_shape=jax.ShapeDtypeStruct((rows, LANES), jnp.float32),
            in_specs=[in_vmem] * 4,
            out_specs=in_vmem,
        )(trajectory, block_weights, wind_speed, source_mask)

        def tabulate(*refs):
            obs_kernel(lat_count, lon_count * cols, rows, cols, window, *refs)

        table = pl.pallas_call(
            tabulate,
            out_shape=jax.ShapeDtypeStruct((2, window, LANES), jnp.float32),
            in_specs=[in_vmem] * 3,
            out_specs=in_vmem,
        )(obs_columns, obs_values, obs_weights)

        other = moved(packed, lambda lon, lat, lev: (lon, lat, 1 - lev))
        levels = jnp.stack([packed, other])
        if lat_count == 2:
            rim = lax.dynamic_slice_in_dim(levels, (1 - lax.axis_index("lat")) * (rows - REACH), REACH, 1)
            rim = moved(rim, lambda lon, lat, lev: (lon, 1 - lat, 1 - lev))
            own = jnp.concatenate([levels, rim[::-1]], axis=1)
        else:
            low = moved(
                levels[:, rows - REACH :],
                lambda lon, lat, lev: (lon, lat - 1, 1 - lev) if lat > 0 else None,
            )
            high = moved(
                levels[:, :REACH],
                lambda lon, lat, lev: (lon, lat + 1, 1 - lev) if lat < lat_count - 1 else None,
            )
            own = jnp.concatenate([levels, low[::-1], high[::-1]], axis=1)
        near = moved(own, lambda lon, lat, lev: (lon ^ 1 if lev == 0 else lon + 1 - 2 * ((lon + 1) % 2), lat, lev))
        far = moved(near, lambda lon, lat, lev: (lon, lat, 1 - lev))

        def cycle(*refs):
            cycle_kernel(lat_count, slots, bins, rows, cols, window, *refs)

        fields = 2 * bins
        field_store = pltpu.VMEM((fields, window, LANES), jnp.float32)
        step_store = pltpu.VMEM((fields, window + 2 * EDGE, LANES), jnp.float32)
        return pl.pallas_call(
            cycle,
            out_shape=(
                jax.ShapeDtypeStruct(trajectory.shape, jnp.bfloat16),
                jax.ShapeDtypeStruct((slots, bins, 1, rows, cols), jnp.float32),
            ),
            in_specs=[in_vmem] * 4 + [pl.BlockSpec(memory_space=pltpu.SMEM), in_vmem, anywhere],
            out_specs=(in_vmem, in_vmem),
            scratch_shapes=[
                pltpu.VMEM(trajectory.shape, jnp.bfloat16),
                step_store,
                step_store,
                field_store,
                field_store,
                pltpu.VMEM((6, window, LANES), jnp.float32),
                pltpu.VMEM((6, window, LANES), jnp.float32),
                pltpu.SemaphoreType.DMA,
            ],
        )(own, near, far, table, settling, block_weights, trajectory)

    placed = (
        P("member", None, "lev", "lat", "lon"),
        P(),
        P("lev", "lat", "lon"),
        P(),
        P("lat", "lon"),
        P("member", None),
        P("member", None, None),
        P("member", None, None),
    )
    return jax.shard_map(
        per_device,
        mesh=mesh,
        in_specs=placed,
        out_specs=(P("member", None, "lev", "lat", "lon"), P("member", None, "lev", "lat", "lon")),
        check_vma=False,
    )
```

time: 421 us -> 27.6 us (0.07)
  blocking collectives: 126 us -> 0 us
  waiting for transfers between devices: 121 us -> 4.57 us
  starting transfers between devices: 99.1 us -> 6.48 us
  matrix products: 25.1 us -> 0 us
  local copies, waits for them, and re-layouts: 27.8 us -> 7.13 us
  other arithmetic: 19.1 us -> 0.01 us
  Pallas kernels: 0 us -> 8.32 us
    psum x2 -> x0, blocking collectives: 122 us -> none  [per_device(): observed = lax.psum(placed, ('lon', 'lat', 'lev'))]
    ppermute x64 -> x4, waiting for transfers between devices: 121 us -> 4.57 us  [moved(): return lax.ppermute(values, AXES, pairs)]
    ppermute x64 -> x4, starting transfers between devices: 92.6 us -> 6.48 us  [moved(): return lax.ppermute(values, AXES, pairs)]
    dot_general x5 -> x0, matrix products: 25.1 us -> none  [the longest x1 24 us: per_device(): jnp.einsum('sbkiajc,ac->sbkij', blocks, block_weights, precision=highest)]
    another operation x43 -> x0, local copies, waits for them, and re-layouts: 11.8 us -> none
    reshape x1 -> x0, local copies, waits for them, and re-layouts: 9.07 us -> none  [per_device(): increment.reshape(slot_count, bin_count, level_block, fine_rows, fine_cols)]
    pallas_call x0 -> x3, Pallas kernels: none -> 8.32 us  [the longest x1 3.99 us: per_device(): pl.pallas_call(cycle, out_shape=(jax.ShapeDtypeStruct(trajectory.shape, j...]
    all_to_all x2 -> x0, starting transfers between devices: 6.45 us -> none  [the longest x1 3.23 us: per_device(): lax.all_to_all(restricted, 'lev', split_axis=3, concat_axis=2, tiled=True)]
  transfers between devices with their start and end apart: 66 -> 4, of which waited for: 51 -> 3; matrix products, arithmetic and copies ran while one was open for 9% -> 10% of each run, Pallas kernels for 0% -> 7%
where the time goes in v1:
time: 27.6 us; the launch traced here: 27.2 us
  Pallas kernels  8.32 us (30%)
  local copies, waits for them, and re-layouts  7.13 us (26%)
  starting transfers between devices  6.48 us (23%)
  waiting for transfers between devices  4.57 us (17%)
  between operations  0.68 us (2%)
    ppermute x4, starting transfers between devices, moved(): return lax.ppermute(values, AXES, pairs)  6.48 us
    unnamed x24, local copies, waits for them, and re-layouts  5.53 us
    ppermute x4, waiting for transfers between devices, moved(): return lax.ppermute(values, AXES, pairs)  4.57 us
    pallas_call x1, Pallas kernels, per_device(): pl.pallas_call(cycle, out_shape=(jax.ShapeDtypeStruct(trajectory.shape, j...  3.99 us
    pallas_call x1, Pallas kernels, per_device(): pl.pallas_call(restrict, out_shape=jax.ShapeDtypeStruct((rows, LANES), jn...  2.41 us
    pallas_call x1, Pallas kernels, per_device(): pl.pallas_call(tabulate, out_shape=jax.ShapeDtypeStruct((2, window, LANES...  1.92 us
    pallas_call x1, local copies, waits for them, and re-layouts, per_device(): pl.pallas_call(cycle, out_shape=(jax.ShapeDtypeStruct(trajectory.shape, j...  1.6 us
  transfers between devices with their start and end apart: 4, of which 3 were waited for; matrix products, arithmetic and copies ran while one was open for 10% of the time, Pallas kernels for 7%

profile of v1, /device:TPU:0, one launch (start us, length us, event | category | flops | bytes accessed | tf_op | source)
XLA Modules:
  0.0 27.2 jit_solution(7836658460277400745)
XLA Ops:
  0.6 1.4 %copy.10.refs_2_ = f32[1,32,16]{2,1,0:T(8,128)} copy(f32[1,32,16]{1,2,0:T(8,128)} %param.10) | data formatting | bytes 4096 | tf_op args[2]
  2.0 0.7 %copy.11.refs_3_ = s32[32,16]{1,0:T(8,128)} copy(s32[32,16]{0,1:T(8,128)S(1)} %copy-done.7) | data formatting | bytes 4096 | tf_op args[4]
  2.7 2.4 %shard_map.95 = f32[32,128]{1,0:T(8,128)} custom-call(bf16[2,3,1,256,128]{4,3,2,1,0:T(8,128)(2,1)} %refs_6_.1, f32[8,8]{1,0:T(8,128)} %refs_5_.1, f32[1,32,16]{2,1,0:T(8,128)} %copy.10.refs_2_, s32[32,16]{1,0:T(8,128)} %copy.11.refs_3_), custom_call_target="tpu_custom_call" | custom-call | tf_op jit(solution)/shard_map/pallas_call | solution.py:321
  5.1 0.5 %collective-permute-start = (f32[32,128]{1,0:T(8,128)}, f32[32,128]{1,0:T(8,128)S(1)}, u32[]{:S(2)}, u32[]{:S(2)}) collective-permute-start(f32[32,128]{1,0:T(8,128)} %shard_map.95), channel_id=1, source_target_pairs={{1,0},{0,1},{3,2},{2,3},{5,4},{4,5},{7,6},{6,7},{9,8},{8,9},{11,10... | collective-permute-start | bytes 49160 | tf_op jit(solution)/shard_map/ppermute | solution.py:299
  5.6 1.0 %collective-permute-done = f32[32,128]{1,0:T(8,128)S(1)} collective-permute-done((f32[32,128]{1,0:T(8,128)}, f32[32,128]{1,0:T(8,128)S(1)}, u32[]{:S(2)}, u32[]{:S(2)}) %collective-permute-start) | collective-permute-done | bytes 16416 | tf_op jit(solution)/shard_map/ppermute | solution.py:299
  6.6 2.6 %collective-permute-start.1 = (f32[2,16,128]{2,1,0:T(8,128)S(1)}, f32[2,16,128]{2,1,0:T(8,128)S(1)}, u32[]{:S(2)}, u32[]{:S(2)}) collective-permute-start(f32[2,16,128]{2,1,0:T(8,128)S(1)} %fusion), channel_id=1, source_target_pairs={{3,0},{2,1},{1,2},{0,3},{7,4},{6,5},{5,6},{4,7},{11,8},{10,9},{9,1... | collective-permute-start | bytes 49160 | tf_op jit(solution)/shard_map/ppermute | solution.py:299
  9.2 1.4 %collective-permute-done.1 = f32[2,16,128]{2,1,0:T(8,128)S(1)} collective-permute-done((f32[2,16,128]{2,1,0:T(8,128)S(1)}, f32[2,16,128]{2,1,0:T(8,128)S(1)}, u32[]{:S(2)}, u32[]{:S(2)}) %collective-permute-start.1) | collective-permute-done | bytes 16416 | tf_op jit(solution)/shard_map/ppermute | solution.py:299
  10.7 0.0 copy-start
  10.7 0.0 copy-start.4
  10.7 2.1 %collective-permute-start.2 = (f32[2,48,128]{2,1,0:T(8,128)S(1)}, f32[2,48,128]{2,1,0:T(8,128)S(1)}, u32[]{:S(2)}, u32[]{:S(2)}) collective-permute-start(f32[2,48,128]{2,1,0:T(8,128)S(1)} %pad_maximum_fusion.refs_0_), channel_id=1, source_target_pairs={{4,0},{13,1},{6,2},{15,3},{0,4},{9,5},{2,6},{11,7},{12,8},{5,9},{1... | collective-permute-start | bytes 147464 | tf_op jit(solution)/shard_map/ppermute | solution.py:299
  12.8 2.1 %collective-permute-done.2.refs_1_ = f32[2,48,128]{2,1,0:T(8,128)S(1)} collective-permute-done((f32[2,48,128]{2,1,0:T(8,128)S(1)}, f32[2,48,128]{2,1,0:T(8,128)S(1)}, u32[]{:S(2)}, u32[]{:S(2)}) %collective-permute-start.2) | collective-permute-done | bytes 49184 | tf_op jit(solution)/shard_map/ppermute | solution.py:299
  14.9 1.3 %collective-permute-start.3 = (f32[2,48,128]{2,1,0:T(8,128)S(1)}, f32[2,48,128]{2,1,0:T(8,128)S(1)}, u32[]{:S(2)}, u32[]{:S(2)}) collective-permute-start(f32[2,48,128]{2,1,0:T(8,128)S(1)} %collective-permute-done.2.refs_1_), channel_id=1, source_target_pairs={{1,0},{0,1},{3,2},{2,3},{5,4},{4,5},{7,6},{6,7},{9,8},{8,9},{11,10... | collective-permute-start | bytes 147464 | tf_op jit(solution)/shard_map/ppermute | solution.py:299
  16.2 0.0 copy-done.8
  16.2 0.7 %copy.15.refs_4_ = f32[3,2]{1,0:T(4,128)} copy(f32[3,2]{0,1:T(2,128)S(1)} %copy-done.8) | data formatting | bytes 48 | tf_op args[3]
  16.9 0.7 %copy.12.refs_0_ = s32[64,32]{1,0:T(8,128)} copy(s32[64,32]{0,1:T(8,128)S(1)} %copy-done.6) | data formatting | bytes 16384 | tf_op args[5]
  17.6 0.7 %copy.13.refs_1_ = f32[2,64,32]{2,1,0:T(8,128)} copy(f32[2,64,32]{1,2,0:T(8,128)S(1)} %copy-done.4) | data formatting | bytes 32768 | tf_op args[6]
  18.3 0.0 copy-done
  18.3 0.0 copy-done.5
  18.3 0.7 %copy.14.refs_2_ = f32[2,64,32]{2,1,0:T(8,128)} copy(f32[2,64,32]{1,2,0:T(8,128)S(1)} %copy-done.5) | data formatting | bytes 32768 | tf_op args[7]
  19.0 1.9 %shard_map.96.refs_3_ = f32[2,48,128]{2,1,0:T(8,128)} custom-call(s32[64,32]{1,0:T(8,128)} %copy.12.refs_0_, f32[2,64,32]{2,1,0:T(8,128)} %copy.13.refs_1_, f32[2,64,32]{2,1,0:T(8,128)} %copy.14.refs_2_), custom_call_target="tpu_custom_call" | custom-call | tf_op jit(solution)/shard_map/pallas_call | solution.py:331
  21.0 0.0 collective-permute-done.3.refs_2_
  21.0 0.6 %copy-done.3 = f32[2,48,128]{2,1,0:T(8,128)} copy-done((f32[2,48,128]{2,1,0:T(8,128)}, f32[2,48,128]{2,1,0:T(8,128)S(1)}, u32[]{:S(2)}) %copy-start.3) | copy-done | bytes 49176
  21.6 4.0 %shard_map.97 = (bf16[2,3,1,256,128]{4,3,2,1,0:T(8,128)(2,1)}, f32[2,3,1,32,16]{4,3,2,1,0:T(8,128)}) custom-call(f32[2,48,128]{2,1,0:T(8,128)} %copy-done, f32[2,48,128]{2,1,0:T(8,128)} %copy-done.2, f32[2,48,128]{2,1,0:T(8,128)} %copy-done.3, f32[2,48,128]{2,1,0:T(8,128)} %shard_map.96.refs_3_, f32[3,2]{1,0:T(4,128)} %copy.15.refs_4_, f32[8,8]{1,0:T(8,128)} %refs_5_.1, ...), custom_call_target="tpu_custom_call" | custom-call | tf_op jit(solution)/shard_map/pallas_call | solution.py:363
  25.6 1.6 %copy.16 = f32[2,3,1,32,16]{3,4,2,1,0:T(8,128)} copy(f32[2,3,1,32,16]{4,3,2,1,0:T(8,128)} %get-tuple-element.3) | data formatting | bytes 24576 | tf_op jit(solution)/shard_map/pallas_call | solution.py:363
  (15 shorter events, 0.0 us)
Async XLA Ops:
  0.6 1.4 %copy-start.7 = (s32[32,16]{0,1:T(8,128)S(1)}, s32[32,16]{0,1:T(8,128)}, u32[]{:S(2)}) copy-start(s32[32,16]{0,1:T(8,128)} %param.12) | copy-start | bytes 6148
  5.1 1.5 %copy-start.1 = (f32[32,128]{1,0:T(8,128)S(1)}, f32[32,128]{1,0:T(8,128)}, u32[]{:S(2)}) copy-start(f32[32,128]{1,0:T(8,128)} %shard_map.95) | copy-start | bytes 49156
  5.1 1.5 %collective-permute-start = (f32[32,128]{1,0:T(8,128)}, f32[32,128]{1,0:T(8,128)S(1)}, u32[]{:S(2)}, u32[]{:S(2)}) collective-permute-start(f32[32,128]{1,0:T(8,128)} %shard_map.95), channel_id=1, source_target_pairs={{1,0},{0,1},{3,2},{2,3},{5,4},{4,5},{7,6},{6,7},{9,8},{8,9},{11,10... | collective-permute-start | bytes 49160 | tf_op jit(solution)/shard_map/ppermute | solution.py:299
  6.6 4.0 %collective-permute-start.1 = (f32[2,16,128]{2,1,0:T(8,128)S(1)}, f32[2,16,128]{2,1,0:T(8,128)S(1)}, u32[]{:S(2)}, u32[]{:S(2)}) collective-permute-start(f32[2,16,128]{2,1,0:T(8,128)S(1)} %fusion), channel_id=1, source_target_pairs={{3,0},{2,1},{1,2},{0,3},{7,4},{6,5},{5,6},{4,7},{11,8},{10,9},{9,1... | collective-permute-start | bytes 49160 | tf_op jit(solution)/shard_map/ppermute | solution.py:299
  10.7 5.5 %copy-start.8 = (f32[3,2]{0,1:T(2,128)S(1)}, f32[3,2]{0,1:T(2,128)}, u32[]{:S(2)}) copy-start(f32[3,2]{0,1:T(2,128)} %param.11) | copy-start | bytes 76
  10.7 6.2 %copy-start.6 = (s32[64,32]{0,1:T(8,128)S(1)}, s32[64,32]{0,1:T(8,128)}, u32[]{:S(2)}) copy-start(s32[64,32]{0,1:T(8,128)} %param.13) | copy-start | bytes 24580
  10.7 7.6 %copy-start = (f32[2,48,128]{2,1,0:T(8,128)}, f32[2,48,128]{2,1,0:T(8,128)S(1)}, u32[]{:S(2)}) copy-start(f32[2,48,128]{2,1,0:T(8,128)S(1)} %pad_maximum_fusion.refs_0_) | copy-start | bytes 147460
  10.7 6.9 %copy-start.4 = (f32[2,64,32]{1,2,0:T(8,128)S(1)}, f32[2,64,32]{1,2,0:T(8,128)}, u32[]{:S(2)}) copy-start(f32[2,64,32]{1,2,0:T(8,128)} %param.14) | copy-start | bytes 49156
  10.7 4.2 %collective-permute-start.2 = (f32[2,48,128]{2,1,0:T(8,128)S(1)}, f32[2,48,128]{2,1,0:T(8,128)S(1)}, u32[]{:S(2)}, u32[]{:S(2)}) collective-permute-start(f32[2,48,128]{2,1,0:T(8,128)S(1)} %pad_maximum_fusion.refs_0_), channel_id=1, source_target_pairs={{4,0},{13,1},{6,2},{15,3},{0,4},{9,5},{2,6},{11,7},{12,8},{5,9},{1... | collective-permute-start | bytes 147464 | tf_op jit(solution)/shard_map/ppermute | solution.py:299
  14.9 3.4 %copy-start.2 = (f32[2,48,128]{2,1,0:T(8,128)}, f32[2,48,128]{2,1,0:T(8,128)S(1)}, u32[]{:S(2)}) copy-start(f32[2,48,128]{2,1,0:T(8,128)S(1)} %collective-permute-done.2.refs_1_) | copy-start | bytes 147460
  14.9 6.1 %collective-permute-start.3 = (f32[2,48,128]{2,1,0:T(8,128)S(1)}, f32[2,48,128]{2,1,0:T(8,128)S(1)}, u32[]{:S(2)}, u32[]{:S(2)}) collective-permute-start(f32[2,48,128]{2,1,0:T(8,128)S(1)} %collective-permute-done.2.refs_1_), channel_id=1, source_target_pairs={{1,0},{0,1},{3,2},{2,3},{5,4},{4,5},{7,6},{6,7},{9,8},{8,9},{11,10... | collective-permute-start | bytes 147464 | tf_op jit(solution)/shard_map/ppermute | solution.py:299
  17.6 0.8 %copy-start.5 = (f32[2,64,32]{1,2,0:T(8,128)S(1)}, f32[2,64,32]{1,2,0:T(8,128)}, u32[]{:S(2)}) copy-start(f32[2,64,32]{1,2,0:T(8,128)} %param.15) | copy-start | bytes 49156
  21.0 0.6 %copy-start.3 = (f32[2,48,128]{2,1,0:T(8,128)}, f32[2,48,128]{2,1,0:T(8,128)S(1)}, u32[]{:S(2)}) copy-start(f32[2,48,128]{2,1,0:T(8,128)S(1)} %collective-permute-done.3.refs_2_) | copy-start | bytes 147460

commit v2 on v1

--- a/solution.py
+++ b/solution.py
@@ -32,37 +32,49 @@
 
 
 def weight_rows(weights):
-    picks = lax.broadcasted_iota(jnp.int32, (BLOCK, LANES), 0) == lane_iota(BLOCK) % BLOCK
-    return jnp.dot(
-        weights,
-        picks.astype(jnp.float32),
-        precision=lax.Precision.HIGHEST,
-        preferred_element_type=jnp.float32,
-    )
-
-
-def restrict_kernel(slots, bins, rows, cols, trajectory, weights, wind, mask, packed):
+    return jnp.concatenate([weights] * (LANES // BLOCK), axis=1)
+
+
+def fetch_all(sources, held, copied):
+    fetches = [
+        pltpu.make_async_copy(source, target, copied.at[index])
+        for index, (source, target) in enumerate(zip(sources, held))
+    ]
+    for fetch in fetches:
+        fetch.start()
+    for fetch in fetches:
+        fetch.wait()
+
+
+def restrict_kernel(lat_count, slots, bins, rows, cols, *refs):
+    sources, packed, held, fine, copied = refs[:4], refs[4], refs[5:9], refs[9], refs[10]
+    fetch_all(sources, held, copied)
+    trajectory, weights, wind, mask = held
     rows_of_weights = weight_rows(weights[...])
-    groups = slots * bins
-    fine = trajectory[...].astype(jnp.float32).reshape(groups * rows, BLOCK, LANES)
-    row_sums = jnp.sum(fine * rows_of_weights[None], axis=1)
+    count = slots * bins * rows
+    fine[...] = trajectory[...].reshape(count * BLOCK, LANES).astype(jnp.float32)
+    row_sums = fine[pl.ds(0, count, stride=BLOCK), :] * rows_of_weights[:1]
+    for index in range(1, BLOCK):
+        row_sums += fine[pl.ds(index, count, stride=BLOCK), :] * rows_of_weights[index : index + 1]
     cell = lax.broadcasted_iota(jnp.int32, (LANES, LANES), 0) // BLOCK
     pool = (cell == lane_iota(LANES) % cols).astype(jnp.float32).astype(jnp.bfloat16)
     pooled = jnp.dot(three_parts(row_sums), pool, preferred_element_type=jnp.float32)
-    count = groups * rows
     pooled = pooled[:count] + pooled[count : 2 * count] + pooled[2 * count :]
     group = lane_iota(rows) // cols
-    filler = jnp.zeros((rows, bins * cols), jnp.float32)
-    out = jnp.concatenate(
-        [filler, wind[0], filler, mask[...].astype(jnp.float32)], axis=1
-    )
+    filler = jnp.zeros((bins * cols, rows), jnp.float32)
+    out = jnp.concatenate([filler, wind[0], filler, mask[...].astype(jnp.float32)], axis=0).T
     for slot in range(slots):
         for size in range(bins):
             start = (slot * bins + size) * rows
             out = jnp.where(
                 group == slot * (bins + 1) + size, pooled[start : start + rows], out
             )
-    packed[...] = out
+    if lat_count == 2:
+        start = pl.multiple_of(jnp.where(lax.axis_index("lat") == 0, rows - REACH, 0), 8)
+        packed[pl.ds(start, REACH)] = out[:REACH]
+        packed[pl.ds(pl.multiple_of(rows - REACH - start, 8), REACH)] = out[REACH:]
+    else:
+        packed[...] = out
 
 
 def window_start(lat_count, rows, window):
@@ -71,23 +83,28 @@
     return lat, own
 
 
-def obs_kernel(lat_count, lon_total, rows, cols, window, columns, values, obs_weights, table):
+def obs_kernel(lat_count, lon_total, rows, cols, window, *refs):
+    sources, (table, scales), held, copied = refs[:5], refs[5:7], refs[7:12], refs[12]
+    fetch_all(sources, held, copied)
+    columns, values, obs_weights, settling, weights = held
     lat, own = window_start(lat_count, rows, window)
-    first = pl.multiple_of(lat * rows - own, 8)
-    span = pl.ds(first, window)
-    slots = values.shape[0]
-    obs = columns.shape[1]
-
-    def turned(pieces):
-        pad = jnp.zeros((HALF - window, obs), pieces[0].dtype)
-        laid = []
-        for piece in pieces:
-            laid += [piece, pad] if window < HALF else [piece]
-        return jnp.concatenate(laid, axis=0).T
-
-    place = turned([columns[span, :].astype(jnp.float32)] * slots)
-    weight = turned([obs_weights[slot, span, :] for slot in range(slots)])
-    product = turned([obs_weights[slot, span, :] * values[slot, span, :] for slot in range(slots)])
+    first = lat * rows - own
+    slots, obs, lat_total = values.shape
+    wide = -(-lat_total // LANES) * LANES
+    low = lane_iota(obs) < HALF
+
+    def windowed(array):
+        if wide > lat_total:
+            array = jnp.concatenate([array, jnp.zeros((obs, wide - lat_total), array.dtype)], axis=1)
+        return pltpu.roll(array, lax.rem(wide - first, wide), 1)[:, :LANES]
+
+    def paired(first_slot, second_slot):
+        return jnp.where(low, windowed(first_slot), pltpu.roll(windowed(second_slot), HALF, 1))
+
+    held = columns[...].astype(jnp.float32)
+    place = paired(held, held)
+    weight = paired(obs_weights[0], obs_weights[1])
+    product = paired(obs_weights[0] * values[0], obs_weights[1] * values[1])
     sub = lax.broadcasted_iota(jnp.int32, (HALF, LANES), 0)
     start = lax.axis_index("lon") * cols - cols + lon_total
     here = lax.rem(sub + start, lon_total).astype(jnp.float32)
@@ -102,6 +119,12 @@
     low = lane_iota(window) < HALF
     table[0] = jnp.where(low, left, pltpu.roll(right, HALF, 1))
     table[1] = jnp.where(low, pltpu.roll(left, HALF, 1), right)
+    levels, bins = settling.shape
+    for k in range(levels):
+        for size in range(bins):
+            rate = settling[k : k + 1, size : size + 1]
+            scales[k * bins + size] = jnp.broadcast_to(rate, (BLOCK, LANES))
+    scales[levels * bins] = (BLOCK * BLOCK) * weight_rows(weights[...])
 
 
 def cycle_kernel(
@@ -115,8 +138,7 @@
     near_cells,
     far_cells,
     table,
-    settling,
-    weights,
+    scales,
     trajectory,
     analysis,
     correction,
@@ -147,11 +169,14 @@
             held[field, EDGE + window :] = edge
 
     def lay(place, block, rank):
-        laid[place, pl.ds(pl.multiple_of(own, 8), rows)] = block[rank, :rows]
         if lat_count == 2:
-            rim = pl.multiple_of(jnp.where(lat == 0, rows, 0), 8)
-            laid[place, pl.ds(rim, REACH)] = block[rank, rows:]
+            outer = pl.multiple_of(lat * 2 * REACH, 8)
+            laid[place, REACH : 2 * REACH] = block[rank, :REACH]
+            laid[place, pl.ds(outer, REACH)] = block[rank, REACH:rows]
+            laid[place, pl.ds(pl.multiple_of(2 * REACH - outer, 8), REACH)] = block[rank, rows:]
         else:
+            laid[place, pl.ds(pl.multiple_of(own, 8), rows)] = block[rank, :rows]
+
             @pl.when(lat == 0)
             def _():
                 laid[place, window - REACH :] = jnp.zeros((REACH, LANES), jnp.float32)
@@ -204,7 +229,7 @@
         if k == 0:
             mask = jnp.where(low, turned, sides)
 
-    rates = [[settling[size, k] for k in range(levels)] for size in range(bins)]
+    rates = [[scales[k * bins + size, :1] for k in range(levels)] for size in range(bins)]
 
     def spread_of(held, field, k, backward):
         cells = held[field, inner]
@@ -263,9 +288,10 @@
     at = pl.ds(pl.multiple_of(own, 8), rows)
     final = [change[level * bins + size, at] for size in range(bins)]
     for size in range(bins):
+        turned = final[size].T
         for slot in range(slots):
-            moved = pltpu.roll(final[size], (LANES - slot * HALF - cols) % LANES, 1)
-            correction[slot, size, 0] = moved[:, :cols]
+            start = slot * HALF + cols
+            correction[slot, size, 0] = turned[start : start + cols]
     source_lane = lax.broadcasted_iota(jnp.int32, (LANES, slots * LANES), 0)
     target_lane = lax.broadcasted_iota(jnp.int32, (LANES, slots * LANES), 1)
     picks = source_lane == target_lane // LANES * HALF + cols + target_lane % LANES // BLOCK
@@ -273,7 +299,7 @@
     wide = jnp.dot(three_parts(jnp.concatenate(final, axis=0)), picks, preferred_element_type=jnp.float32)
     count = bins * rows
     wide = wide[:count] + wide[count : 2 * count] + wide[2 * count :]
-    growth = (BLOCK * BLOCK) * weight_rows(weights[...])
+    growth = scales[levels * bins]
     fetch.wait()
     for slot in range(slots):
         for size in range(bins):
@@ -312,34 +338,60 @@
         rows, cols = fine_rows // BLOCK, fine_cols // BLOCK
         rims = min(lat_count - 1, 2)
         window = rows + rims * REACH
+        small = pltpu.CompilerParams(vmem_limit_bytes=8 * 1024 * 1024)
         in_vmem = pl.BlockSpec(memory_space=pltpu.VMEM)
-        anywhere = pl.BlockSpec(memory_space=pl.ANY)
+
+        def kept(array):
+            return pltpu.with_memory_space_constraint(array, pltpu.HBM)
+
+        in_hbm = pl.BlockSpec(memory_space=pltpu.HBM)
 
         def restrict(*refs):
-            restrict_kernel(slots, bins, rows, cols, *refs)
+            restrict_kernel(lat_count, slots, bins, rows, cols, *refs)
 
         packed = pl.pallas_call(
             restrict,
-            out_shape=jax.ShapeDtypeStruct((rows, LANES), jnp.float32),
-            in_specs=[in_vmem] * 4,
+            out_shape=pltpu.VMEM((rows, LANES), jnp.float32),
+            in_specs=[in_hbm] * 4,
             out_specs=in_vmem,
-        )(trajectory, block_weights, wind_speed, source_mask)
+            scratch_shapes=[
+                pltpu.VMEM(trajectory.shape, jnp.bfloat16),
+                pltpu.VMEM((BLOCK, BLOCK), jnp.float32),
+                pltpu.VMEM((1, cols, rows), jnp.float32),
+                pltpu.VMEM((cols, rows), jnp.int32),
+                pltpu.VMEM((slots * bins * fine_rows, LANES), jnp.float32),
+                pltpu.SemaphoreType.DMA((4,)),
+            ],
+            compiler_params=small,
+        )(*map(kept, (trajectory, block_weights, wind_speed.swapaxes(1, 2), source_mask.T)))
 
         def tabulate(*refs):
             obs_kernel(lat_count, lon_count * cols, rows, cols, window, *refs)
 
-        table = pl.pallas_call(
+        observed = (
+            obs_columns.T,
+            obs_values.swapaxes(1, 2),
+            obs_weights.swapaxes(1, 2),
+            settling.T,
+            block_weights,
+        )
+        table, scales = pl.pallas_call(
             tabulate,
-            out_shape=jax.ShapeDtypeStruct((2, window, LANES), jnp.float32),
-            in_specs=[in_vmem] * 3,
-            out_specs=in_vmem,
-        )(obs_columns, obs_values, obs_weights)
+            out_shape=(
+                pltpu.VMEM((2, window, LANES), jnp.float32),
+                pltpu.VMEM((2 * bins + 1, BLOCK, LANES), jnp.float32),
+            ),
+            in_specs=[in_hbm] * 5,
+            out_specs=(in_vmem, in_vmem),
+            scratch_shapes=[pltpu.VMEM(array.shape, array.dtype) for array in observed]
+            + [pltpu.SemaphoreType.DMA((5,))],
+            compiler_params=small,
+        )(*map(kept, observed))
 
         other = moved(packed, lambda lon, lat, lev: (lon, lat, 1 - lev))
         levels = jnp.stack([packed, other])
         if lat_count == 2:
-            rim = lax.dynamic_slice_in_dim(levels, (1 - lax.axis_index("lat")) * (rows - REACH), REACH, 1)
-            rim = moved(rim, lambda lon, lat, lev: (lon, 1 - lat, 1 - lev))
+            rim = moved(levels[:, :REACH], lambda lon, lat, lev: (lon, 1 - lat, 1 - lev))
             own = jnp.concatenate([levels, rim[::-1]], axis=1)
         else:
             low = moved(
@@ -352,6 +404,7 @@
             )
             own = jnp.concatenate([levels, low[::-1], high[::-1]], axis=1)
         near = moved(own, lambda lon, lat, lev: (lon ^ 1 if lev == 0 else lon + 1 - 2 * ((lon + 1) % 2), lat, lev))
+        near, table, scales = lax.optimization_barrier((near, table, scales))
         far = moved(near, lambda lon, lat, lev: (lon, lat, 1 - lev))
 
         def cycle(*refs):
@@ -360,13 +413,13 @@
         fields = 2 * bins
         field_store = pltpu.VMEM((fields, window, LANES), jnp.float32)
         step_store = pltpu.VMEM((fields, window + 2 * EDGE, LANES), jnp.float32)
-        return pl.pallas_call(
+        analysis, correction = pl.pallas_call(
             cycle,
             out_shape=(
                 jax.ShapeDtypeStruct(trajectory.shape, jnp.bfloat16),
-                jax.ShapeDtypeStruct((slots, bins, 1, rows, cols), jnp.float32),
+                jax.ShapeDtypeStruct((slots, bins, 1, cols, rows), jnp.float32),
             ),
-            in_specs=[in_vmem] * 4 + [pl.BlockSpec(memory_space=pltpu.SMEM), in_vmem, anywhere],
+            in_specs=[in_vmem] * 5 + [in_hbm],
             out_specs=(in_vmem, in_vmem),
             scratch_shapes=[
                 pltpu.VMEM(trajectory.shape, jnp.bfloat16),
@@ -378,7 +431,9 @@
                 pltpu.VMEM((6, window, LANES), jnp.float32),
                 pltpu.SemaphoreType.DMA,
             ],
-        )(own, near, far, table, settling, block_weights, trajectory)
+            compiler_params=small,
+        )(own, near, far, table, scales, trajectory)
+        return analysis, correction.swapaxes(3, 4)
 
     placed = (
         P("member", None, "lev", "lat", "lon"),

time: 27.6 us -> 17.4 us (0.63)
  local copies, waits for them, and re-layouts: 7.13 us -> 0.01 us
  Pallas kernels: 8.32 us -> 6.1 us
  waiting for transfers between devices: 4.57 us -> 3.88 us
    unnamed x24 -> x2, local copies, waits for them, and re-layouts: 5.53 us -> 0.01 us
    pallas_call x1 -> x0, local copies, waits for them, and re-layouts: 1.6 us -> none  [per_device(): pl.pallas_call(cycle, out_shape=(jax.ShapeDtypeStruct(trajectory.shape, j...]
    pallas_call x2, Pallas kernels: 4.33 us -> 2.81 us  [the longest x1 1.46 us: per_device(): pl.pallas_call(restrict, out_shape=pltpu.VMEM((rows, LANES), jnp.float32)...]
    pallas_call x1, Pallas kernels: 3.99 us -> 3.29 us  [per_device(): pl.pallas_call(cycle, out_shape=(jax.ShapeDtypeStruct(trajectory.shape, j...]
    ppermute x4, waiting for transfers between devices: 4.57 us -> 3.88 us  [moved(): return lax.ppermute(values, AXES, pairs)]
  transfers between devices with their start and end apart: 4 -> 4, of which waited for: 3 -> 4; matrix products, arithmetic and copies ran while one was open for 10% -> 0% of each run, Pallas kernels for 7% -> 8%
where the time goes in v2:
time: 17.4 us; the launch traced here: 17.2 us
  starting transfers between devices  6.53 us (38%)
  Pallas kernels  6.1 us (35%)
  waiting for transfers between devices  3.88 us (22%)
  between operations  0.66 us (4%)
    ppermute x4, starting transfers between devices, moved(): return lax.ppermute(values, AXES, pairs)  6.53 us
    ppermute x4, waiting for transfers between devices, moved(): return lax.ppermute(values, AXES, pairs)  3.88 us
    pallas_call x1, Pallas kernels, per_device(): pl.pallas_call(cycle, out_shape=(jax.ShapeDtypeStruct(trajectory.shape, j...  3.29 us
    pallas_call x1, Pallas kernels, per_device(): pl.pallas_call(restrict, out_shape=pltpu.VMEM((rows, LANES), jnp.float32)...  1.46 us
    pallas_call x1, Pallas kernels, per_device(): pl.pallas_call(tabulate, out_shape=(pltpu.VMEM((2, window, LANES), jnp.fl...  1.35 us
  transfers between devices with their start and end apart: 4, of which 4 were waited for; matrix products, arithmetic and copies ran while one was open for 0% of the time, Pallas kernels for 8%

profile of v2, /device:TPU:0, one launch (start us, length us, event | category | flops | bytes accessed | tf_op | source)
XLA Modules:
  0.0 17.2 jit_solution(1269296320133121049)
XLA Ops:
  0.6 0.0 copy-start
  0.6 1.5 %shard_map.95 = f32[32,128]{1,0:T(8,128)S(1)} custom-call(bf16[2,3,1,256,128]{4,3,2,1,0:T(8,128)(2,1)} %refs_5_.1, f32[8,8]{1,0:T(8,128)} %refs_4_.1, f32[1,16,32]{2,1,0:T(8,128)} %bitcast.16, s32[16,32]{1,0:T(8,128)} %bitcast.17), custom_call_target="tpu_custom_call" | custom-call | tf_op jit(solution)/shard_map/pallas_call | solution.py:352
  2.1 0.5 %collective-permute-start = (f32[32,128]{1,0:T(8,128)S(1)}, f32[32,128]{1,0:T(8,128)S(1)}, u32[]{:S(2)}, u32[]{:S(2)}) collective-permute-start(f32[32,128]{1,0:T(8,128)S(1)} %shard_map.95), channel_id=1, source_target_pairs={{1,0},{0,1},{3,2},{2,3},{5,4},{4,5},{7,6},{6,7},{9,8},{8,9},{11,10... | collective-permute-start | bytes 49160 | tf_op jit(solution)/shard_map/ppermute | solution.py:325
  2.6 0.8 %collective-permute-done = f32[32,128]{1,0:T(8,128)S(1)} collective-permute-done((f32[32,128]{1,0:T(8,128)S(1)}, f32[32,128]{1,0:T(8,128)S(1)}, u32[]{:S(2)}, u32[]{:S(2)}) %collective-permute-start) | collective-permute-done | bytes 16416 | tf_op jit(solution)/shard_map/ppermute | solution.py:325
  3.5 2.6 %collective-permute-start.1 = (f32[2,16,128]{2,1,0:T(8,128)S(1)}, f32[2,16,128]{2,1,0:T(8,128)S(1)}, u32[]{:S(2)}, u32[]{:S(2)}) collective-permute-start(f32[2,16,128]{2,1,0:T(8,128)S(1)} %pad_maximum_fusion.1), channel_id=1, source_target_pairs={{3,0},{2,1},{1,2},{0,3},{7,4},{6,5},{5,6},{4,7},{11,8},{10,9},{9,1... | collective-permute-start | bytes 49160 | tf_op jit(solution)/shard_map/ppermute | solution.py:325
  6.1 1.4 %collective-permute-done.1 = f32[2,16,128]{2,1,0:T(8,128)S(1)} collective-permute-done((f32[2,16,128]{2,1,0:T(8,128)S(1)}, f32[2,16,128]{2,1,0:T(8,128)S(1)}, u32[]{:S(2)}, u32[]{:S(2)}) %collective-permute-start.1) | collective-permute-done | bytes 16416 | tf_op jit(solution)/shard_map/ppermute | solution.py:325
  7.5 2.1 %collective-permute-start.2 = (f32[2,48,128]{2,1,0:T(8,128)S(1)}, f32[2,48,128]{2,1,0:T(8,128)S(1)}, u32[]{:S(2)}, u32[]{:S(2)}) collective-permute-start(f32[2,48,128]{2,1,0:T(8,128)S(1)} %pad_maximum_fusion.refs_0_), channel_id=1, source_target_pairs={{4,0},{13,1},{6,2},{15,3},{0,4},{9,5},{2,6},{11,7},{12,8},{5,9},{1... | collective-permute-start | bytes 147464 | tf_op jit(solution)/shard_map/ppermute | solution.py:325
  9.6 1.3 %shard_map.96 = (f32[2,48,128]{2,1,0:T(8,128)S(1)}, f32[7,8,128]{2,1,0:T(8,128)S(1)}) custom-call(s32[32,64]{1,0:T(8,128)} %bitcast.15, f32[2,32,64]{2,1,0:T(8,128)} %bitcast.13, f32[2,32,64]{2,1,0:T(8,128)} %bitcast.14, f32[2,3]{1,0:T(2,128)} %bitcast.18, f32[8,8]{1,0:T(8,128)} %refs_4_.1), custom_call_target="tpu_custom_call" | custom-call | tf_op jit(solution)/shard_map/pallas_call | solution.py:378
  11.0 0.7 %collective-permute-done.2.refs_1_ = f32[2,48,128]{2,1,0:T(8,128)S(1)} collective-permute-done((f32[2,48,128]{2,1,0:T(8,128)S(1)}, f32[2,48,128]{2,1,0:T(8,128)S(1)}, u32[]{:S(2)}, u32[]{:S(2)}) %collective-permute-start.2) | collective-permute-done | bytes 49184 | tf_op jit(solution)/shard_map/ppermute | solution.py:325
  11.7 1.3 %collective-permute-start.3 = (f32[2,48,128]{2,1,0:T(8,128)S(1)}, f32[2,48,128]{2,1,0:T(8,128)S(1)}, u32[]{:S(2)}, u32[]{:S(2)}) collective-permute-start(f32[2,48,128]{2,1,0:T(8,128)S(1)} %collective-permute-done.2.refs_1_), channel_id=1, source_target_pairs={{1,0},{0,1},{3,2},{2,3},{5,4},{4,5},{7,6},{6,7},{9,8},{8,9},{11,10... | collective-permute-start | bytes 147464 | tf_op jit(solution)/shard_map/ppermute | solution.py:325
  13.0 0.9 %collective-permute-done.3.refs_2_ = f32[2,48,128]{2,1,0:T(8,128)S(1)} collective-permute-done((f32[2,48,128]{2,1,0:T(8,128)S(1)}, f32[2,48,128]{2,1,0:T(8,128)S(1)}, u32[]{:S(2)}, u32[]{:S(2)}) %collective-permute-start.3) | collective-permute-done | bytes 49184 | tf_op jit(solution)/shard_map/ppermute | solution.py:325
  13.9 0.0 copy-done
  13.9 3.3 %shard_map.97 = (bf16[2,3,1,256,128]{4,3,2,1,0:T(8,128)(2,1)}, f32[2,3,1,16,32]{4,3,2,1,0:T(8,128)}) custom-call(f32[2,48,128]{2,1,0:T(8,128)S(1)} %pad_maximum_fusion.refs_0_, f32[2,48,128]{2,1,0:T(8,128)S(1)} %collective-permute-done.2.refs_1_, f32[2,48,128]{2,1,0:T(8,128)S(1)} %collective-permute-done.3.refs_2_, ...), custom_call_target="tpu_custom_call" | custom-call | tf_op jit(solution)/shard_map/pallas_call | solution.py:416
  (3 shorter events, 0.0 us)
Async XLA Ops:
  0.6 13.3 %copy-start = (bf16[2,3,1,256,128]{4,3,2,1,0:T(8,128)(2,1)S(1)}, bf16[2,3,1,256,128]{4,3,2,1,0:T(8,128)(2,1)}, u32[]{:S(2)}) copy-start(bf16[2,3,1,256,128]{4,3,2,1,0:T(8,128)(2,1)} %refs_5_.1) | copy-start | bytes 1179652
  2.1 1.4 %collective-permute-start = (f32[32,128]{1,0:T(8,128)S(1)}, f32[32,128]{1,0:T(8,128)S(1)}, u32[]{:S(2)}, u32[]{:S(2)}) collective-permute-start(f32[32,128]{1,0:T(8,128)S(1)} %shard_map.95), channel_id=1, source_target_pairs={{1,0},{0,1},{3,2},{2,3},{5,4},{4,5},{7,6},{6,7},{9,8},{8,9},{11,10... | collective-permute-start | bytes 49160 | tf_op jit(solution)/shard_map/ppermute | solution.py:325
  3.5 4.0 %collective-permute-start.1 = (f32[2,16,128]{2,1,0:T(8,128)S(1)}, f32[2,16,128]{2,1,0:T(8,128)S(1)}, u32[]{:S(2)}, u32[]{:S(2)}) collective-permute-start(f32[2,16,128]{2,1,0:T(8,128)S(1)} %pad_maximum_fusion.1), channel_id=1, source_target_pairs={{3,0},{2,1},{1,2},{0,3},{7,4},{6,5},{5,6},{4,7},{11,8},{10,9},{9,1... | collective-permute-start | bytes 49160 | tf_op jit(solution)/shard_map/ppermute | solution.py:325
  7.5 4.2 %collective-permute-start.2 = (f32[2,48,128]{2,1,0:T(8,128)S(1)}, f32[2,48,128]{2,1,0:T(8,128)S(1)}, u32[]{:S(2)}, u32[]{:S(2)}) collective-permute-start(f32[2,48,128]{2,1,0:T(8,128)S(1)} %pad_maximum_fusion.refs_0_), channel_id=1, source_target_pairs={{4,0},{13,1},{6,2},{15,3},{0,4},{9,5},{2,6},{11,7},{12,8},{5,9},{1... | collective-permute-start | bytes 147464 | tf_op jit(solution)/shard_map/ppermute | solution.py:325
  11.7 2.2 %collective-permute-start.3 = (f32[2,48,128]{2,1,0:T(8,128)S(1)}, f32[2,48,128]{2,1,0:T(8,128)S(1)}, u32[]{:S(2)}, u32[]{:S(2)}) collective-permute-start(f32[2,48,128]{2,1,0:T(8,128)S(1)} %collective-permute-done.2.refs_1_), channel_id=1, source_target_pairs={{1,0},{0,1},{3,2},{2,3},{5,4},{4,5},{7,6},{6,7},{9,8},{8,9},{11,10... | collective-permute-start | bytes 147464 | tf_op jit(solution)/shard_map/ppermute | solution.py:325

commit v3 on v2

--- a/solution.py
+++ b/solution.py
@@ -136,7 +136,8 @@
     window,
     own_cells,
     near_cells,
-    far_cells,
+    near_rims,
+    far,
     table,
     scales,
     trajectory,
@@ -168,14 +169,14 @@
             held[field, :EDGE] = edge
             held[field, EDGE + window :] = edge
 
-    def lay(place, block, rank):
+    def lay(place, block, rims):
         if lat_count == 2:
             outer = pl.multiple_of(lat * 2 * REACH, 8)
-            laid[place, REACH : 2 * REACH] = block[rank, :REACH]
-            laid[place, pl.ds(outer, REACH)] = block[rank, REACH:rows]
-            laid[place, pl.ds(pl.multiple_of(2 * REACH - outer, 8), REACH)] = block[rank, rows:]
+            laid[place, REACH : 2 * REACH] = block[:REACH]
+            laid[place, pl.ds(outer, REACH)] = block[REACH:]
+            laid[place, pl.ds(pl.multiple_of(2 * REACH - outer, 8), REACH)] = rims[...]
         else:
-            laid[place, pl.ds(pl.multiple_of(own, 8), rows)] = block[rank, :rows]
+            laid[place, pl.ds(pl.multiple_of(own, 8), rows)] = block[...]
 
             @pl.when(lat == 0)
             def _():
@@ -187,17 +188,25 @@
 
             @pl.when(lat > 0)
             def _():
-                laid[place, pl.ds(pl.multiple_of(own - REACH, 8), REACH)] = block[rank, rows : rows + REACH]
+                laid[place, pl.ds(pl.multiple_of(own - REACH, 8), REACH)] = rims[:REACH]
 
             @pl.when(lat < lat_count - 1)
             def _():
-                laid[place, pl.ds(pl.multiple_of(own + rows, 8), REACH)] = block[rank, rows + REACH :]
+                laid[place, pl.ds(pl.multiple_of(own + rows, 8), REACH)] = rims[REACH:]
+
+    height = window - rows
+
+    def far_cells(rank):
+        return far.at[pl.ds(rank * rows, rows)]
+
+    def far_rims(rank):
+        return far.at[pl.ds(levels * rows + rank * height, height)]
 
     for rank in range(levels):
         at = (rank + level) % levels
-        lay(at * 3 + 2 * (1 - near_is_west), near_cells, rank)
-        lay(at * 3 + 1, own_cells, rank)
-        lay(at * 3 + 2 * near_is_west, far_cells, levels - 1 - rank)
+        lay(at * 3 + 1, own_cells.at[rank], far_rims(0) if rank else near_rims.at[0])
+        lay(at * 3 + 2 * (1 - near_is_west), near_cells.at[rank], near_rims.at[1 + rank])
+        lay(at * 3 + 2 * near_is_west, far_cells(1 - rank), far_rims(2 - rank))
 
     lane = lane_iota(window)
     spot = lane % HALF // cols
@@ -388,24 +397,22 @@
             compiler_params=small,
         )(*map(kept, observed))
 
-        other = moved(packed, lambda lon, lat, lev: (lon, lat, 1 - lev))
-        levels = jnp.stack([packed, other])
+        own = jnp.stack([packed, moved(packed, lambda lon, lat, lev: (lon, lat, 1 - lev))])
+        near = moved(own, lambda lon, lat, lev: (lon ^ 1 if lev == 0 else lon + 1 - 2 * ((lon + 1) % 2), lat, lev))
+        near, table, scales = lax.optimization_barrier((near, table, scales))
+        held = jnp.concatenate([packed[None], near])
         if lat_count == 2:
-            rim = moved(levels[:, :REACH], lambda lon, lat, lev: (lon, 1 - lat, 1 - lev))
-            own = jnp.concatenate([levels, rim[::-1]], axis=1)
+            rims = moved(held[:, :REACH], lambda lon, lat, lev: (lon, 1 - lat, lev))
         else:
             low = moved(
-                levels[:, rows - REACH :],
-                lambda lon, lat, lev: (lon, lat - 1, 1 - lev) if lat > 0 else None,
+                held[:, rows - REACH :], lambda lon, lat, lev: (lon, lat - 1, lev) if lat > 0 else None
             )
             high = moved(
-                levels[:, :REACH],
-                lambda lon, lat, lev: (lon, lat + 1, 1 - lev) if lat < lat_count - 1 else None,
+                held[:, :REACH], lambda lon, lat, lev: (lon, lat + 1, lev) if lat < lat_count - 1 else None
             )
-            own = jnp.concatenate([levels, low[::-1], high[::-1]], axis=1)
-        near = moved(own, lambda lon, lat, lev: (lon ^ 1 if lev == 0 else lon + 1 - 2 * ((lon + 1) % 2), lat, lev))
-        near, table, scales = lax.optimization_barrier((near, table, scales))
-        far = moved(near, lambda lon, lat, lev: (lon, lat, 1 - lev))
+            rims = jnp.concatenate([low, high], axis=1)
+        brought = jnp.concatenate([near.reshape(-1, LANES), rims.reshape(-1, LANES)])
+        far = moved(brought, lambda lon, lat, lev: (lon, lat, 1 - lev))
 
         def cycle(*refs):
             cycle_kernel(lat_count, slots, bins, rows, cols, window, *refs)
@@ -419,7 +426,7 @@
                 jax.ShapeDtypeStruct(trajectory.shape, jnp.bfloat16),
                 jax.ShapeDtypeStruct((slots, bins, 1, cols, rows), jnp.float32),
             ),
-            in_specs=[in_vmem] * 5 + [in_hbm],
+            in_specs=[in_vmem] * 6 + [in_hbm],
             out_specs=(in_vmem, in_vmem),
             scratch_shapes=[
                 pltpu.VMEM(trajectory.shape, jnp.bfloat16),
@@ -432,7 +439,7 @@
                 pltpu.SemaphoreType.DMA,
             ],
             compiler_params=small,
-        )(own, near, far, table, scales, trajectory)
+        )(own, near, rims, far, table, scales, kept(trajectory))
         return analysis, correction.swapaxes(3, 4)
 
     placed = (

time: 17.4 us -> 16.6 us (0.954)
  starting transfers between devices: 6.53 us -> 5.68 us
  waiting for transfers between devices: 3.88 us -> 4.2 us
  Pallas kernels: 6.1 us -> 5.84 us
    ppermute x4, starting transfers between devices: 6.53 us -> 5.68 us  [moved(): return lax.ppermute(values, AXES, pairs)]
    ppermute x4, waiting for transfers between devices: 3.88 us -> 4.2 us  [moved(): return lax.ppermute(values, AXES, pairs)]
    pallas_call x1, Pallas kernels: 3.29 us -> 3.09 us  [per_device(): pl.pallas_call(cycle, out_shape=(jax.ShapeDtypeStruct(trajectory.shape, j...]
where the time goes in v3:
time: 16.6 us; the launch traced here: 16.4 us
  Pallas kernels  5.84 us (35%)
  starting transfers between devices  5.68 us (34%)
  waiting for transfers between devices  4.2 us (25%)
  between operations  0.65 us (4%)
    ppermute x4, starting transfers between devices, moved(): return lax.ppermute(values, AXES, pairs)  5.68 us
    ppermute x4, waiting for transfers between devices, moved(): return lax.ppermute(values, AXES, pairs)  4.2 us
    pallas_call x1, Pallas kernels, per_device(): pl.pallas_call(cycle, out_shape=(jax.ShapeDtypeStruct(trajectory.shape, j...  3.09 us
    pallas_call x1, Pallas kernels, per_device(): pl.pallas_call(restrict, out_shape=pltpu.VMEM((rows, LANES), jnp.float32)...  1.4 us
    pallas_call x1, Pallas kernels, per_device(): pl.pallas_call(tabulate, out_shape=(pltpu.VMEM((2, window, LANES), jnp.fl...  1.35 us
  transfers between devices with their start and end apart: 4, of which 4 were waited for; matrix products, arithmetic and copies ran while one was open for 0% of the time, Pallas kernels for 8%

profile of v3, /device:TPU:0, one launch (start us, length us, event | category | flops | bytes accessed | tf_op | source)
XLA Modules:
  0.0 16.4 jit_solution(4835567479650401766)
XLA Ops:
  0.6 1.4 %shard_map.95 = f32[32,128]{1,0:T(8,128)S(1)} custom-call(bf16[2,3,1,256,128]{4,3,2,1,0:T(8,128)(2,1)} %refs_6_.1, f32[8,8]{1,0:T(8,128)} %refs_4_.1, f32[1,16,32]{2,1,0:T(8,128)} %bitcast.19, s32[16,32]{1,0:T(8,128)} %bitcast.20), custom_call_target="tpu_custom_call" | custom-call | tf_op jit(solution)/shard_map/pallas_call | solution.py:361
  2.0 0.5 %collective-permute-start = (f32[32,128]{1,0:T(8,128)S(1)}, f32[32,128]{1,0:T(8,128)S(1)}, u32[]{:S(2)}, u32[]{:S(2)}) collective-permute-start(f32[32,128]{1,0:T(8,128)S(1)} %shard_map.95), channel_id=1, source_target_pairs={{1,0},{0,1},{3,2},{2,3},{5,4},{4,5},{7,6},{6,7},{9,8},{8,9},{11,10... | collective-permute-start | bytes 49160 | tf_op jit(solution)/shard_map/ppermute | solution.py:334
  2.6 0.8 %collective-permute-done = f32[32,128]{1,0:T(8,128)S(1)} collective-permute-done((f32[32,128]{1,0:T(8,128)S(1)}, f32[32,128]{1,0:T(8,128)S(1)}, u32[]{:S(2)}, u32[]{:S(2)}) %collective-permute-start) | collective-permute-done | bytes 16416 | tf_op jit(solution)/shard_map/ppermute | solution.py:334
  3.4 2.9 %collective-permute-start.1 = (f32[2,32,128]{2,1,0:T(8,128)S(1)}, f32[2,32,128]{2,1,0:T(8,128)S(1)}, u32[]{:S(2)}, u32[]{:S(2)}) collective-permute-start(f32[2,32,128]{2,1,0:T(8,128)S(1)} %pad_maximum_fusion.1.refs_0_), channel_id=1, source_target_pairs={{4,0},{13,1},{6,2},{15,3},{0,4},{9,5},{2,6},{11,7},{12,8},{5,9},{1... | collective-permute-start | bytes 98312 | tf_op jit(solution)/shard_map/ppermute | solution.py:334
  6.3 1.3 %shard_map.96 = (f32[2,48,128]{2,1,0:T(8,128)S(1)}, f32[7,8,128]{2,1,0:T(8,128)S(1)}) custom-call(s32[32,64]{1,0:T(8,128)} %bitcast.17, f32[2,32,64]{2,1,0:T(8,128)} %bitcast.15, f32[2,32,64]{2,1,0:T(8,128)} %bitcast.16, f32[2,3]{1,0:T(2,128)} %bitcast.21, f32[8,8]{1,0:T(8,128)} %refs_4_.1), custom_call_target="tpu_custom_call" | custom-call | tf_op jit(solution)/shard_map/pallas_call | solution.py:387
  7.7 0.5 %collective-permute-done.1.refs_1_ = f32[2,32,128]{2,1,0:T(8,128)S(1)} collective-permute-done((f32[2,32,128]{2,1,0:T(8,128)S(1)}, f32[2,32,128]{2,1,0:T(8,128)S(1)}, u32[]{:S(2)}, u32[]{:S(2)}) %collective-permute-start.1) | collective-permute-done | bytes 32800 | tf_op jit(solution)/shard_map/ppermute | solution.py:334
  8.2 1.9 %collective-permute-start.2 = (f32[3,16,128]{2,1,0:T(8,128)S(1)}, f32[3,16,128]{2,1,0:T(8,128)S(1)}, u32[]{:S(2)}, u32[]{:S(2)}) collective-permute-start(f32[3,16,128]{2,1,0:T(8,128)S(1)} %pad_maximum_fusion.2), channel_id=1, source_target_pairs={{2,0},{3,1},{0,2},{1,3},{6,4},{7,5},{4,6},{5,7},{10,8},{11,9},{8,1... | collective-permute-start | bytes 73736 | tf_op jit(solution)/shard_map/ppermute | solution.py:334
  10.1 1.9 %collective-permute-done.2.refs_2_ = f32[3,16,128]{2,1,0:T(8,128)S(1)} collective-permute-done((f32[3,16,128]{2,1,0:T(8,128)S(1)}, f32[3,16,128]{2,1,0:T(8,128)S(1)}, u32[]{:S(2)}, u32[]{:S(2)}) %collective-permute-start.2) | collective-permute-done | bytes 24608 | tf_op jit(solution)/shard_map/ppermute | solution.py:334
  12.0 0.3 %collective-permute-start.3 = (f32[112,128]{1,0:T(8,128)S(1)}, f32[112,128]{1,0:T(8,128)S(1)}, u32[]{:S(2)}, u32[]{:S(2)}) collective-permute-start(f32[112,128]{1,0:T(8,128)S(1)} %pad_maximum_fusion), channel_id=1, source_target_pairs={{1,0},{0,1},{3,2},{2,3},{5,4},{4,5},{7,6},{6,7},{9,8},{8,9},{11,10... | collective-permute-start | bytes 172040 | tf_op jit(solution)/shard_map/ppermute | solution.py:334
  12.4 0.9 %collective-permute-done.3.refs_3_ = f32[112,128]{1,0:T(8,128)S(1)} collective-permute-done((f32[112,128]{1,0:T(8,128)S(1)}, f32[112,128]{1,0:T(8,128)S(1)}, u32[]{:S(2)}, u32[]{:S(2)}) %collective-permute-start.3) | collective-permute-done | bytes 57376 | tf_op jit(solution)/shard_map/ppermute | solution.py:334
  13.3 3.1 %shard_map.97 = (bf16[2,3,1,256,128]{4,3,2,1,0:T(8,128)(2,1)}, f32[2,3,1,16,32]{4,3,2,1,0:T(8,128)}) custom-call(f32[2,32,128]{2,1,0:T(8,128)S(1)} %pad_maximum_fusion.1.refs_0_, f32[2,32,128]{2,1,0:T(8,128)S(1)} %collective-permute-done.1.refs_1_, f32[3,16,128]{2,1,0:T(8,128)S(1)} %collective-permute-done.2.refs_2_, ...), custom_call_target="tpu_custom_call" | custom-call | tf_op jit(solution)/shard_map/pallas_call | solution.py:423
  (3 shorter events, 0.0 us)
Async XLA Ops:
  2.0 1.4 %collective-permute-start = (f32[32,128]{1,0:T(8,128)S(1)}, f32[32,128]{1,0:T(8,128)S(1)}, u32[]{:S(2)}, u32[]{:S(2)}) collective-permute-start(f32[32,128]{1,0:T(8,128)S(1)} %shard_map.95), channel_id=1, source_target_pairs={{1,0},{0,1},{3,2},{2,3},{5,4},{4,5},{7,6},{6,7},{9,8},{8,9},{11,10... | collective-permute-start | bytes 49160 | tf_op jit(solution)/shard_map/ppermute | solution.py:334
  3.4 4.8 %collective-permute-start.1 = (f32[2,32,128]{2,1,0:T(8,128)S(1)}, f32[2,32,128]{2,1,0:T(8,128)S(1)}, u32[]{:S(2)}, u32[]{:S(2)}) collective-permute-start(f32[2,32,128]{2,1,0:T(8,128)S(1)} %pad_maximum_fusion.1.refs_0_), channel_id=1, source_target_pairs={{4,0},{13,1},{6,2},{15,3},{0,4},{9,5},{2,6},{11,7},{12,8},{5,9},{1... | collective-permute-start | bytes 98312 | tf_op jit(solution)/shard_map/ppermute | solution.py:334
  8.2 3.8 %collective-permute-start.2 = (f32[3,16,128]{2,1,0:T(8,128)S(1)}, f32[3,16,128]{2,1,0:T(8,128)S(1)}, u32[]{:S(2)}, u32[]{:S(2)}) collective-permute-start(f32[3,16,128]{2,1,0:T(8,128)S(1)} %pad_maximum_fusion.2), channel_id=1, source_target_pairs={{2,0},{3,1},{0,2},{1,3},{6,4},{7,5},{4,6},{5,7},{10,8},{11,9},{8,1... | collective-permute-start | bytes 73736 | tf_op jit(solution)/shard_map/ppermute | solution.py:334
  12.0 1.2 %collective-permute-start.3 = (f32[112,128]{1,0:T(8,128)S(1)}, f32[112,128]{1,0:T(8,128)S(1)}, u32[]{:S(2)}, u32[]{:S(2)}) collective-permute-start(f32[112,128]{1,0:T(8,128)S(1)} %pad_maximum_fusion), channel_id=1, source_target_pairs={{1,0},{0,1},{3,2},{2,3},{5,4},{4,5},{7,6},{6,7},{9,8},{8,9},{11,10... | collective-permute-start | bytes 172040 | tf_op jit(solution)/shard_map/ppermute | solution.py:334

commit v4 on v3

v4 whole, which is shorter than its diff:
```python
import jax
import jax.numpy as jnp
from jax import lax
from jax.experimental import pallas as pl
from jax.experimental.pallas import tpu as pltpu
from jax.sharding import PartitionSpec as P

BLOCK = 8
STEPS = 4
SWEEPS = 2
REACH = STEPS * 2 * SWEEPS
LANES = 128
HALF = LANES // 2
EDGE = 8

diffusion = 0.05
background = 0.1
step_length = 4.0
AXES = ("lon", "lat", "lev")


def lane_iota(rows):
    return lax.broadcasted_iota(jnp.int32, (rows, LANES), 1)


def three_parts(values):
    high = values.astype(jnp.bfloat16)
    rest = values - high.astype(jnp.float32)
    middle = rest.astype(jnp.bfloat16)
    low = (rest - middle.astype(jnp.float32)).astype(jnp.bfloat16)
    return jnp.concatenate([high, middle, low], axis=1)


def weight_rows(weights):
    return jnp.concatenate([weights] * (LANES // BLOCK), axis=1)


def fetches_of(sources, held, copied):
    return [
        pltpu.make_async_copy(source, target, copied.at[index])
        for index, (source, target) in enumerate(zip(sources, held))
    ]


def restrict_kernel(lat_count, slots, bins, rows, cols, *refs):
    sources, packed, held, fine, copied = refs[:4], refs[4], refs[5:9], refs[9], refs[10]
    trajectory, weights, wind, mask = held
    parts = [(slot, size) for slot in range(slots) for size in range(bins)]
    fetches = fetches_of(
        [*sources[1:], *(sources[0].at[at] for at in parts)],
        [*held[1:], *(trajectory.at[at] for at in parts)],
        copied,
    )
    for fetch in fetches:
        fetch.start()
    for fetch in fetches[:3]:
        fetch.wait()
    rows_of_weights = weight_rows(weights[...])
    row_sums = []
    for index, at in enumerate(parts):
        fetches[3 + index].wait()
        start = index * rows * BLOCK
        fine[start : start + rows * BLOCK] = trajectory[at].reshape(rows * BLOCK, LANES).astype(jnp.float32)
        total = fine[pl.ds(start, rows, stride=BLOCK), :] * rows_of_weights[:1]
        for row in range(1, BLOCK):
            total += fine[pl.ds(start + row, rows, stride=BLOCK), :] * rows_of_weights[row : row + 1]
        row_sums.append(total)
    row_sums = jnp.concatenate(row_sums)
    cell = lax.broadcasted_iota(jnp.int32, (LANES, LANES), 0) // BLOCK
    pool = (cell == lane_iota(LANES) % cols).astype(jnp.float32).astype(jnp.bfloat16)
    pooled = jnp.dot(three_parts(row_sums), jnp.concatenate([pool] * 3), preferred_element_type=jnp.float32)
    group = lane_iota(rows) // cols
    filler = jnp.zeros((bins * cols, rows), jnp.float32)
    out = jnp.concatenate([filler, wind[0], filler, mask[...].astype(jnp.float32)], axis=0).T
    for slot in range(slots):
        for size in range(bins):
            start = (slot * bins + size) * rows
            out = jnp.where(
                group == slot * (bins + 1) + size, pooled[start : start + rows], out
            )
    if lat_count == 2:
        start = pl.multiple_of(jnp.where(lax.axis_index("lat") == 0, rows - REACH, 0), 8)
        packed[pl.ds(start, REACH)] = out[:REACH]
        packed[pl.ds(pl.multiple_of(rows - REACH - start, 8), REACH)] = out[REACH:]
    else:
        packed[...] = out


def window_start(lat_count, rows, window):
    lat = lax.axis_index("lat")
    own = jnp.where(lat == 0, 0, jnp.where(lat == lat_count - 1, window - rows, REACH))
    return lat, own


def obs_kernel(lat_count, lon_total, rows, cols, window, *refs):
    sources, (table, scales), held, copied = refs[:5], refs[5:7], refs[7:12], refs[12]
    fetches = fetches_of(sources, held, copied)
    for fetch in fetches:
        fetch.start()
    for fetch in fetches:
        fetch.wait()
    columns, values, obs_weights, settling, weights = held
    lat, own = window_start(lat_count, rows, window)
    first = lat * rows - own
    slots, obs, lat_total = values.shape
    wide = -(-lat_total // LANES) * LANES
    low = lane_iota(obs) < HALF

    def windowed(array):
        if wide > lat_total:
            array = jnp.concatenate([array, jnp.zeros((obs, wide - lat_total), array.dtype)], axis=1)
        return pltpu.roll(array, lax.rem(wide - first, wide), 1)[:, :LANES]

    def paired(first_slot, second_slot):
        return jnp.where(low, windowed(first_slot), pltpu.roll(windowed(second_slot), HALF, 1))

    held = columns[...].astype(jnp.float32)
    place = paired(held, held)
    weight = paired(obs_weights[0], obs_weights[1])
    product = paired(obs_weights[0] * values[0], obs_weights[1] * values[1])
    sub = lax.broadcasted_iota(jnp.int32, (HALF, LANES), 0)
    start = lax.axis_index("lon") * cols - cols + lon_total
    here = lax.rem(sub + start, lon_total).astype(jnp.float32)
    sum_weight = jnp.zeros((HALF, LANES), jnp.float32)
    sum_product = jnp.zeros((HALF, LANES), jnp.float32)
    for index in range(obs):
        hit = here == place[index : index + 1]
        sum_weight += jnp.where(hit, weight[index : index + 1], 0.0)
        sum_product += jnp.where(hit, product[index : index + 1], 0.0)
    both = jnp.concatenate([sum_weight, sum_product], axis=0).T
    left, right = both[:window], both[HALF : HALF + window]
    low = lane_iota(window) < HALF
    table[0] = jnp.where(low, left, pltpu.roll(right, HALF, 1))
    table[1] = jnp.where(low, pltpu.roll(left, HALF, 1), right)
    levels, bins = settling.shape
    for k in range(levels):
        for size in range(bins):
            rate = settling[k : k + 1, size : size + 1]
            scales[k * bins + size] = jnp.broadcast_to(rate, (BLOCK, LANES))
    scales[levels * bins] = (BLOCK * BLOCK) * weight_rows(weights[...])


def rows_of(ref, field, window, spot):
    return ref[pl.ds(field * window + spot, EDGE, stride=window // EDGE), :]


def piece(field, window, spot):
    start = field * window + spot * EDGE
    return slice(start, start + EDGE)


def lay(lat_count, window, laid, place, block, rims):
    lat, own = window_start(lat_count, block.shape[0], window)
    rows = block.shape[0]

    def at(row, size):
        return pl.ds(pl.multiple_of(place * window + row, 8), size)

    if lat_count == 2:
        outer = lat * 2 * REACH
        laid[at(REACH, REACH)] = block[:REACH]
        laid[at(outer, REACH)] = block[REACH:]
        laid[at(2 * REACH - outer, REACH)] = rims[...]
    else:
        laid[at(own, rows)] = block[...]

        @pl.when(lat == 0)
        def _():
            laid[at(window - REACH, REACH)] = jnp.zeros((REACH, LANES), jnp.float32)

        @pl.when(lat == lat_count - 1)
        def _():
            laid[at(0, REACH)] = jnp.zeros((REACH, LANES), jnp.float32)

        @pl.when(lat > 0)
        def _():
            laid[at(own - REACH, REACH)] = rims[:REACH]

        @pl.when(lat < lat_count - 1)
        def _():
            laid[at(own + rows, REACH)] = rims[REACH:]


def near_is_west():
    return lax.rem(lax.axis_index("lon") + lax.axis_index("lev"), 2) == 1


def shares(block, place, bins, cols):
    lane = lane_iota(EDGE)
    low = lane < HALF
    zero = jnp.zeros((EDGE, LANES), jnp.float32)

    def turned(turn):
        return pltpu.roll(block, lax.rem(turn + 2 * LANES, LANES), 1)

    def inside(shift):
        from_start = lane - shift - place * cols
        return (from_start & (HALF - 1)) < cols

    out = [jnp.where(inside(0), turned((place - size) * cols), zero) for size in range(bins)]
    turn = (place - bins) * cols
    straight, crossed = turned(turn), turned(turn + HALF)
    out.append(jnp.where(inside(0), jnp.where(low, straight, crossed), zero))
    next_low = lax.rem(lane + LANES - 1, LANES) < HALF
    out.append(jnp.where(inside(1), jnp.where(next_low, turned(turn + 1), turned(turn + HALF + 1)), zero))
    out.append(jnp.where(inside(0), jnp.where(low, crossed, straight), zero))
    return out


def unpack_kernel(lat_count, bins, rows, cols, window, own_cells, near_cells, rims, begun, laid):
    levels = 2
    fields = levels * bins
    level = lax.axis_index("lev")
    for rank in range(levels):
        at = (rank + level) % levels
        lay(lat_count, window, laid, at * 2, own_cells.at[rank], rims.at[rank])
        lay(lat_count, window, laid, at * 2 + 1, near_cells.at[rank], rims.at[levels + rank])
    side = jnp.where(near_is_west(), 0, 2)
    for k in range(levels):
        for spot in range(window // EDGE):
            center = shares(rows_of(laid, 2 * k, window, spot), 1, bins, cols)
            beside = shares(rows_of(laid, 2 * k + 1, window, spot), side, bins, cols)
            both = [a + b for a, b in zip(center, beside)]
            for size in range(bins):
                begun[piece(k * bins + size, window, spot)] = both[size]
            wind, wind_next, mask = both[bins:]
            begun[piece(fields + 3 * k, window, spot)] = 1.0 - 4.0 * diffusion - wind
            begun[piece(fields + 3 * k + 1, window, spot)] = wind_next + diffusion
            begun[piece(fields + 3 * k + 2, window, spot)] = wind + diffusion
            if k == 0:
                begun[piece(fields + 3 * levels, window, spot)] = mask


def cycle_kernel(
    lat_count,
    slots,
    bins,
    rows,
    cols,
    window,
    begun,
    far,
    table,
    scales,
    trajectory,
    analysis_out,
    correction_out,
    fine,
    analysis,
    correction,
    coarse,
    change,
    winds,
    laid,
    copied,
    written,
):
    fetch = pltpu.make_async_copy(trajectory, fine, copied)
    fetch.start()
    levels = 2
    fields = levels * bins
    lat, own = window_start(lat_count, rows, window)
    level = lax.axis_index("lev")
    count = window // EDGE
    spots = range(count)
    for rank in range(levels):
        at = (rank + level) % levels
        lay(lat_count, window, laid, at, far.at[1 - rank, pl.ds(0, rows)], far.at[1 - rank, pl.ds(rows, window - rows)])
    side = jnp.where(near_is_west(), 2, 0)
    for k in range(levels):
        for spot in spots:
            share = shares(rows_of(laid, k, window, spot), side, bins, cols)
            for size in range(bins):
                at = piece(k * bins + size, window, spot)
                coarse[at] = begun[at] + share[size]
            wind, wind_next, mask_share = share[bins:]
            for index, value in enumerate((-wind, wind_next, wind)):
                winds[piece(3 * k + index, window, spot)] = begun[piece(fields + 3 * k + index, window, spot)] + value
            if k == 0:
                at = piece(3 * levels, window, spot)
                winds[at] = begun[piece(fields + 3 * levels, window, spot)] + mask_share

    sub = lax.broadcasted_iota(jnp.int32, (EDGE, LANES), 0)

    def carried(cells, k, backward):
        out = []
        for spot in spots:
            if spot:
                south = cells[spot - 1]
            else:
                south = jnp.where(sub == 0, 0.0, pltpu.roll(cells[-1], 1, 0))
            if spot < count - 1:
                north = cells[spot + 1]
            else:
                north = jnp.where(sub == EDGE - 1, 0.0, pltpu.roll(cells[0], EDGE - 1, 0))
            west, east = pltpu.roll(cells[spot], 1, 1), pltpu.roll(cells[spot], LANES - 1, 1)
            swept, other = (east, west) if backward else (west, east)
            near = diffusion * ((north + south) + other)
            out.append(
                (near + winds[piece(3 * k, window, spot)] * cells[spot])
                + winds[piece(3 * k + 1 + backward, window, spot)] * swept
            )
        return out

    def each(function, *lists):
        return [function(*values) for values in zip(*lists)]

    def added(first, second):
        return each(lambda a, b: a + b, first, second)

    def total_of(lists):
        out = lists[0]
        for values in lists[1:]:
            out = added(out, values)
        return out

    def scaled(factor, values):
        return [factor * value for value in values]

    def more(base, factor, values):
        return each(lambda a, b: a + factor * b, base, values)

    sizes = range(bins)
    upper = [scales[size, :1] for size in sizes]
    lower = [scales[bins + size, :1] for size in sizes]

    def summed_forward(top, bottom):
        sunk = [[] for _ in range(3)]
        cells = top
        for index in range(3):
            sunk[index] = [scaled(upper[size], cells[size]) for size in sizes]
            if index < 2:
                cells = [each(lambda a, b: a - b, carried(cells[size], 0, False), sunk[index][size]) for size in sizes]
        both = total_of(cells)
        both = each(lambda a, b: a - b, carried(both, 0, False), total_of(sunk[2]))
        both = carried(both, 0, False)
        factors = []
        for size in sizes:
            rate = -lower[size]
            first = scaled(rate, bottom[size])
            b3 = added(sunk[0][size], first)
            b2 = more(sunk[1][size], rate, b3)
            b1 = more(sunk[2][size], rate, b2)
            c0 = scaled(rate, b1)
            e3 = added(b3, first)
            e2 = more(b2, rate, e3)
            c1 = more(b1, rate, e2)
            f3 = added(e3, first)
            c2 = more(e2, rate, f3)
            c3 = added(f3, first)
            factors.append([c3, c2, c1, c0])
        moved = total_of(bottom)
        for index in range(4):
            moved = added(carried(moved, 1, False), total_of([factor[index] for factor in factors]))
        return added(both, moved)

    def spread_backward(start):
        powers = [start]
        for _ in range(4):
            powers.append(carried(powers[-1], 1, True))
        twice, thrice, thrice_more = scaled(2.0, powers[1]), scaled(3.0, powers[1]), scaled(3.0, powers[2])
        four, six, four_more = scaled(4.0, powers[1]), scaled(6.0, powers[2]), scaled(4.0, powers[3])
        first = carried(start, 0, True)
        second = carried(first, 0, True)
        gap = each(lambda a, b: a - b, powers[1], first)
        tops, bottoms = [], []
        for size in sizes:
            rate = -lower[size]
            low_two = more(powers[2], rate, more(twice, rate, start))
            low_three = more(powers[3], rate, more(thrice_more, rate, more(thrice, rate, start)))
            low_four = more(powers[4], rate, more(four_more, rate, more(six, rate, more(four, rate, start))))
            cells = more(second, upper[size], more(gap, rate, start))
            for below in (low_two, low_three):
                cells = more(carried(cells, 0, True), upper[size], each(lambda a, b: a - b, below, cells))
            tops.append(cells)
            bottoms.append(low_four)
        return tops + bottoms

    scale = 1.0 / fields
    mask = [winds[piece(3 * levels, window, spot)] for spot in spots]
    for field in range(fields):
        for spot in spots:
            change[piece(field, window, spot)] = jnp.zeros((EDGE, LANES), jnp.float32)

    def one_sweep(sweep, carry):
        cells = [[coarse[piece(field, window, spot)] for spot in spots] for field in range(fields)]
        if True:
            cells = [added(cells[field], [change[piece(field, window, spot)] for spot in spots]) for field in range(fields)]
        total = summed_forward(cells[:bins], cells[bins:])
        start = [
            rows_of(table, 0, window, spot) * (total[spot] * (scale * scale)) - rows_of(table, 1, window, spot) * scale
            for spot in spots
        ]
        adjoint = spread_backward(start)
        for field in range(fields):
            for spot in spots:
                if True:
                    old = change[piece(field, window, spot)]
                    value = old - step_length * (background * old + adjoint[field][spot])
                else:
                    value = -step_length * adjoint[field][spot]
                change[piece(field, window, spot)] = mask[spot] * value
        return carry

    lax.fori_loop(0, SWEEPS, one_sweep, 0)

    for field in range(fields):
        for spot in spots:
            coarse[pl.ds(field * window + spot, EDGE, stride=count), :] = change[piece(field, window, spot)]
    final = [
        coarse[pl.ds(pl.multiple_of((level * bins + size) * window + own, 8), rows)] for size in range(bins)
    ]
    for size in range(bins):
        turned = final[size].T
        for slot in range(slots):
            start = slot * HALF + cols
            correction[slot, size, 0] = turned[start : start + cols]
    writes = [pltpu.make_async_copy(correction, correction_out, written.at[slots * bins])]
    writes[0].start()
    source_lane = lax.broadcasted_iota(jnp.int32, (LANES, slots * LANES), 0)
    target_lane = lax.broadcasted_iota(jnp.int32, (LANES, slots * LANES), 1)
    picks = source_lane == target_lane // LANES * HALF + cols + target_lane % LANES // BLOCK
    picks = picks.astype(jnp.float32).astype(jnp.bfloat16)
    wide = jnp.dot(
        three_parts(jnp.concatenate(final)), jnp.concatenate([picks] * 3), preferred_element_type=jnp.float32
    )
    growth = scales[levels * bins]
    fetch.wait()
    for slot in range(slots):
        for size in range(bins):
            cells = wide[size * rows : (size + 1) * rows, slot * LANES : (slot + 1) * LANES]
            raised = (cells[:, None, :] * growth[None]).reshape(rows * BLOCK, LANES)
            analysis[slot, size, 0] = (fine[slot, size, 0].astype(jnp.float32) + raised).astype(jnp.bfloat16)
            at = (slot, size)
            writes.append(pltpu.make_async_copy(analysis.at[at], analysis_out.at[at], written.at[slot * bins + size]))
            writes[-1].start()
    for write in writes:
        write.wait()


def solution(mesh):
    lon_count, lat_count, lev_count = (mesh.shape[axis] for axis in AXES)

    def place_of(lon, lat, lev):
        return (lon % lon_count * lat_count + lat) * lev_count + lev

    def moved(values, source_of):
        pairs = []
        for lon in range(lon_count):
            for lat in range(lat_count):
                for lev in range(lev_count):
                    source = source_of(lon, lat, lev)
                    if source is not None:
                        pairs.append((place_of(*source), place_of(lon, lat, lev)))
        return lax.ppermute(values, AXES, pairs)

    def per_device(
        trajectory,
        block_weights,
        wind_speed,
        settling,
        source_mask,
        obs_columns,
        obs_values,
        obs_weights,
    ):
        slots, bins, _, fine_rows, fine_cols = trajectory.shape
        rows, cols = fine_rows // BLOCK, fine_cols // BLOCK
        rims = min(lat_count - 1, 2)
        window = rows + rims * REACH
        small = pltpu.CompilerParams(vmem_limit_bytes=8 * 1024 * 1024)
        in_vmem = pl.BlockSpec(memory_space=pltpu.VMEM)

        def kept(array):
            return pltpu.with_memory_space_constraint(array, pltpu.HBM)

        in_hbm = pl.BlockSpec(memory_space=pltpu.HBM)

        def restrict(*refs):
            restrict_kernel(lat_count, slots, bins, rows, cols, *refs)

        packed = pl.pallas_call(
            restrict,
            out_shape=pltpu.VMEM((rows, LANES), jnp.float32),
            in_specs=[in_hbm] * 4,
            out_specs=in_vmem,
            scratch_shapes=[
                pltpu.VMEM(trajectory.shape, jnp.bfloat16),
                pltpu.VMEM((BLOCK, BLOCK), jnp.float32),
                pltpu.VMEM((1, cols, rows), jnp.float32),
                pltpu.VMEM((cols, rows), jnp.int32),
                pltpu.VMEM((slots * bins * fine_rows, LANES), jnp.float32),
                pltpu.SemaphoreType.DMA((3 + slots * bins,)),
            ],
            compiler_params=small,
        )(*map(kept, (trajectory, block_weights, wind_speed.swapaxes(1, 2), source_mask.T)))

        def tabulate(*refs):
            obs_kernel(lat_count, lon_count * cols, rows, cols, window, *refs)

        observed = (
            obs_columns.T,
            obs_values.swapaxes(1, 2),
            obs_weights.swapaxes(1, 2),
            settling.T,
            block_weights,
        )
        table, scales = pl.pallas_call(
            tabulate,
            out_shape=(
                pltpu.VMEM((2, window, LANES), jnp.float32),
                pltpu.VMEM((2 * bins + 1, BLOCK, LANES), jnp.float32),
            ),
            in_specs=[in_hbm] * 5,
            out_specs=(in_vmem, in_vmem),
            scratch_shapes=[pltpu.VMEM(array.shape, array.dtype) for array in observed]
            + [pltpu.SemaphoreType.DMA((5,))],
            compiler_params=small,
        )(*map(kept, observed))

        own = jnp.stack([packed, moved(packed, lambda lon, lat, lev: (lon, lat, 1 - lev))])
        near = moved(own, lambda lon, lat, lev: (lon ^ 1 if lev == 0 else lon + 1 - 2 * ((lon + 1) % 2), lat, lev))
        near, table, scales = lax.optimization_barrier((near, table, scales))
        held = jnp.concatenate([own, near])
        if lat_count == 2:
            rims = moved(held[:, :REACH], lambda lon, lat, lev: (lon, 1 - lat, lev))
        else:
            low = moved(
                held[:, rows - REACH :], lambda lon, lat, lev: (lon, lat - 1, lev) if lat > 0 else None
            )
            high = moved(
                held[:, :REACH], lambda lon, lat, lev: (lon, lat + 1, lev) if lat < lat_count - 1 else None
            )
            rims = jnp.concatenate([low, high], axis=1)
        brought = jnp.concatenate([near, rims[2:]], axis=1)
        far = moved(brought, lambda lon, lat, lev: (lon, lat, 1 - lev))

        def cycle(*refs):
            cycle_kernel(lat_count, slots, bins, rows, cols, window, *refs)

        fields = 2 * bins
        fields = 2 * bins
        field_shape = ((fields + 7) * window, LANES)

        def unpack(*refs):
            unpack_kernel(lat_count, bins, rows, cols, window, *refs)

        begun = pl.pallas_call(
            unpack,
            out_shape=pltpu.VMEM(field_shape, jnp.float32),
            in_specs=[in_vmem] * 3,
            out_specs=in_vmem,
            scratch_shapes=[pltpu.VMEM((4 * window, LANES), jnp.float32)],
            compiler_params=small,
        )(own, near, rims)
        begun, far = lax.optimization_barrier((begun, far))
        field_store = pltpu.VMEM((fields * window, LANES), jnp.float32)
        analysis, correction = pl.pallas_call(
            cycle,
            out_shape=(
                jax.ShapeDtypeStruct(trajectory.shape, jnp.bfloat16),
                jax.ShapeDtypeStruct((slots, bins, 1, cols, rows), jnp.float32),
            ),
            in_specs=[in_vmem] * 4 + [in_hbm],
            out_specs=(in_hbm, in_hbm),
            scratch_shapes=[
                pltpu.VMEM(trajectory.shape, jnp.bfloat16),
                pltpu.VMEM(trajectory.shape, jnp.bfloat16),
                pltpu.VMEM((slots, bins, 1, cols, rows), jnp.float32),
                field_store,
                field_store,
                pltpu.VMEM((7 * window, LANES), jnp.float32),
                pltpu.VMEM((2 * window, LANES), jnp.float32),
                pltpu.SemaphoreType.DMA,
                pltpu.SemaphoreType.DMA((slots * bins + 1,)),
            ],
            compiler_params=small,
        )(begun, far, table.reshape(-1, LANES), scales, kept(trajectory))
        return analysis, correction.swapaxes(3, 4)

    placed = (
        P("member", None, "lev", "lat", "lon"),
        P(),
        P("lev", "lat", "lon"),
        P(),
        P("lat", "lon"),
        P("member", None),
        P("member", None, None),
        P("member", None, None),
    )
    return jax.shard_map(
        per_device,
        mesh=mesh,
        in_specs=placed,
        out_specs=(P("member", None, "lev", "lat", "lon"), P("member", None, "lev", "lat", "lon")),
        check_vma=False,
    )
```

time: 16.6 us -> 16.4 us (0.988)
  waiting for transfers between devices: 4.2 us -> 4.03 us
    pallas_call x1, Pallas kernels: 3.09 us -> 2.76 us  [per_device(): pl.pallas_call(cycle, out_shape=(jax.ShapeDtypeStruct(trajectory.shape, j...]
    pallas_call x0 -> x1, Pallas kernels: none -> 0.24 us  [per_device(): pl.pallas_call(unpack, out_shape=pltpu.VMEM(field_shape, jnp.float32), in...]
    ppermute x4, waiting for transfers between devices: 4.2 us -> 4.03 us  [moved(): return lax.ppermute(values, AXES, pairs)]
  transfers between devices with their start and end apart: 4 -> 4, of which waited for: 4 -> 4; matrix products, arithmetic and copies ran while one was open for 0% -> 0% of each run, Pallas kernels for 8% -> 10%
where the time goes in v4:
time: 16.4 us; the launch traced here: 16.1 us
  starting transfers between devices  5.74 us (35%)
  Pallas kernels  5.68 us (35%)
  waiting for transfers between devices  4.03 us (25%)
  between operations  0.66 us (4%)
    ppermute x4, starting transfers between devices, moved(): return lax.ppermute(values, AXES, pairs)  5.74 us
    ppermute x4, waiting for transfers between devices, moved(): return lax.ppermute(values, AXES, pairs)  4.03 us
    pallas_call x1, Pallas kernels, per_device(): pl.pallas_call(cycle, out_shape=(jax.ShapeDtypeStruct(trajectory.shape, j...  2.76 us
    pallas_call x1, Pallas kernels, per_device(): pl.pallas_call(tabulate, out_shape=(pltpu.VMEM((2, window, LANES), jnp.fl...  1.35 us
    pallas_call x1, Pallas kernels, per_device(): pl.pallas_call(restrict, out_shape=pltpu.VMEM((rows, LANES), jnp.float32)...  1.34 us
  transfers between devices with their start and end apart: 4, of which 4 were waited for; matrix products, arithmetic and copies ran while one was open for 0% of the time, Pallas kernels for 10%

profile of v4, /device:TPU:0, one launch (start us, length us, event | category | flops | bytes accessed | tf_op | source)
XLA Modules:
  0.0 16.1 jit_solution(12545688144749625438)
XLA Ops:
  0.6 1.3 %shard_map.95 = f32[32,128]{1,0:T(8,128)S(1)} custom-call(bf16[2,3,1,256,128]{4,3,2,1,0:T(8,128)(2,1)} %refs_4_.3, f32[8,8]{1,0:T(8,128)} %refs_4_.2, f32[1,16,32]{2,1,0:T(8,128)} %bitcast.18, s32[16,32]{1,0:T(8,128)} %bitcast.19), custom_call_target="tpu_custom_call" | custom-call | tf_op jit(solution)/shard_map/pallas_call | solution.py:482
  2.0 0.5 %collective-permute-start = (f32[32,128]{1,0:T(8,128)S(1)}, f32[32,128]{1,0:T(8,128)S(1)}, u32[]{:S(2)}, u32[]{:S(2)}) collective-permute-start(f32[32,128]{1,0:T(8,128)S(1)} %shard_map.95), channel_id=1, source_target_pairs={{1,0},{0,1},{3,2},{2,3},{5,4},{4,5},{7,6},{6,7},{9,8},{8,9},{11,10... | collective-permute-start | bytes 49160 | tf_op jit(solution)/shard_map/ppermute | solution.py:455
  2.5 0.8 %collective-permute-done = f32[32,128]{1,0:T(8,128)S(1)} collective-permute-done((f32[32,128]{1,0:T(8,128)S(1)}, f32[32,128]{1,0:T(8,128)S(1)}, u32[]{:S(2)}, u32[]{:S(2)}) %collective-permute-start) | collective-permute-done | bytes 16416 | tf_op jit(solution)/shard_map/ppermute | solution.py:455
  3.3 2.9 %collective-permute-start.1 = (f32[2,32,128]{2,1,0:T(8,128)S(1)}, f32[2,32,128]{2,1,0:T(8,128)S(1)}, u32[]{:S(2)}, u32[]{:S(2)}) collective-permute-start(f32[2,32,128]{2,1,0:T(8,128)S(1)} %pad_maximum_fusion.3.refs_0_), channel_id=1, source_target_pairs={{4,0},{13,1},{6,2},{15,3},{0,4},{9,5},{2,6},{11,7},{12,8},{5,9},{1... | collective-permute-start | bytes 98312 | tf_op jit(solution)/shard_map/ppermute | solution.py:455
  6.3 1.3 %shard_map.96 = (f32[2,48,128]{2,1,0:T(8,128)S(1)}, f32[7,8,128]{2,1,0:T(8,128)S(1)}) custom-call(s32[32,64]{1,0:T(8,128)} %bitcast.17, f32[2,32,64]{2,1,0:T(8,128)} %bitcast.15, f32[2,32,64]{2,1,0:T(8,128)} %bitcast.16, f32[2,3]{1,0:T(2,128)} %bitcast.20, f32[8,8]{1,0:T(8,128)} %refs_4_.2), custom_call_target="tpu_custom_call" | custom-call | tf_op jit(solution)/shard_map/pallas_call | solution.py:508
  7.6 0.5 %collective-permute-done.1.refs_1_ = f32[2,32,128]{2,1,0:T(8,128)S(1)} collective-permute-done((f32[2,32,128]{2,1,0:T(8,128)S(1)}, f32[2,32,128]{2,1,0:T(8,128)S(1)}, u32[]{:S(2)}, u32[]{:S(2)}) %collective-permute-start.1) | collective-permute-done | bytes 32800 | tf_op jit(solution)/shard_map/ppermute | solution.py:455
  8.1 1.9 %collective-permute-start.2 = (f32[4,16,128]{2,1,0:T(8,128)S(1)}, f32[4,16,128]{2,1,0:T(8,128)S(1)}, u32[]{:S(2)}, u32[]{:S(2)}) collective-permute-start(f32[4,16,128]{2,1,0:T(8,128)S(1)} %pad_maximum_fusion.1), channel_id=1, source_target_pairs={{2,0},{3,1},{0,2},{1,3},{6,4},{7,5},{4,6},{5,7},{10,8},{11,9},{8,1... | collective-permute-start | bytes 98312 | tf_op jit(solution)/shard_map/ppermute | solution.py:455
  10.1 2.0 %collective-permute-done.2.refs_2_ = f32[4,16,128]{2,1,0:T(8,128)S(1)} collective-permute-done((f32[4,16,128]{2,1,0:T(8,128)S(1)}, f32[4,16,128]{2,1,0:T(8,128)S(1)}, u32[]{:S(2)}, u32[]{:S(2)}) %collective-permute-start.2) | collective-permute-done | bytes 32800 | tf_op jit(solution)/shard_map/ppermute | solution.py:455
  12.1 0.4 %collective-permute-start.3 = (f32[2,48,128]{2,1,0:T(8,128)S(1)}, f32[2,48,128]{2,1,0:T(8,128)S(1)}, u32[]{:S(2)}, u32[]{:S(2)}) collective-permute-start(f32[2,48,128]{2,1,0:T(8,128)S(1)} %pad_maximum_fusion), channel_id=1, source_target_pairs={{1,0},{0,1},{3,2},{2,3},{5,4},{4,5},{7,6},{6,7},{9,8},{8,9},{11,10... | collective-permute-start | bytes 147464 | tf_op jit(solution)/shard_map/ppermute | solution.py:455
  12.4 0.2 %shard_map.97.refs_0_ = f32[624,128]{1,0:T(8,128)S(1)} custom-call(f32[2,32,128]{2,1,0:T(8,128)S(1)} %pad_maximum_fusion.3.refs_0_, f32[2,32,128]{2,1,0:T(8,128)S(1)} %collective-permute-done.1.refs_1_, f32[4,16,128]{2,1,0:T(8,128)S(1)} %collective-permute-done.2.refs_2_), custom_call_target="tpu_custom_call" | custom-call | tf_op jit(solution)/shard_map/pallas_call | solution.py:548
  12.7 0.7 %collective-permute-done.3.refs_1_ = f32[2,48,128]{2,1,0:T(8,128)S(1)} collective-permute-done((f32[2,48,128]{2,1,0:T(8,128)S(1)}, f32[2,48,128]{2,1,0:T(8,128)S(1)}, u32[]{:S(2)}, u32[]{:S(2)}) %collective-permute-start.3) | collective-permute-done | bytes 49184 | tf_op jit(solution)/shard_map/ppermute | solution.py:455
  13.4 2.8 %shard_map.98 = (bf16[2,3,1,256,128]{4,3,2,1,0:T(8,128)(2,1)}, f32[2,3,1,16,32]{4,3,2,1,0:T(8,128)}) custom-call(f32[624,128]{1,0:T(8,128)S(1)} %shard_map.97.refs_0_, f32[2,48,128]{2,1,0:T(8,128)S(1)} %collective-permute-done.3.refs_1_, f32[96,128]{1,0:T(8,128)S(1)} %bitcast.12, f32[7,8,128]{2,1,0:T(8,128)S(1)} %get-tuple-element.17.refs_3_, ...), custom_call_target="tpu_custom_call" | custom-call | tf_op jit(solution)/shard_map/pallas_call | solution.py:558
  (4 shorter events, 0.0 us)
Async XLA Ops:
  2.0 1.4 %collective-permute-start = (f32[32,128]{1,0:T(8,128)S(1)}, f32[32,128]{1,0:T(8,128)S(1)}, u32[]{:S(2)}, u32[]{:S(2)}) collective-permute-start(f32[32,128]{1,0:T(8,128)S(1)} %shard_map.95), channel_id=1, source_target_pairs={{1,0},{0,1},{3,2},{2,3},{5,4},{4,5},{7,6},{6,7},{9,8},{8,9},{11,10... | collective-permute-start | bytes 49160 | tf_op jit(solution)/shard_map/ppermute | solution.py:455
  3.3 4.8 %collective-permute-start.1 = (f32[2,32,128]{2,1,0:T(8,128)S(1)}, f32[2,32,128]{2,1,0:T(8,128)S(1)}, u32[]{:S(2)}, u32[]{:S(2)}) collective-permute-start(f32[2,32,128]{2,1,0:T(8,128)S(1)} %pad_maximum_fusion.3.refs_0_), channel_id=1, source_target_pairs={{4,0},{13,1},{6,2},{15,3},{0,4},{9,5},{2,6},{11,7},{12,8},{5,9},{1... | collective-permute-start | bytes 98312 | tf_op jit(solution)/shard_map/ppermute | solution.py:455
  8.1 3.9 %collective-permute-start.2 = (f32[4,16,128]{2,1,0:T(8,128)S(1)}, f32[4,16,128]{2,1,0:T(8,128)S(1)}, u32[]{:S(2)}, u32[]{:S(2)}) collective-permute-start(f32[4,16,128]{2,1,0:T(8,128)S(1)} %pad_maximum_fusion.1), channel_id=1, source_target_pairs={{2,0},{3,1},{0,2},{1,3},{6,4},{7,5},{4,6},{5,7},{10,8},{11,9},{8,1... | collective-permute-start | bytes 98312 | tf_op jit(solution)/shard_map/ppermute | solution.py:455
  12.1 1.3 %collective-permute-start.3 = (f32[2,48,128]{2,1,0:T(8,128)S(1)}, f32[2,48,128]{2,1,0:T(8,128)S(1)}, u32[]{:S(2)}, u32[]{:S(2)}) collective-permute-start(f32[2,48,128]{2,1,0:T(8,128)S(1)} %pad_maximum_fusion), channel_id=1, source_target_pairs={{1,0},{0,1},{3,2},{2,3},{5,4},{4,5},{7,6},{6,7},{9,8},{8,9},{11,10... | collective-permute-start | bytes 147464 | tf_op jit(solution)/shard_map/ppermute | solution.py:455

commit v5 on v4

--- a/solution.py
+++ b/solution.py
@@ -274,15 +274,30 @@
                 at = piece(k * bins + size, window, spot)
                 coarse[at] = begun[at] + share[size]
             wind, wind_next, mask_share = share[bins:]
-            for index, value in enumerate((-wind, wind_next, wind)):
-                winds[piece(3 * k + index, window, spot)] = begun[piece(fields + 3 * k + index, window, spot)] + value
+            stay, next_sweep, sweep = (
+                begun[piece(fields + 3 * k + index, window, spot)] + value
+                for index, value in enumerate((-wind, wind_next, wind))
+            )
+            last_sweep, over_sweep = pltpu.roll(sweep, LANES - 1, 1), pltpu.roll(next_sweep, 1, 1)
+            kept = 1.0 - 3.0 * diffusion
+            for index, value in enumerate(
+                (kept - last_sweep, stay, kept - next_sweep, last_sweep, sweep, next_sweep, over_sweep)
+            ):
+                winds[piece(7 * k + index, window, spot)] = value
             if k == 0:
-                at = piece(3 * levels, window, spot)
-                winds[at] = begun[piece(fields + 3 * levels, window, spot)] + mask_share
+                winds[piece(7 * levels, window, spot)] = begun[piece(fields + 3 * levels, window, spot)] + mask_share
 
     sub = lax.broadcasted_iota(jnp.int32, (EDGE, LANES), 0)
 
-    def carried(cells, k, backward):
+    def copies(cells, reach):
+        out = {0: cells}
+        for turn in range(1, reach + 1):
+            out[turn] = [pltpu.roll(value, turn, 1) for value in cells]
+            out[-turn] = [pltpu.roll(value, LANES - turn, 1) for value in cells]
+        return out
+
+    def carried_at(turned, k, backward, turn):
+        cells, west, east = turned[turn], turned[turn + 1], turned[turn - 1]
         out = []
         for spot in spots:
             if spot:
@@ -293,14 +308,17 @@
                 north = cells[spot + 1]
             else:
                 north = jnp.where(sub == EDGE - 1, 0.0, pltpu.roll(cells[0], EDGE - 1, 0))
-            west, east = pltpu.roll(cells[spot], 1, 1), pltpu.roll(cells[spot], LANES - 1, 1)
-            swept, other = (east, west) if backward else (west, east)
+            swept, other = (east[spot], west[spot]) if backward else (west[spot], east[spot])
             near = diffusion * ((north + south) + other)
+            sweep = 7 * k + 4 + turn + (not backward)
             out.append(
-                (near + winds[piece(3 * k, window, spot)] * cells[spot])
-                + winds[piece(3 * k + 1 + backward, window, spot)] * swept
+                (near + winds[piece(7 * k + 1 + turn, window, spot)] * cells[spot])
+                + winds[piece(sweep, window, spot)] * swept
             )
         return out
+
+    def carried(cells, k, backward):
+        return carried_at(copies(cells, 1), k, backward, 0)
 
     def each(function, *lists):
         return [function(*values) for values in zip(*lists)]
@@ -331,9 +349,11 @@
             sunk[index] = [scaled(upper[size], cells[size]) for size in sizes]
             if index < 2:
                 cells = [each(lambda a, b: a - b, carried(cells[size], 0, False), sunk[index][size]) for size in sizes]
-        both = total_of(cells)
-        both = each(lambda a, b: a - b, carried(both, 0, False), total_of(sunk[2]))
-        both = carried(both, 0, False)
+        turned, sinking = copies(total_of(cells), 2), copies(total_of(sunk[2]), 1)
+        both = {
+            turn: each(lambda a, b: a - b, carried_at(turned, 0, False, turn), sinking[turn]) for turn in (-1, 0, 1)
+        }
+        both = carried_at(both, 0, False, 0)
         factors = []
         for size in sizes:
             rate = -lower[size]
@@ -350,18 +370,24 @@
             c3 = added(f3, first)
             factors.append([c3, c2, c1, c0])
         moved = total_of(bottom)
-        for index in range(4):
-            moved = added(carried(moved, 1, False), total_of([factor[index] for factor in factors]))
-        return added(both, moved)
+        sums = [total_of([factor[index] for factor in factors]) for index in range(4)]
+        for index in range(2):
+            moved = added(carried(moved, 1, False), sums[index])
+        turned, third = copies(moved, 2), copies(sums[2], 1)
+        moved = {turn: added(carried_at(turned, 1, False, turn), third[turn]) for turn in (-1, 0, 1)}
+        return added(both, added(carried_at(moved, 1, False, 0), sums[3]))
 
     def spread_backward(start):
-        powers = [start]
-        for _ in range(4):
+        turned = copies(start, 2)
+        lower_one, upper_one = (
+            {turn: carried_at(turned, k, True, turn) for turn in (-1, 0, 1)} for k in (1, 0)
+        )
+        powers = [start, lower_one[0], carried_at(lower_one, 1, True, 0)]
+        for _ in range(2):
             powers.append(carried(powers[-1], 1, True))
         twice, thrice, thrice_more = scaled(2.0, powers[1]), scaled(3.0, powers[1]), scaled(3.0, powers[2])
         four, six, four_more = scaled(4.0, powers[1]), scaled(6.0, powers[2]), scaled(4.0, powers[3])
-        first = carried(start, 0, True)
-        second = carried(first, 0, True)
+        first, second = upper_one[0], carried_at(upper_one, 0, True, 0)
         gap = each(lambda a, b: a - b, powers[1], first)
         tops, bottoms = [], []
         for size in sizes:
@@ -377,7 +403,7 @@
         return tops + bottoms
 
     scale = 1.0 / fields
-    mask = [winds[piece(3 * levels, window, spot)] for spot in spots]
+    mask = [winds[piece(7 * levels, window, spot)] for spot in spots]
     for field in range(fields):
         for spot in spots:
             change[piece(field, window, spot)] = jnp.zeros((EDGE, LANES), jnp.float32)
@@ -569,7 +595,7 @@
                 pltpu.VMEM((slots, bins, 1, cols, rows), jnp.float32),
                 field_store,
                 field_store,
-                pltpu.VMEM((7 * window, LANES), jnp.float32),
+                pltpu.VMEM((15 * window, LANES), jnp.float32),
                 pltpu.VMEM((2 * window, LANES), jnp.float32),
                 pltpu.SemaphoreType.DMA,
                 pltpu.SemaphoreType.DMA((slots * bins + 1,)),

time: 16.4 us -> 16.2 us (0.988)
  Pallas kernels: 5.68 us -> 5.49 us
    pallas_call x1, Pallas kernels: 2.76 us -> 2.56 us  [per_device(): pl.pallas_call(cycle, out_shape=(jax.ShapeDtypeStruct(trajectory.shape, j...]
where the time goes in v5:
time: 16.2 us; the launch traced here: 15.9 us
  starting transfers between devices  5.74 us (35%)
  Pallas kernels  5.49 us (34%)
  waiting for transfers between devices  4.03 us (25%)
  between operations  0.66 us (4%)
    ppermute x4, starting transfers between devices, moved(): return lax.ppermute(values, AXES, pairs)  5.74 us
    ppermute x4, waiting for transfers between devices, moved(): return lax.ppermute(values, AXES, pairs)  4.03 us
    pallas_call x1, Pallas kernels, per_device(): pl.pallas_call(cycle, out_shape=(jax.ShapeDtypeStruct(trajectory.shape, j...  2.56 us
    pallas_call x1, Pallas kernels, per_device(): pl.pallas_call(tabulate, out_shape=(pltpu.VMEM((2, window, LANES), jnp.fl...  1.35 us
    pallas_call x1, Pallas kernels, per_device(): pl.pallas_call(restrict, out_shape=pltpu.VMEM((rows, LANES), jnp.float32)...  1.34 us
  transfers between devices with their start and end apart: 4, of which 4 were waited for; matrix products, arithmetic and copies ran while one was open for 0% of the time, Pallas kernels for 10%

profile of v5, /device:TPU:0, one launch (start us, length us, event | category | flops | bytes accessed | tf_op | source)
XLA Modules:
  0.0 15.9 jit_solution(6219282705120016574)
XLA Ops:
  0.6 1.3 %shard_map.95 = f32[32,128]{1,0:T(8,128)S(1)} custom-call(bf16[2,3,1,256,128]{4,3,2,1,0:T(8,128)(2,1)} %refs_4_.3, f32[8,8]{1,0:T(8,128)} %refs_4_.2, f32[1,16,32]{2,1,0:T(8,128)} %bitcast.18, s32[16,32]{1,0:T(8,128)} %bitcast.19), custom_call_target="tpu_custom_call" | custom-call | tf_op jit(solution)/shard_map/pallas_call | solution.py:508
  2.0 0.5 %collective-permute-start = (f32[32,128]{1,0:T(8,128)S(1)}, f32[32,128]{1,0:T(8,128)S(1)}, u32[]{:S(2)}, u32[]{:S(2)}) collective-permute-start(f32[32,128]{1,0:T(8,128)S(1)} %shard_map.95), channel_id=1, source_target_pairs={{1,0},{0,1},{3,2},{2,3},{5,4},{4,5},{7,6},{6,7},{9,8},{8,9},{11,10... | collective-permute-start | bytes 49160 | tf_op jit(solution)/shard_map/ppermute | solution.py:481
  2.5 0.8 %collective-permute-done = f32[32,128]{1,0:T(8,128)S(1)} collective-permute-done((f32[32,128]{1,0:T(8,128)S(1)}, f32[32,128]{1,0:T(8,128)S(1)}, u32[]{:S(2)}, u32[]{:S(2)}) %collective-permute-start) | collective-permute-done | bytes 16416 | tf_op jit(solution)/shard_map/ppermute | solution.py:481
  3.3 2.9 %collective-permute-start.1 = (f32[2,32,128]{2,1,0:T(8,128)S(1)}, f32[2,32,128]{2,1,0:T(8,128)S(1)}, u32[]{:S(2)}, u32[]{:S(2)}) collective-permute-start(f32[2,32,128]{2,1,0:T(8,128)S(1)} %pad_maximum_fusion.3.refs_0_), channel_id=1, source_target_pairs={{4,0},{13,1},{6,2},{15,3},{0,4},{9,5},{2,6},{11,7},{12,8},{5,9},{1... | collective-permute-start | bytes 98312 | tf_op jit(solution)/shard_map/ppermute | solution.py:481
  6.3 1.3 %shard_map.96 = (f32[2,48,128]{2,1,0:T(8,128)S(1)}, f32[7,8,128]{2,1,0:T(8,128)S(1)}) custom-call(s32[32,64]{1,0:T(8,128)} %bitcast.17, f32[2,32,64]{2,1,0:T(8,128)} %bitcast.15, f32[2,32,64]{2,1,0:T(8,128)} %bitcast.16, f32[2,3]{1,0:T(2,128)} %bitcast.20, f32[8,8]{1,0:T(8,128)} %refs_4_.2), custom_call_target="tpu_custom_call" | custom-call | tf_op jit(solution)/shard_map/pallas_call | solution.py:534
  7.6 0.5 %collective-permute-done.1.refs_1_ = f32[2,32,128]{2,1,0:T(8,128)S(1)} collective-permute-done((f32[2,32,128]{2,1,0:T(8,128)S(1)}, f32[2,32,128]{2,1,0:T(8,128)S(1)}, u32[]{:S(2)}, u32[]{:S(2)}) %collective-permute-start.1) | collective-permute-done | bytes 32800 | tf_op jit(solution)/shard_map/ppermute | solution.py:481
  8.1 1.9 %collective-permute-start.2 = (f32[4,16,128]{2,1,0:T(8,128)S(1)}, f32[4,16,128]{2,1,0:T(8,128)S(1)}, u32[]{:S(2)}, u32[]{:S(2)}) collective-permute-start(f32[4,16,128]{2,1,0:T(8,128)S(1)} %pad_maximum_fusion.1), channel_id=1, source_target_pairs={{2,0},{3,1},{0,2},{1,3},{6,4},{7,5},{4,6},{5,7},{10,8},{11,9},{8,1... | collective-permute-start | bytes 98312 | tf_op jit(solution)/shard_map/ppermute | solution.py:481
  10.1 2.0 %collective-permute-done.2.refs_2_ = f32[4,16,128]{2,1,0:T(8,128)S(1)} collective-permute-done((f32[4,16,128]{2,1,0:T(8,128)S(1)}, f32[4,16,128]{2,1,0:T(8,128)S(1)}, u32[]{:S(2)}, u32[]{:S(2)}) %collective-permute-start.2) | collective-permute-done | bytes 32800 | tf_op jit(solution)/shard_map/ppermute | solution.py:481
  12.1 0.4 %collective-permute-start.3 = (f32[2,48,128]{2,1,0:T(8,128)S(1)}, f32[2,48,128]{2,1,0:T(8,128)S(1)}, u32[]{:S(2)}, u32[]{:S(2)}) collective-permute-start(f32[2,48,128]{2,1,0:T(8,128)S(1)} %pad_maximum_fusion), channel_id=1, source_target_pairs={{1,0},{0,1},{3,2},{2,3},{5,4},{4,5},{7,6},{6,7},{9,8},{8,9},{11,10... | collective-permute-start | bytes 147464 | tf_op jit(solution)/shard_map/ppermute | solution.py:481
  12.4 0.2 %shard_map.97.refs_0_ = f32[624,128]{1,0:T(8,128)S(1)} custom-call(f32[2,32,128]{2,1,0:T(8,128)S(1)} %pad_maximum_fusion.3.refs_0_, f32[2,32,128]{2,1,0:T(8,128)S(1)} %collective-permute-done.1.refs_1_, f32[4,16,128]{2,1,0:T(8,128)S(1)} %collective-permute-done.2.refs_2_), custom_call_target="tpu_custom_call" | custom-call | tf_op jit(solution)/shard_map/pallas_call | solution.py:574
  12.7 0.7 %collective-permute-done.3.refs_1_ = f32[2,48,128]{2,1,0:T(8,128)S(1)} collective-permute-done((f32[2,48,128]{2,1,0:T(8,128)S(1)}, f32[2,48,128]{2,1,0:T(8,128)S(1)}, u32[]{:S(2)}, u32[]{:S(2)}) %collective-permute-start.3) | collective-permute-done | bytes 49184 | tf_op jit(solution)/shard_map/ppermute | solution.py:481
  13.4 2.6 %shard_map.98 = (bf16[2,3,1,256,128]{4,3,2,1,0:T(8,128)(2,1)}, f32[2,3,1,16,32]{4,3,2,1,0:T(8,128)}) custom-call(f32[624,128]{1,0:T(8,128)S(1)} %shard_map.97.refs_0_, f32[2,48,128]{2,1,0:T(8,128)S(1)} %collective-permute-done.3.refs_1_, f32[96,128]{1,0:T(8,128)S(1)} %bitcast.12, f32[7,8,128]{2,1,0:T(8,128)S(1)} %get-tuple-element.17.refs_3_, ...), custom_call_target="tpu_custom_call" | custom-call | tf_op jit(solution)/shard_map/pallas_call | solution.py:584
  (4 shorter events, 0.0 us)
Async XLA Ops:
  2.0 1.4 %collective-permute-start = (f32[32,128]{1,0:T(8,128)S(1)}, f32[32,128]{1,0:T(8,128)S(1)}, u32[]{:S(2)}, u32[]{:S(2)}) collective-permute-start(f32[32,128]{1,0:T(8,128)S(1)} %shard_map.95), channel_id=1, source_target_pairs={{1,0},{0,1},{3,2},{2,3},{5,4},{4,5},{7,6},{6,7},{9,8},{8,9},{11,10... | collective-permute-start | bytes 49160 | tf_op jit(solution)/shard_map/ppermute | solution.py:481
  3.3 4.8 %collective-permute-start.1 = (f32[2,32,128]{2,1,0:T(8,128)S(1)}, f32[2,32,128]{2,1,0:T(8,128)S(1)}, u32[]{:S(2)}, u32[]{:S(2)}) collective-permute-start(f32[2,32,128]{2,1,0:T(8,128)S(1)} %pad_maximum_fusion.3.refs_0_), channel_id=1, source_target_pairs={{4,0},{13,1},{6,2},{15,3},{0,4},{9,5},{2,6},{11,7},{12,8},{5,9},{1... | collective-permute-start | bytes 98312 | tf_op jit(solution)/shard_map/ppermute | solution.py:481
  8.1 3.9 %collective-permute-start.2 = (f32[4,16,128]{2,1,0:T(8,128)S(1)}, f32[4,16,128]{2,1,0:T(8,128)S(1)}, u32[]{:S(2)}, u32[]{:S(2)}) collective-permute-start(f32[4,16,128]{2,1,0:T(8,128)S(1)} %pad_maximum_fusion.1), channel_id=1, source_target_pairs={{2,0},{3,1},{0,2},{1,3},{6,4},{7,5},{4,6},{5,7},{10,8},{11,9},{8,1... | collective-permute-start | bytes 98312 | tf_op jit(solution)/shard_map/ppermute | solution.py:481
  12.1 1.3 %collective-permute-start.3 = (f32[2,48,128]{2,1,0:T(8,128)S(1)}, f32[2,48,128]{2,1,0:T(8,128)S(1)}, u32[]{:S(2)}, u32[]{:S(2)}) collective-permute-start(f32[2,48,128]{2,1,0:T(8,128)S(1)} %pad_maximum_fusion), channel_id=1, source_target_pairs={{1,0},{0,1},{3,2},{2,3},{5,4},{4,5},{7,6},{6,7},{9,8},{8,9},{11,10... | collective-permute-start | bytes 147464 | tf_op jit(solution)/shard_map/ppermute | solution.py:481

commit v6 on v5

--- a/solution.py
+++ b/solution.py
@@ -149,36 +149,22 @@
     return slice(start, start + EDGE)
 
 
-def lay(lat_count, window, laid, place, block, rims):
-    lat, own = window_start(lat_count, block.shape[0], window)
-    rows = block.shape[0]
-
-    def at(row, size):
-        return pl.ds(pl.multiple_of(place * window + row, 8), size)
-
+def lay_block(lat_count, window, rows, store):
+    lat, own = window_start(lat_count, rows, window)
     if lat_count == 2:
-        outer = lat * 2 * REACH
-        laid[at(REACH, REACH)] = block[:REACH]
-        laid[at(outer, REACH)] = block[REACH:]
-        laid[at(2 * REACH - outer, REACH)] = rims[...]
+        store(0, REACH, REACH)
+        store(REACH, rows - REACH, lat * 2 * REACH)
     else:
-        laid[at(own, rows)] = block[...]
-
-        @pl.when(lat == 0)
-        def _():
-            laid[at(window - REACH, REACH)] = jnp.zeros((REACH, LANES), jnp.float32)
-
-        @pl.when(lat == lat_count - 1)
-        def _():
-            laid[at(0, REACH)] = jnp.zeros((REACH, LANES), jnp.float32)
-
-        @pl.when(lat > 0)
-        def _():
-            laid[at(own - REACH, REACH)] = rims[:REACH]
-
-        @pl.when(lat < lat_count - 1)
-        def _():
-            laid[at(own + rows, REACH)] = rims[REACH:]
+        store(0, rows, own)
+
+
+def lay_rims(lat_count, window, rows, store):
+    lat, own = window_start(lat_count, rows, window)
+    if lat_count == 2:
+        store(0, REACH, 2 * REACH - lat * 2 * REACH)
+    else:
+        pl.when(lat > 0)(lambda: store(0, REACH, own - REACH))
+        pl.when(lat < lat_count - 1)(lambda: store(REACH, REACH, own + rows))
 
 
 def near_is_west():
@@ -211,10 +197,21 @@
     levels = 2
     fields = levels * bins
     level = lax.axis_index("lev")
+    laid[...] = jnp.zeros(laid.shape, jnp.float32)
     for rank in range(levels):
         at = (rank + level) % levels
-        lay(lat_count, window, laid, at * 2, own_cells.at[rank], rims.at[rank])
-        lay(lat_count, window, laid, at * 2 + 1, near_cells.at[rank], rims.at[levels + rank])
+
+        def store_of(block, place):
+            def store(start, size, row):
+                laid[pl.ds(pl.multiple_of(place * window + row, 8), size)] = block[pl.ds(start, size)]
+
+            return store
+
+        lay_block(lat_count, window, rows, store_of(own_cells.at[rank], at * 2))
+        lay_block(lat_count, window, rows, store_of(near_cells.at[rank], at * 2 + 1))
+        if rank == 0:
+            lay_rims(lat_count, window, rows, store_of(rims.at[0], at * 2))
+        lay_rims(lat_count, window, rows, store_of(rims.at[1 + rank], at * 2 + 1))
     side = jnp.where(near_is_west(), 0, 2)
     for k in range(levels):
         for spot in range(window // EDGE):
@@ -263,13 +260,32 @@
     level = lax.axis_index("lev")
     count = window // EDGE
     spots = range(count)
+    kinds = bins + 3
+    side = jnp.where(near_is_west(), 2, 0)
+    if lat_count != 2:
+        laid[...] = jnp.zeros(laid.shape, jnp.float32)
+
+    def store_of(first, at, place, more_to):
+        def store(start, size, row):
+            for part in range(0, size, EDGE):
+                share = shares(far[pl.ds(first + start + part, EDGE)], place, bins, cols)
+                for kind in range(kinds):
+                    target = (at * kinds + kind) * window + row + part
+                    target = pl.ds(pl.multiple_of(target, 8), EDGE)
+                    laid[target] = laid[target] + share[kind] if more_to else share[kind]
+
+        return store
+
+    height = window - rows
     for rank in range(levels):
         at = (rank + level) % levels
-        lay(lat_count, window, laid, at, far.at[1 - rank, pl.ds(0, rows)], far.at[1 - rank, pl.ds(rows, window - rows)])
-    side = jnp.where(near_is_west(), 2, 0)
+        lay_block(lat_count, window, rows, store_of((1 - rank) * rows, at, side, False))
+        first = levels * rows + (2 - rank) * height
+        lay_rims(lat_count, window, rows, store_of(first, at, side, False))
+    lay_rims(lat_count, window, rows, store_of(levels * rows, 1 - level, 1, True))
     for k in range(levels):
         for spot in spots:
-            share = shares(rows_of(laid, k, window, spot), side, bins, cols)
+            share = [rows_of(laid, k * kinds + kind, window, spot) for kind in range(kinds)]
             for size in range(bins):
                 at = piece(k * bins + size, window, spot)
                 coarse[at] = begun[at] + share[size]
@@ -546,8 +562,7 @@
 
         own = jnp.stack([packed, moved(packed, lambda lon, lat, lev: (lon, lat, 1 - lev))])
         near = moved(own, lambda lon, lat, lev: (lon ^ 1 if lev == 0 else lon + 1 - 2 * ((lon + 1) % 2), lat, lev))
-        near, table, scales = lax.optimization_barrier((near, table, scales))
-        held = jnp.concatenate([own, near])
+        held = jnp.concatenate([packed[None], near])
         if lat_count == 2:
             rims = moved(held[:, :REACH], lambda lon, lat, lev: (lon, 1 - lat, lev))
         else:
@@ -558,7 +573,8 @@
                 held[:, :REACH], lambda lon, lat, lev: (lon, lat + 1, lev) if lat < lat_count - 1 else None
             )
             rims = jnp.concatenate([low, high], axis=1)
-        brought = jnp.concatenate([near, rims[2:]], axis=1)
+        rims, table, scales = lax.optimization_barrier((rims, table, scales))
+        brought = jnp.concatenate([near.reshape(-1, LANES), rims.reshape(-1, LANES)])
         far = moved(brought, lambda lon, lat, lev: (lon, lat, 1 - lev))
 
         def cycle(*refs):
@@ -596,7 +612,7 @@
                 field_store,
                 field_store,
                 pltpu.VMEM((15 * window, LANES), jnp.float32),
-                pltpu.VMEM((2 * window, LANES), jnp.float32),
+                pltpu.VMEM((2 * (bins + 3) * window, LANES), jnp.float32),
                 pltpu.SemaphoreType.DMA,
                 pltpu.SemaphoreType.DMA((slots * bins + 1,)),
             ],

time: 16.2 us -> 16.1 us (level)
  starting transfers between devices: 5.74 us -> 5.55 us
    ppermute x4, starting transfers between devices: 5.74 us -> 5.55 us  [moved(): return lax.ppermute(values, AXES, pairs)]
where the time goes in v6:
time: 16.1 us; the launch traced here: 15.8 us
  Pallas kernels  5.55 us (34%)
  starting transfers between devices  5.55 us (34%)
  waiting for transfers between devices  4.09 us (25%)
  between operations  0.66 us (4%)
    ppermute x4, starting transfers between devices, moved(): return lax.ppermute(values, AXES, pairs)  5.55 us
    ppermute x4, waiting for transfers between devices, moved(): return lax.ppermute(values, AXES, pairs)  4.09 us
    pallas_call x1, Pallas kernels, per_device(): pl.pallas_call(cycle, out_shape=(jax.ShapeDtypeStruct(trajectory.shape, j...  2.62 us
    pallas_call x1, Pallas kernels, per_device(): pl.pallas_call(tabulate, out_shape=(pltpu.VMEM((2, window, LANES), jnp.fl...  1.35 us
    pallas_call x1, Pallas kernels, per_device(): pl.pallas_call(restrict, out_shape=pltpu.VMEM((rows, LANES), jnp.float32)...  1.34 us
  transfers between devices with their start and end apart: 4, of which 4 were waited for; matrix products, arithmetic and copies ran while one was open for 0% of the time, Pallas kernels for 10%

profile of v6, /device:TPU:0, one launch (start us, length us, event | category | flops | bytes accessed | tf_op | source)
XLA Modules:
  0.0 15.8 jit_solution(136554222925309089)
XLA Ops:
  0.6 1.3 %shard_map.95 = f32[32,128]{1,0:T(8,128)S(1)} custom-call(bf16[2,3,1,256,128]{4,3,2,1,0:T(8,128)(2,1)} %refs_4_.3, f32[8,8]{1,0:T(8,128)} %refs_4_.2, f32[1,16,32]{2,1,0:T(8,128)} %bitcast.21, s32[16,32]{1,0:T(8,128)} %bitcast.22), custom_call_target="tpu_custom_call" | custom-call | tf_op jit(solution)/shard_map/pallas_call | solution.py:524
  2.0 0.5 %collective-permute-start = (f32[32,128]{1,0:T(8,128)S(1)}, f32[32,128]{1,0:T(8,128)S(1)}, u32[]{:S(2)}, u32[]{:S(2)}) collective-permute-start(f32[32,128]{1,0:T(8,128)S(1)} %shard_map.95), channel_id=1, source_target_pairs={{1,0},{0,1},{3,2},{2,3},{5,4},{4,5},{7,6},{6,7},{9,8},{8,9},{11,10... | collective-permute-start | bytes 49160 | tf_op jit(solution)/shard_map/ppermute | solution.py:497
  2.5 0.8 %collective-permute-done = f32[32,128]{1,0:T(8,128)S(1)} collective-permute-done((f32[32,128]{1,0:T(8,128)S(1)}, f32[32,128]{1,0:T(8,128)S(1)}, u32[]{:S(2)}, u32[]{:S(2)}) %collective-permute-start) | collective-permute-done | bytes 16416 | tf_op jit(solution)/shard_map/ppermute | solution.py:497
  3.3 2.9 %collective-permute-start.1 = (f32[2,32,128]{2,1,0:T(8,128)S(1)}, f32[2,32,128]{2,1,0:T(8,128)S(1)}, u32[]{:S(2)}, u32[]{:S(2)}) collective-permute-start(f32[2,32,128]{2,1,0:T(8,128)S(1)} %pad_maximum_fusion.1.refs_0_), channel_id=1, source_target_pairs={{4,0},{13,1},{6,2},{15,3},{0,4},{9,5},{2,6},{11,7},{12,8},{5,9},{1... | collective-permute-start | bytes 98312 | tf_op jit(solution)/shard_map/ppermute | solution.py:497
  6.3 1.9 %collective-permute-done.1.refs_1_ = f32[2,32,128]{2,1,0:T(8,128)S(1)} collective-permute-done((f32[2,32,128]{2,1,0:T(8,128)S(1)}, f32[2,32,128]{2,1,0:T(8,128)S(1)}, u32[]{:S(2)}, u32[]{:S(2)}) %collective-permute-start.1) | collective-permute-done | bytes 32800 | tf_op jit(solution)/shard_map/ppermute | solution.py:497
  8.1 1.9 %collective-permute-start.2 = (f32[3,16,128]{2,1,0:T(8,128)S(1)}, f32[3,16,128]{2,1,0:T(8,128)S(1)}, u32[]{:S(2)}, u32[]{:S(2)}) collective-permute-start(f32[3,16,128]{2,1,0:T(8,128)S(1)} %pad_maximum_fusion.2), channel_id=1, source_target_pairs={{2,0},{3,1},{0,2},{1,3},{6,4},{7,5},{4,6},{5,7},{10,8},{11,9},{8,1... | collective-permute-start | bytes 73736 | tf_op jit(solution)/shard_map/ppermute | solution.py:497
  10.1 1.3 %shard_map.96 = (f32[2,48,128]{2,1,0:T(8,128)S(1)}, f32[7,8,128]{2,1,0:T(8,128)S(1)}) custom-call(s32[32,64]{1,0:T(8,128)} %bitcast.19, f32[2,32,64]{2,1,0:T(8,128)} %bitcast.17, f32[2,32,64]{2,1,0:T(8,128)} %bitcast.18, f32[2,3]{1,0:T(2,128)} %bitcast.23, f32[8,8]{1,0:T(8,128)} %refs_4_.2), custom_call_target="tpu_custom_call" | custom-call | tf_op jit(solution)/shard_map/pallas_call | solution.py:550
  11.4 0.5 %collective-permute-done.2.refs_2_ = f32[3,16,128]{2,1,0:T(8,128)S(1)} collective-permute-done((f32[3,16,128]{2,1,0:T(8,128)S(1)}, f32[3,16,128]{2,1,0:T(8,128)S(1)}, u32[]{:S(2)}, u32[]{:S(2)}) %collective-permute-start.2) | collective-permute-done | bytes 24608 | tf_op jit(solution)/shard_map/ppermute | solution.py:497
  12.0 0.2 %collective-permute-start.3 = (f32[112,128]{1,0:T(8,128)S(1)}, f32[112,128]{1,0:T(8,128)S(1)}, u32[]{:S(2)}, u32[]{:S(2)}) collective-permute-start(f32[112,128]{1,0:T(8,128)S(1)} %pad_maximum_fusion), channel_id=1, source_target_pairs={{1,0},{0,1},{3,2},{2,3},{5,4},{4,5},{7,6},{6,7},{9,8},{8,9},{11,10... | collective-permute-start | bytes 172040 | tf_op jit(solution)/shard_map/ppermute | solution.py:497
  12.2 0.2 %shard_map.97.refs_0_ = f32[624,128]{1,0:T(8,128)S(1)} custom-call(f32[2,32,128]{2,1,0:T(8,128)S(1)} %pad_maximum_fusion.1.refs_0_, f32[2,32,128]{2,1,0:T(8,128)S(1)} %collective-permute-done.1.refs_1_, f32[3,16,128]{2,1,0:T(8,128)S(1)} %collective-permute-done.2.refs_2_), custom_call_target="tpu_custom_call" | custom-call | tf_op jit(solution)/shard_map/pallas_call | solution.py:590
  12.4 0.8 %collective-permute-done.3.refs_1_ = f32[112,128]{1,0:T(8,128)S(1)} collective-permute-done((f32[112,128]{1,0:T(8,128)S(1)}, f32[112,128]{1,0:T(8,128)S(1)}, u32[]{:S(2)}, u32[]{:S(2)}) %collective-permute-start.3) | collective-permute-done | bytes 57376 | tf_op jit(solution)/shard_map/ppermute | solution.py:497
  13.2 2.6 %shard_map.98 = (bf16[2,3,1,256,128]{4,3,2,1,0:T(8,128)(2,1)}, f32[2,3,1,16,32]{4,3,2,1,0:T(8,128)}) custom-call(f32[624,128]{1,0:T(8,128)S(1)} %shard_map.97.refs_0_, f32[112,128]{1,0:T(8,128)S(1)} %collective-permute-done.3.refs_1_, f32[96,128]{1,0:T(8,128)S(1)} %bitcast.16, f32[7,8,128]{2,1,0:T(8,128)S(1)} %get-tuple-element.17.refs_3_, ...), custom_call_target="tpu_custom_call" | custom-call | tf_op jit(solution)/shard_map/pallas_call | solution.py:600
  (3 shorter events, 0.0 us)
Async XLA Ops:
  2.0 1.4 %collective-permute-start = (f32[32,128]{1,0:T(8,128)S(1)}, f32[32,128]{1,0:T(8,128)S(1)}, u32[]{:S(2)}, u32[]{:S(2)}) collective-permute-start(f32[32,128]{1,0:T(8,128)S(1)} %shard_map.95), channel_id=1, source_target_pairs={{1,0},{0,1},{3,2},{2,3},{5,4},{4,5},{7,6},{6,7},{9,8},{8,9},{11,10... | collective-permute-start | bytes 49160 | tf_op jit(solution)/shard_map/ppermute | solution.py:497
  3.3 4.8 %collective-permute-start.1 = (f32[2,32,128]{2,1,0:T(8,128)S(1)}, f32[2,32,128]{2,1,0:T(8,128)S(1)}, u32[]{:S(2)}, u32[]{:S(2)}) collective-permute-start(f32[2,32,128]{2,1,0:T(8,128)S(1)} %pad_maximum_fusion.1.refs_0_), channel_id=1, source_target_pairs={{4,0},{13,1},{6,2},{15,3},{0,4},{9,5},{2,6},{11,7},{12,8},{5,9},{1... | collective-permute-start | bytes 98312 | tf_op jit(solution)/shard_map/ppermute | solution.py:497
  8.1 3.8 %collective-permute-start.2 = (f32[3,16,128]{2,1,0:T(8,128)S(1)}, f32[3,16,128]{2,1,0:T(8,128)S(1)}, u32[]{:S(2)}, u32[]{:S(2)}) collective-permute-start(f32[3,16,128]{2,1,0:T(8,128)S(1)} %pad_maximum_fusion.2), channel_id=1, source_target_pairs={{2,0},{3,1},{0,2},{1,3},{6,4},{7,5},{4,6},{5,7},{10,8},{11,9},{8,1... | collective-permute-start | bytes 73736 | tf_op jit(solution)/shard_map/ppermute | solution.py:497
  12.0 1.2 %collective-permute-start.3 = (f32[112,128]{1,0:T(8,128)S(1)}, f32[112,128]{1,0:T(8,128)S(1)}, u32[]{:S(2)}, u32[]{:S(2)}) collective-permute-start(f32[112,128]{1,0:T(8,128)S(1)} %pad_maximum_fusion), channel_id=1, source_target_pairs={{1,0},{0,1},{3,2},{2,3},{5,4},{4,5},{7,6},{6,7},{9,8},{8,9},{11,10... | collective-permute-start | bytes 172040 | tf_op jit(solution)/shard_map/ppermute | solution.py:497

commit v7 on v6

--- a/solution.py
+++ b/solution.py
@@ -399,12 +399,15 @@
             {turn: carried_at(turned, k, True, turn) for turn in (-1, 0, 1)} for k in (1, 0)
         )
         powers = [start, lower_one[0], carried_at(lower_one, 1, True, 0)]
-        for _ in range(2):
-            powers.append(carried(powers[-1], 1, True))
+        later = copies(powers[2], 2)
+        lower_three = {turn: carried_at(later, 1, True, turn) for turn in (-1, 0, 1)}
+        powers += [lower_three[0], carried_at(lower_three, 1, True, 0)]
         twice, thrice, thrice_more = scaled(2.0, powers[1]), scaled(3.0, powers[1]), scaled(3.0, powers[2])
         four, six, four_more = scaled(4.0, powers[1]), scaled(6.0, powers[2]), scaled(4.0, powers[3])
         first, second = upper_one[0], carried_at(upper_one, 0, True, 0)
         gap = each(lambda a, b: a - b, powers[1], first)
+        third = carried(second, 0, True)
+        next_gap = each(lambda a, b: a - b, carried_at(lower_one, 0, True, 0), second)
         tops, bottoms = [], []
         for size in sizes:
             rate = -lower[size]
@@ -412,21 +415,19 @@
             low_three = more(powers[3], rate, more(thrice_more, rate, more(thrice, rate, start)))
             low_four = more(powers[4], rate, more(four_more, rate, more(six, rate, more(four, rate, start))))
             cells = more(second, upper[size], more(gap, rate, start))
-            for below in (low_two, low_three):
-                cells = more(carried(cells, 0, True), upper[size], each(lambda a, b: a - b, below, cells))
+            gain = added(more(next_gap, rate, first), each(lambda a, b: a - b, low_two, cells))
+            cells = more(third, upper[size], gain)
+            gain = each(lambda a, b: a - b, low_three, cells)
+            cells = more(carried(cells, 0, True), upper[size], gain)
             tops.append(cells)
             bottoms.append(low_four)
         return tops + bottoms
 
     scale = 1.0 / fields
     mask = [winds[piece(7 * levels, window, spot)] for spot in spots]
-    for field in range(fields):
-        for spot in spots:
-            change[piece(field, window, spot)] = jnp.zeros((EDGE, LANES), jnp.float32)
-
-    def one_sweep(sweep, carry):
+    for sweep in range(SWEEPS):
         cells = [[coarse[piece(field, window, spot)] for spot in spots] for field in range(fields)]
-        if True:
+        if sweep:
             cells = [added(cells[field], [change[piece(field, window, spot)] for spot in spots]) for field in range(fields)]
         total = summed_forward(cells[:bins], cells[bins:])
         start = [
@@ -436,19 +437,16 @@
         adjoint = spread_backward(start)
         for field in range(fields):
             for spot in spots:
-                if True:
+                if sweep:
                     old = change[piece(field, window, spot)]
                     value = old - step_length * (background * old + adjoint[field][spot])
                 else:
                     value = -step_length * adjoint[field][spot]
-                change[piece(field, window, spot)] = mask[spot] * value
-        return carry
-
-    lax.fori_loop(0, SWEEPS, one_sweep, 0)
-
-    for field in range(fields):
-        for spot in spots:
-            coarse[pl.ds(field * window + spot, EDGE, stride=count), :] = change[piece(field, window, spot)]
+                if sweep < SWEEPS - 1:
+                    change[piece(field, window, spot)] = mask[spot] * value
+                else:
+                    coarse[pl.ds(field * window + spot, EDGE, stride=count), :] = mask[spot] * value
+
     final = [
         coarse[pl.ds(pl.multiple_of((level * bins + size) * window + own, 8), rows)] for size in range(bins)
     ]

time: 16.1 us -> 15.9 us (0.988)
  Pallas kernels: 5.55 us -> 5.31 us
    pallas_call x1, Pallas kernels: 2.62 us -> 2.39 us  [per_device(): pl.pallas_call(cycle, out_shape=(jax.ShapeDtypeStruct(trajectory.shape, j...]
where the time goes in v7:
time: 15.9 us; the launch traced here: 15.6 us
  starting transfers between devices  5.55 us (35%)
  Pallas kernels  5.31 us (33%)
  waiting for transfers between devices  4.09 us (26%)
  between operations  0.66 us (4%)
    ppermute x4, starting transfers between devices, moved(): return lax.ppermute(values, AXES, pairs)  5.55 us
    ppermute x4, waiting for transfers between devices, moved(): return lax.ppermute(values, AXES, pairs)  4.09 us
    pallas_call x1, Pallas kernels, per_device(): pl.pallas_call(cycle, out_shape=(jax.ShapeDtypeStruct(trajectory.shape, j...  2.39 us
    pallas_call x1, Pallas kernels, per_device(): pl.pallas_call(tabulate, out_shape=(pltpu.VMEM((2, window, LANES), jnp.fl...  1.35 us
    pallas_call x1, Pallas kernels, per_device(): pl.pallas_call(restrict, out_shape=pltpu.VMEM((rows, LANES), jnp.float32)...  1.34 us
  transfers between devices with their start and end apart: 4, of which 4 were waited for; matrix products, arithmetic and copies ran while one was open for 0% of the time, Pallas kernels for 10%

profile of v7, /device:TPU:0, one launch (start us, length us, event | category | flops | bytes accessed | tf_op | source)
XLA Modules:
  0.0 15.6 jit_solution(1325456880858640808)
XLA Ops:
  0.6 1.3 %shard_map.95 = f32[32,128]{1,0:T(8,128)S(1)} custom-call(bf16[2,3,1,256,128]{4,3,2,1,0:T(8,128)(2,1)} %refs_4_.3, f32[8,8]{1,0:T(8,128)} %refs_4_.2, f32[1,16,32]{2,1,0:T(8,128)} %bitcast.21, s32[16,32]{1,0:T(8,128)} %bitcast.22), custom_call_target="tpu_custom_call" | custom-call | tf_op jit(solution)/shard_map/pallas_call | solution.py:522
  2.0 0.5 %collective-permute-start = (f32[32,128]{1,0:T(8,128)S(1)}, f32[32,128]{1,0:T(8,128)S(1)}, u32[]{:S(2)}, u32[]{:S(2)}) collective-permute-start(f32[32,128]{1,0:T(8,128)S(1)} %shard_map.95), channel_id=1, source_target_pairs={{1,0},{0,1},{3,2},{2,3},{5,4},{4,5},{7,6},{6,7},{9,8},{8,9},{11,10... | collective-permute-start | bytes 49160 | tf_op jit(solution)/shard_map/ppermute | solution.py:495
  2.5 0.8 %collective-permute-done = f32[32,128]{1,0:T(8,128)S(1)} collective-permute-done((f32[32,128]{1,0:T(8,128)S(1)}, f32[32,128]{1,0:T(8,128)S(1)}, u32[]{:S(2)}, u32[]{:S(2)}) %collective-permute-start) | collective-permute-done | bytes 16416 | tf_op jit(solution)/shard_map/ppermute | solution.py:495
  3.3 2.9 %collective-permute-start.1 = (f32[2,32,128]{2,1,0:T(8,128)S(1)}, f32[2,32,128]{2,1,0:T(8,128)S(1)}, u32[]{:S(2)}, u32[]{:S(2)}) collective-permute-start(f32[2,32,128]{2,1,0:T(8,128)S(1)} %pad_maximum_fusion.1.refs_0_), channel_id=1, source_target_pairs={{4,0},{13,1},{6,2},{15,3},{0,4},{9,5},{2,6},{11,7},{12,8},{5,9},{1... | collective-permute-start | bytes 98312 | tf_op jit(solution)/shard_map/ppermute | solution.py:495
  6.3 1.9 %collective-permute-done.1.refs_1_ = f32[2,32,128]{2,1,0:T(8,128)S(1)} collective-permute-done((f32[2,32,128]{2,1,0:T(8,128)S(1)}, f32[2,32,128]{2,1,0:T(8,128)S(1)}, u32[]{:S(2)}, u32[]{:S(2)}) %collective-permute-start.1) | collective-permute-done | bytes 32800 | tf_op jit(solution)/shard_map/ppermute | solution.py:495
  8.1 1.9 %collective-permute-start.2 = (f32[3,16,128]{2,1,0:T(8,128)S(1)}, f32[3,16,128]{2,1,0:T(8,128)S(1)}, u32[]{:S(2)}, u32[]{:S(2)}) collective-permute-start(f32[3,16,128]{2,1,0:T(8,128)S(1)} %pad_maximum_fusion.2), channel_id=1, source_target_pairs={{2,0},{3,1},{0,2},{1,3},{6,4},{7,5},{4,6},{5,7},{10,8},{11,9},{8,1... | collective-permute-start | bytes 73736 | tf_op jit(solution)/shard_map/ppermute | solution.py:495
  10.1 1.3 %shard_map.96 = (f32[2,48,128]{2,1,0:T(8,128)S(1)}, f32[7,8,128]{2,1,0:T(8,128)S(1)}) custom-call(s32[32,64]{1,0:T(8,128)} %bitcast.19, f32[2,32,64]{2,1,0:T(8,128)} %bitcast.17, f32[2,32,64]{2,1,0:T(8,128)} %bitcast.18, f32[2,3]{1,0:T(2,128)} %bitcast.23, f32[8,8]{1,0:T(8,128)} %refs_4_.2), custom_call_target="tpu_custom_call" | custom-call | tf_op jit(solution)/shard_map/pallas_call | solution.py:548
  11.4 0.5 %collective-permute-done.2.refs_2_ = f32[3,16,128]{2,1,0:T(8,128)S(1)} collective-permute-done((f32[3,16,128]{2,1,0:T(8,128)S(1)}, f32[3,16,128]{2,1,0:T(8,128)S(1)}, u32[]{:S(2)}, u32[]{:S(2)}) %collective-permute-start.2) | collective-permute-done | bytes 24608 | tf_op jit(solution)/shard_map/ppermute | solution.py:495
  12.0 0.2 %collective-permute-start.3 = (f32[112,128]{1,0:T(8,128)S(1)}, f32[112,128]{1,0:T(8,128)S(1)}, u32[]{:S(2)}, u32[]{:S(2)}) collective-permute-start(f32[112,128]{1,0:T(8,128)S(1)} %pad_maximum_fusion), channel_id=1, source_target_pairs={{1,0},{0,1},{3,2},{2,3},{5,4},{4,5},{7,6},{6,7},{9,8},{8,9},{11,10... | collective-permute-start | bytes 172040 | tf_op jit(solution)/shard_map/ppermute | solution.py:495
  12.2 0.2 %shard_map.97.refs_0_ = f32[624,128]{1,0:T(8,128)S(1)} custom-call(f32[2,32,128]{2,1,0:T(8,128)S(1)} %pad_maximum_fusion.1.refs_0_, f32[2,32,128]{2,1,0:T(8,128)S(1)} %collective-permute-done.1.refs_1_, f32[3,16,128]{2,1,0:T(8,128)S(1)} %collective-permute-done.2.refs_2_), custom_call_target="tpu_custom_call" | custom-call | tf_op jit(solution)/shard_map/pallas_call | solution.py:588
  12.4 0.8 %collective-permute-done.3.refs_1_ = f32[112,128]{1,0:T(8,128)S(1)} collective-permute-done((f32[112,128]{1,0:T(8,128)S(1)}, f32[112,128]{1,0:T(8,128)S(1)}, u32[]{:S(2)}, u32[]{:S(2)}) %collective-permute-start.3) | collective-permute-done | bytes 57376 | tf_op jit(solution)/shard_map/ppermute | solution.py:495
  13.2 2.4 %shard_map.98 = (bf16[2,3,1,256,128]{4,3,2,1,0:T(8,128)(2,1)}, f32[2,3,1,16,32]{4,3,2,1,0:T(8,128)}) custom-call(f32[624,128]{1,0:T(8,128)S(1)} %shard_map.97.refs_0_, f32[112,128]{1,0:T(8,128)S(1)} %collective-permute-done.3.refs_1_, f32[96,128]{1,0:T(8,128)S(1)} %bitcast.16, f32[7,8,128]{2,1,0:T(8,128)S(1)} %get-tuple-element.17.refs_3_, ...), custom_call_target="tpu_custom_call" | custom-call | tf_op jit(solution)/shard_map/pallas_call | solution.py:598
  (3 shorter events, 0.0 us)
Async XLA Ops:
  2.0 1.4 %collective-permute-start = (f32[32,128]{1,0:T(8,128)S(1)}, f32[32,128]{1,0:T(8,128)S(1)}, u32[]{:S(2)}, u32[]{:S(2)}) collective-permute-start(f32[32,128]{1,0:T(8,128)S(1)} %shard_map.95), channel_id=1, source_target_pairs={{1,0},{0,1},{3,2},{2,3},{5,4},{4,5},{7,6},{6,7},{9,8},{8,9},{11,10... | collective-permute-start | bytes 49160 | tf_op jit(solution)/shard_map/ppermute | solution.py:495
  3.3 4.8 %collective-permute-start.1 = (f32[2,32,128]{2,1,0:T(8,128)S(1)}, f32[2,32,128]{2,1,0:T(8,128)S(1)}, u32[]{:S(2)}, u32[]{:S(2)}) collective-permute-start(f32[2,32,128]{2,1,0:T(8,128)S(1)} %pad_maximum_fusion.1.refs_0_), channel_id=1, source_target_pairs={{4,0},{13,1},{6,2},{15,3},{0,4},{9,5},{2,6},{11,7},{12,8},{5,9},{1... | collective-permute-start | bytes 98312 | tf_op jit(solution)/shard_map/ppermute | solution.py:495
  8.1 3.8 %collective-permute-start.2 = (f32[3,16,128]{2,1,0:T(8,128)S(1)}, f32[3,16,128]{2,1,0:T(8,128)S(1)}, u32[]{:S(2)}, u32[]{:S(2)}) collective-permute-start(f32[3,16,128]{2,1,0:T(8,128)S(1)} %pad_maximum_fusion.2), channel_id=1, source_target_pairs={{2,0},{3,1},{0,2},{1,3},{6,4},{7,5},{4,6},{5,7},{10,8},{11,9},{8,1... | collective-permute-start | bytes 73736 | tf_op jit(solution)/shard_map/ppermute | solution.py:495
  12.0 1.2 %collective-permute-start.3 = (f32[112,128]{1,0:T(8,128)S(1)}, f32[112,128]{1,0:T(8,128)S(1)}, u32[]{:S(2)}, u32[]{:S(2)}) collective-permute-start(f32[112,128]{1,0:T(8,128)S(1)} %pad_maximum_fusion), channel_id=1, source_target_pairs={{1,0},{0,1},{3,2},{2,3},{5,4},{4,5},{7,6},{6,7},{9,8},{8,9},{11,10... | collective-permute-start | bytes 172040 | tf_op jit(solution)/shard_map/ppermute | solution.py:495

commit v8 on v7

--- a/solution.py
+++ b/solution.py
@@ -193,7 +193,7 @@
     return out
 
 
-def unpack_kernel(lat_count, bins, rows, cols, window, own_cells, near_cells, rims, begun, laid):
+def unpack_kernel(lat_count, bins, rows, cols, window, own_cells, near_cells, own_rims, near_rims, begun, laid):
     levels = 2
     fields = levels * bins
     level = lax.axis_index("lev")
@@ -209,9 +209,8 @@
 
         lay_block(lat_count, window, rows, store_of(own_cells.at[rank], at * 2))
         lay_block(lat_count, window, rows, store_of(near_cells.at[rank], at * 2 + 1))
-        if rank == 0:
-            lay_rims(lat_count, window, rows, store_of(rims.at[0], at * 2))
-        lay_rims(lat_count, window, rows, store_of(rims.at[1 + rank], at * 2 + 1))
+        lay_rims(lat_count, window, rows, store_of(own_rims.at[rank], at * 2))
+        lay_rims(lat_count, window, rows, store_of(near_rims.at[rank], at * 2 + 1))
     side = jnp.where(near_is_west(), 0, 2)
     for k in range(levels):
         for spot in range(window // EDGE):
@@ -265,24 +264,21 @@
     if lat_count != 2:
         laid[...] = jnp.zeros(laid.shape, jnp.float32)
 
-    def store_of(first, at, place, more_to):
+    def store_of(first, at):
         def store(start, size, row):
             for part in range(0, size, EDGE):
-                share = shares(far[pl.ds(first + start + part, EDGE)], place, bins, cols)
+                share = shares(far[pl.ds(first + start + part, EDGE)], side, bins, cols)
                 for kind in range(kinds):
                     target = (at * kinds + kind) * window + row + part
-                    target = pl.ds(pl.multiple_of(target, 8), EDGE)
-                    laid[target] = laid[target] + share[kind] if more_to else share[kind]
+                    laid[pl.ds(pl.multiple_of(target, 8), EDGE)] = share[kind]
 
         return store
 
     height = window - rows
     for rank in range(levels):
         at = (rank + level) % levels
-        lay_block(lat_count, window, rows, store_of((1 - rank) * rows, at, side, False))
-        first = levels * rows + (2 - rank) * height
-        lay_rims(lat_count, window, rows, store_of(first, at, side, False))
-    lay_rims(lat_count, window, rows, store_of(levels * rows, 1 - level, 1, True))
+        lay_block(lat_count, window, rows, store_of((1 - rank) * rows, at))
+        lay_rims(lat_count, window, rows, store_of(levels * rows + (1 - rank) * height, at))
     for k in range(levels):
         for spot in spots:
             share = [rows_of(laid, k * kinds + kind, window, spot) for kind in range(kinds)]
@@ -560,19 +556,21 @@
 
         own = jnp.stack([packed, moved(packed, lambda lon, lat, lev: (lon, lat, 1 - lev))])
         near = moved(own, lambda lon, lat, lev: (lon ^ 1 if lev == 0 else lon + 1 - 2 * ((lon + 1) % 2), lat, lev))
-        held = jnp.concatenate([packed[None], near])
-        if lat_count == 2:
-            rims = moved(held[:, :REACH], lambda lon, lat, lev: (lon, 1 - lat, lev))
-        else:
+
+        def rims_of(held):
+            if lat_count == 2:
+                return moved(held[:, :REACH], lambda lon, lat, lev: (lon, 1 - lat, lev))
             low = moved(
                 held[:, rows - REACH :], lambda lon, lat, lev: (lon, lat - 1, lev) if lat > 0 else None
             )
             high = moved(
                 held[:, :REACH], lambda lon, lat, lev: (lon, lat + 1, lev) if lat < lat_count - 1 else None
             )
-            rims = jnp.concatenate([low, high], axis=1)
-        rims, table, scales = lax.optimization_barrier((rims, table, scales))
-        brought = jnp.concatenate([near.reshape(-1, LANES), rims.reshape(-1, LANES)])
+            return jnp.concatenate([low, high], axis=1)
+
+        own_rims, near_rims = lax.optimization_barrier((rims_of(own), rims_of(near)))
+        near_rims, table, scales = lax.optimization_barrier((near_rims, table, scales))
+        brought = jnp.concatenate([near.reshape(-1, LANES), near_rims.reshape(-1, LANES)])
         far = moved(brought, lambda lon, lat, lev: (lon, lat, 1 - lev))
 
         def cycle(*refs):
@@ -588,11 +586,11 @@
         begun = pl.pallas_call(
             unpack,
             out_shape=pltpu.VMEM(field_shape, jnp.float32),
-            in_specs=[in_vmem] * 3,
+            in_specs=[in_vmem] * 4,
             out_specs=in_vmem,
             scratch_shapes=[pltpu.VMEM((4 * window, LANES), jnp.float32)],
             compiler_params=small,
-        )(own, near, rims)
+        )(own, near, own_rims, near_rims)
         begun, far = lax.optimization_barrier((begun, far))
         field_store = pltpu.VMEM((fields * window, LANES), jnp.float32)
         analysis, correction = pl.pallas_call(

time: 15.9 us -> 15.8 us (level)
  waiting for transfers between devices: 4.09 us -> 2.41 us
  starting transfers between devices: 5.55 us -> 7.11 us
    ppermute x4 -> x5, waiting for transfers between devices: 4.09 us -> 2.41 us  [moved(): return lax.ppermute(values, AXES, pairs)]
    ppermute x4 -> x5, starting transfers between devices: 5.55 us -> 7.11 us  [moved(): return lax.ppermute(values, AXES, pairs)]
  transfers between devices with their start and end apart: 4 -> 5, of which waited for: 4 -> 4; matrix products, arithmetic and copies ran while one was open for 0% -> 0% of each run, Pallas kernels for 10% -> 10%
where the time goes in v8:
time: 15.8 us; the launch traced here: 15.5 us
  starting transfers between devices  7.11 us (45%)
  Pallas kernels  5.29 us (33%)
  waiting for transfers between devices  2.41 us (15%)
  between operations  0.67 us (4%)
    ppermute x5, starting transfers between devices, moved(): return lax.ppermute(values, AXES, pairs)  7.11 us
    ppermute x5, waiting for transfers between devices, moved(): return lax.ppermute(values, AXES, pairs)  2.41 us
    pallas_call x1, Pallas kernels, per_device(): pl.pallas_call(cycle, out_shape=(jax.ShapeDtypeStruct(trajectory.shape, j...  2.37 us
    pallas_call x1, Pallas kernels, per_device(): pl.pallas_call(tabulate, out_shape=(pltpu.VMEM((2, window, LANES), jnp.fl...  1.35 us
    pallas_call x1, Pallas kernels, per_device(): pl.pallas_call(restrict, out_shape=pltpu.VMEM((rows, LANES), jnp.float32)...  1.34 us
  transfers between devices with their start and end apart: 5, of which 4 were waited for; matrix products, arithmetic and copies ran while one was open for 0% of the time, Pallas kernels for 10%

profile of v8, /device:TPU:0, one launch (start us, length us, event | category | flops | bytes accessed | tf_op | source)
XLA Modules:
  0.0 15.5 jit_solution(1868165083608235329)
XLA Ops:
  0.6 1.3 %shard_map.95 = f32[32,128]{1,0:T(8,128)S(1)} custom-call(bf16[2,3,1,256,128]{4,3,2,1,0:T(8,128)(2,1)} %refs_4_.3, f32[8,8]{1,0:T(8,128)} %refs_4_.2, f32[1,16,32]{2,1,0:T(8,128)} %bitcast.22, s32[16,32]{1,0:T(8,128)} %bitcast.23), custom_call_target="tpu_custom_call" | custom-call | tf_op jit(solution)/shard_map/pallas_call | solution.py:518
  2.0 0.5 %collective-permute-start = (f32[32,128]{1,0:T(8,128)S(1)}, f32[32,128]{1,0:T(8,128)S(1)}, u32[]{:S(2)}, u32[]{:S(2)}) collective-permute-start(f32[32,128]{1,0:T(8,128)S(1)} %shard_map.95), channel_id=1, source_target_pairs={{1,0},{0,1},{3,2},{2,3},{5,4},{4,5},{7,6},{6,7},{9,8},{8,9},{11,10... | collective-permute-start | bytes 49160 | tf_op jit(solution)/shard_map/ppermute | solution.py:491
  2.5 0.8 %collective-permute-done = f32[32,128]{1,0:T(8,128)S(1)} collective-permute-done((f32[32,128]{1,0:T(8,128)S(1)}, f32[32,128]{1,0:T(8,128)S(1)}, u32[]{:S(2)}, u32[]{:S(2)}) %collective-permute-start) | collective-permute-done | bytes 16416 | tf_op jit(solution)/shard_map/ppermute | solution.py:491
  3.3 2.9 %collective-permute-start.1 = (f32[2,32,128]{2,1,0:T(8,128)S(1)}, f32[2,32,128]{2,1,0:T(8,128)S(1)}, u32[]{:S(2)}, u32[]{:S(2)}) collective-permute-start(f32[2,32,128]{2,1,0:T(8,128)S(1)} %pad_maximum_fusion.1.refs_0_), channel_id=1, source_target_pairs={{4,0},{13,1},{6,2},{15,3},{0,4},{9,5},{2,6},{11,7},{12,8},{5,9},{1... | collective-permute-start | bytes 98312 | tf_op jit(solution)/shard_map/ppermute | solution.py:491
  6.3 1.5 %collective-permute-start.2 = (f32[2,16,128]{2,1,0:T(8,128)S(1)}, f32[2,16,128]{2,1,0:T(8,128)S(1)}, u32[]{:S(2)}, u32[]{:S(2)}) collective-permute-start(f32[2,16,128]{2,1,0:T(8,128)S(1)} %fusion), channel_id=1, source_target_pairs={{2,0},{3,1},{0,2},{1,3},{6,4},{7,5},{4,6},{5,7},{10,8},{11,9},{8,1... | collective-permute-start | bytes 49160 | tf_op jit(solution)/shard_map/ppermute | solution.py:491
  7.7 0.4 %collective-permute-done.1.refs_1_ = f32[2,32,128]{2,1,0:T(8,128)S(1)} collective-permute-done((f32[2,32,128]{2,1,0:T(8,128)S(1)}, f32[2,32,128]{2,1,0:T(8,128)S(1)}, u32[]{:S(2)}, u32[]{:S(2)}) %collective-permute-start.1) | collective-permute-done | bytes 32800 | tf_op jit(solution)/shard_map/ppermute | solution.py:491
  8.1 1.9 %collective-permute-start.3 = (f32[2,16,128]{2,1,0:T(8,128)S(1)}, f32[2,16,128]{2,1,0:T(8,128)S(1)}, u32[]{:S(2)}, u32[]{:S(2)}) collective-permute-start(f32[2,16,128]{2,1,0:T(8,128)S(1)} %slice.10), channel_id=1, source_target_pairs={{2,0},{3,1},{0,2},{1,3},{6,4},{7,5},{4,6},{5,7},{10,8},{11,9},{8,1... | collective-permute-start | bytes 49160 | tf_op jit(solution)/shard_map/ppermute | solution.py:491
  10.1 1.3 %shard_map.96 = (f32[2,48,128]{2,1,0:T(8,128)S(1)}, f32[7,8,128]{2,1,0:T(8,128)S(1)}) custom-call(s32[32,64]{1,0:T(8,128)} %bitcast.21, f32[2,32,64]{2,1,0:T(8,128)} %bitcast.19, f32[2,32,64]{2,1,0:T(8,128)} %bitcast.20, f32[2,3]{1,0:T(2,128)} %bitcast.24, f32[8,8]{1,0:T(8,128)} %refs_4_.2), custom_call_target="tpu_custom_call" | custom-call | tf_op jit(solution)/shard_map/pallas_call | solution.py:544
  11.4 0.0 collective-permute-done.2.refs_2_
  11.5 0.4 %collective-permute-done.3.refs_3_ = f32[2,16,128]{2,1,0:T(8,128)S(1)} collective-permute-done((f32[2,16,128]{2,1,0:T(8,128)S(1)}, f32[2,16,128]{2,1,0:T(8,128)S(1)}, u32[]{:S(2)}, u32[]{:S(2)}) %collective-permute-start.3) | collective-permute-done | bytes 16416 | tf_op jit(solution)/shard_map/ppermute | solution.py:491
  11.9 0.2 %collective-permute-start.4 = (f32[96,128]{1,0:T(8,128)S(1)}, f32[96,128]{1,0:T(8,128)S(1)}, u32[]{:S(2)}, u32[]{:S(2)}) collective-permute-start(f32[96,128]{1,0:T(8,128)S(1)} %pad_maximum_fusion), channel_id=1, source_target_pairs={{1,0},{0,1},{3,2},{2,3},{5,4},{4,5},{7,6},{6,7},{9,8},{8,9},{11,10... | collective-permute-start | bytes 147464 | tf_op jit(solution)/shard_map/ppermute | solution.py:491
  12.1 0.2 %shard_map.97.refs_0_ = f32[624,128]{1,0:T(8,128)S(1)} custom-call(f32[2,32,128]{2,1,0:T(8,128)S(1)} %pad_maximum_fusion.1.refs_0_, f32[2,32,128]{2,1,0:T(8,128)S(1)} %collective-permute-done.1.refs_1_, f32[2,16,128]{2,1,0:T(8,128)S(1)} %collective-permute-done.2.refs_2_, f32[2,16,128]{2,1,0:T(8,128)S(1)} %collective-permute-done.3.refs_3_), custom_call_target="tpu_custom_call" | custom-call | tf_op jit(solution)/shard_map/pallas_call | solution.py:586
  12.4 0.7 %collective-permute-done.4.refs_1_ = f32[96,128]{1,0:T(8,128)S(1)} collective-permute-done((f32[96,128]{1,0:T(8,128)S(1)}, f32[96,128]{1,0:T(8,128)S(1)}, u32[]{:S(2)}, u32[]{:S(2)}) %collective-permute-start.4) | collective-permute-done | bytes 49184 | tf_op jit(solution)/shard_map/ppermute | solution.py:491
  13.1 2.4 %shard_map.98 = (bf16[2,3,1,256,128]{4,3,2,1,0:T(8,128)(2,1)}, f32[2,3,1,16,32]{4,3,2,1,0:T(8,128)}) custom-call(f32[624,128]{1,0:T(8,128)S(1)} %shard_map.97.refs_0_, f32[96,128]{1,0:T(8,128)S(1)} %collective-permute-done.4.refs_1_, f32[96,128]{1,0:T(8,128)S(1)} %bitcast.16, f32[7,8,128]{2,1,0:T(8,128)S(1)} %get-tuple-element.21.refs_3_, ...), custom_call_target="tpu_custom_call" | custom-call | tf_op jit(solution)/shard_map/pallas_call | solution.py:596
  (4 shorter events, 0.0 us)
Async XLA Ops:
  2.0 1.4 %collective-permute-start = (f32[32,128]{1,0:T(8,128)S(1)}, f32[32,128]{1,0:T(8,128)S(1)}, u32[]{:S(2)}, u32[]{:S(2)}) collective-permute-start(f32[32,128]{1,0:T(8,128)S(1)} %shard_map.95), channel_id=1, source_target_pairs={{1,0},{0,1},{3,2},{2,3},{5,4},{4,5},{7,6},{6,7},{9,8},{8,9},{11,10... | collective-permute-start | bytes 49160 | tf_op jit(solution)/shard_map/ppermute | solution.py:491
  3.3 4.8 %collective-permute-start.1 = (f32[2,32,128]{2,1,0:T(8,128)S(1)}, f32[2,32,128]{2,1,0:T(8,128)S(1)}, u32[]{:S(2)}, u32[]{:S(2)}) collective-permute-start(f32[2,32,128]{2,1,0:T(8,128)S(1)} %pad_maximum_fusion.1.refs_0_), channel_id=1, source_target_pairs={{4,0},{13,1},{6,2},{15,3},{0,4},{9,5},{2,6},{11,7},{12,8},{5,9},{1... | collective-permute-start | bytes 98312 | tf_op jit(solution)/shard_map/ppermute | solution.py:491
  6.3 5.2 %collective-permute-start.2 = (f32[2,16,128]{2,1,0:T(8,128)S(1)}, f32[2,16,128]{2,1,0:T(8,128)S(1)}, u32[]{:S(2)}, u32[]{:S(2)}) collective-permute-start(f32[2,16,128]{2,1,0:T(8,128)S(1)} %fusion), channel_id=1, source_target_pairs={{2,0},{3,1},{0,2},{1,3},{6,4},{7,5},{4,6},{5,7},{10,8},{11,9},{8,1... | collective-permute-start | bytes 49160 | tf_op jit(solution)/shard_map/ppermute | solution.py:491
  8.1 3.7 %collective-permute-start.3 = (f32[2,16,128]{2,1,0:T(8,128)S(1)}, f32[2,16,128]{2,1,0:T(8,128)S(1)}, u32[]{:S(2)}, u32[]{:S(2)}) collective-permute-start(f32[2,16,128]{2,1,0:T(8,128)S(1)} %slice.10), channel_id=1, source_target_pairs={{2,0},{3,1},{0,2},{1,3},{6,4},{7,5},{4,6},{5,7},{10,8},{11,9},{8,1... | collective-permute-start | bytes 49160 | tf_op jit(solution)/shard_map/ppermute | solution.py:491
  11.9 1.2 %collective-permute-start.4 = (f32[96,128]{1,0:T(8,128)S(1)}, f32[96,128]{1,0:T(8,128)S(1)}, u32[]{:S(2)}, u32[]{:S(2)}) collective-permute-start(f32[96,128]{1,0:T(8,128)S(1)} %pad_maximum_fusion), channel_id=1, source_target_pairs={{1,0},{0,1},{3,2},{2,3},{5,4},{4,5},{7,6},{6,7},{9,8},{8,9},{11,10... | collective-permute-start | bytes 147464 | tf_op jit(solution)/shard_map/ppermute | solution.py:491
